TPU v7x, 128 devices: a whole 4x4x4 slice. The times are simulated.
128 devices in a mesh: dp: 8 (over y_hi, x), seq: 16 (over y_lo, z, core).
Axes of the slice: x: 4, y: 4 (y_hi: 2, y_lo: 2; y = y_hi * 2 + y_lo), z: 4, core: 2. Of those that a mesh axis runs over, the one named last changes fastest.
Arguments:
- tokens: bfloat16 [16384, 2048], P(('dp', 'seq')), may hold values from -6 to 6
- doc_lengths: int32 [8, 3], P('dp'), may hold values from 32 to 2048, as said below
- first_gain: bfloat16 [2048], P('seq'), may hold values from 0.25 to 1.75
- query_down: bfloat16 [2048, 1024], P('seq'), may hold values from -0.125 to 0.125
- key_proj: bfloat16 [2048, 256], P('seq'), may hold values from -0.125 to 0.125
- value_proj: bfloat16 [2048, 256], P('seq'), may hold values from -0.125 to 0.125
- query_gain: bfloat16 [1024], P('seq'), may hold values from 0.25 to 1.75
- query_up: bfloat16 [1024, 4096], P('seq'), may hold values from -0.1875 to 0.1875
- out_proj: bfloat16 [4096, 2048], P('seq'), may hold values from -0.75 to 0.75
- second_gain: bfloat16 [2048], P('seq'), may hold values from 0.25 to 1.75
- gate_proj: bfloat16 [2048, 5632], P('seq'), may hold values from -0.125 to 0.125
- up_proj: bfloat16 [2048, 5632], P('seq'), may hold values from -0.125 to 0.125
- down_proj: bfloat16 [5632, 2048], P('seq'), may hold values from -0.078125 to 0.078125
- cotangent: bfloat16 [16384, 2048], P(('dp', 'seq')), may hold values from -6 to 6
Outputs:
- layer_out: bfloat16 [16384, 2048], P(('dp', 'seq'))
- input_grad: float32 [16384, 2048], P(('dp', 'seq'))
- first_gain_grad: float32 [2048], P('seq')
- query_down_grad: float32 [2048, 1024], P('seq')
- key_proj_grad: float32 [2048, 256], P('seq')
- value_proj_grad: float32 [2048, 256], P('seq')
- query_gain_grad: float32 [1024], P('seq')
- query_up_grad: float32 [1024, 4096], P('seq')
- out_proj_grad: float32 [4096, 2048], P('seq')
- second_gain_grad: float32 [2048], P('seq')
- gate_proj_grad: float32 [2048, 5632], P('seq')
- up_proj_grad: float32 [2048, 5632], P('seq')
- down_proj_grad: float32 [5632, 2048], P('seq')
Inputs may be any that keep to these rules, and one draw needn't show every extreme that they name: Each row of doc_lengths sums to 2048. In each row one document, in a slot drawn from the seed, holds at least 1922 tokens; the others hold 32 to 63 each.
All inputs are finite; a program needn't handle non-finite values.
Results may differ from a plain program's by a relative error of at most 0.028.
Values may be sent and summed in bfloat16 or wider, within the bound.
No kernel may reach another device: no remote copies, remote signals or barrier semaphores. Data moves between devices by JAX's collectives and lax.ppermute only.
A program may use at most 320 MiB of HBM per device.

v0:
```python
import jax
import jax.numpy as jnp
from jax import lax
from jax.sharding import PartitionSpec as P

HEADS = 16


NORM_EPSILON = 1e-05


def inverse_rms(values):
    return lax.rsqrt(jnp.mean(values * values, axis=-1, keepdims=True) + NORM_EPSILON)


def rms_back(values, inv_root, gain_row, grad_normed):
    scaled = grad_normed * gain_row
    gain_grad = jnp.sum(grad_normed * values * inv_root, axis=0)
    grad_values = inv_root * scaled - values * inv_root**3 * jnp.mean(
        scaled * values, axis=-1, keepdims=True
    )
    return (grad_values, gain_grad)


def layout(lengths, token_index):
    doc_ends = jnp.cumsum(lengths)
    starts = doc_ends - lengths
    doc_id = jnp.sum((token_index[:, None] >= doc_ends[None, :]).astype(jnp.int32), axis=1)
    numbers = jnp.arange(lengths.shape[0], dtype=jnp.int32)
    doc_start = jnp.sum(jnp.where(doc_id[:, None] == numbers[None, :], starts[None, :], 0), axis=1)
    return (doc_id, token_index - doc_start)


def rope_tables(position, head_width):
    half_width = head_width // 2
    frequency = 10000.0 ** (-(2.0 * jnp.arange(half_width, dtype=jnp.float32)) / head_width)
    angles = position.astype(jnp.float32)[:, None] * frequency[None, :]
    cosine = jnp.cos(angles)
    sine_table = jnp.sin(angles)
    return (
        jnp.concatenate([cosine, cosine], axis=-1),
        jnp.concatenate([sine_table, sine_table], axis=-1),
    )


def rotate(values, cosine, sine_table):
    half_width = values.shape[-1] // 2
    turned = jnp.concatenate([-values[..., half_width:], values[..., :half_width]], axis=-1)
    return values * cosine + turned * sine_table


def rotate_back(grads, cosine, sine_table):
    half_width = grads.shape[-1] // 2
    moved = grads * sine_table
    back = jnp.concatenate([moved[..., half_width:], -moved[..., :half_width]], axis=-1)
    return grads * cosine + back


def shards(
    tokens,
    doc_lengths,
    first_gain,
    query_down,
    key_proj,
    value_proj,
    query_gain,
    query_up,
    out_proj,
    second_gain,
    gate_proj,
    up_proj,
    down_proj,
    cotangent,
):
    f32 = jnp.float32
    bf16 = jnp.bfloat16
    (
        gain_one,
        down_all,
        key_all,
        value_all,
        gain_query,
        up_all,
        out_all,
        gain_two,
        gate_all,
        lift_all,
        fall_all,
    ) = (
        lax.all_gather(first_gain, "seq", axis=0, tiled=True),
        lax.all_gather(query_down, "seq", axis=0, tiled=True),
        lax.all_gather(key_proj, "seq", axis=0, tiled=True),
        lax.all_gather(value_proj, "seq", axis=0, tiled=True),
        lax.all_gather(query_gain, "seq", axis=0, tiled=True),
        lax.all_gather(query_up, "seq", axis=0, tiled=True),
        lax.all_gather(out_proj, "seq", axis=0, tiled=True),
        lax.all_gather(second_gain, "seq", axis=0, tiled=True),
        lax.all_gather(gate_proj, "seq", axis=0, tiled=True),
        lax.all_gather(up_proj, "seq", axis=0, tiled=True),
        lax.all_gather(down_proj, "seq", axis=0, tiled=True),
    )
    local_rows = tokens.shape[0]
    head_width = key_proj.shape[1]
    group_size = local_rows * lax.axis_size("seq")
    my_index = lax.axis_index("seq")
    token_index = my_index * local_rows + jnp.arange(local_rows, dtype=jnp.int32)
    key_index = jnp.arange(group_size, dtype=jnp.int32)
    lengths = doc_lengths[0]
    doc_query, position = layout(lengths, token_index)
    doc_key, key_place = layout(lengths, key_index)
    cosine, sine_table = rope_tables(position, head_width)
    score_scale = head_width ** (-0.5)
    block_count = my_index + 1
    tokens_float = tokens.astype(f32)
    inv_one = inverse_rms(tokens_float)
    normed = (tokens_float * inv_one * gain_one.astype(f32)).astype(bf16)
    latent = jnp.dot(normed, down_all, preferred_element_type=f32)
    inv_latent = inverse_rms(latent)
    latent_n = (latent * inv_latent * gain_query.astype(f32)).astype(bf16)
    queries = jnp.dot(latent_n, up_all, preferred_element_type=f32).reshape(
        local_rows, HEADS, head_width
    )
    key_raw = jnp.dot(normed, key_all, preferred_element_type=f32)
    value_raw = jnp.dot(normed, value_all, preferred_element_type=f32)
    query_rot = rotate(queries, cosine[:, None, :], sine_table[:, None, :]).astype(bf16)
    key_rot = rotate(key_raw, cosine, sine_table).astype(bf16)
    value_low = value_raw.astype(bf16)
    keys_all, values_all = (
        lax.all_gather(key_rot, "seq", axis=0, tiled=True),
        lax.all_gather(value_low, "seq", axis=0, tiled=True),
    )

    def block_scores(block, key_source):
        start = block * local_rows
        key_block = lax.dynamic_slice_in_dim(key_source, start, local_rows, 0)
        doc_block = lax.dynamic_slice_in_dim(doc_key, start, local_rows, 0)
        index_block = start + jnp.arange(local_rows, dtype=jnp.int32)
        allowed = (doc_query[:, None] == doc_block[None, :]) & (
            index_block[None, :] <= token_index[:, None]
        )
        scores = (
            jnp.einsum("qhd,kd->hqk", query_rot, key_block, preferred_element_type=f32)
            * score_scale
        )
        return (jnp.where(allowed[None], scores, -1e30), allowed, key_block, start)

    def forward_block(block, carry):
        running_max, running_total, running_sum = carry
        scores, allowed, key_block, start = block_scores(block, keys_all)
        value_block = lax.dynamic_slice_in_dim(values_all, start, local_rows, 0)
        new_max = jnp.maximum(running_max, jnp.max(scores, axis=-1, keepdims=True))
        factor = jnp.exp(running_max - new_max)
        weights_raw = jnp.where(allowed[None], jnp.exp(scores - new_max), 0.0)
        new_total = running_total * factor + jnp.sum(weights_raw, axis=-1, keepdims=True)
        product = jnp.einsum(
            "hqk,kd->qhd", weights_raw.astype(bf16), value_block, preferred_element_type=f32
        )
        new_sum = running_sum * jnp.transpose(factor, (1, 0, 2)) + product
        return (new_max, new_total, new_sum)

    start_max = jnp.full((HEADS, local_rows, 1), -1e30, f32)
    start_total = jnp.zeros((HEADS, local_rows, 1), f32)
    start_sum = jnp.zeros((local_rows, HEADS, head_width), f32)
    maxima, totals, summed_values = lax.fori_loop(
        0, block_count, forward_block, (start_max, start_total, start_sum)
    )
    log_total = maxima + jnp.log(totals)
    attended_pre = summed_values / jnp.transpose(totals, (1, 0, 2))
    attended = attended_pre.reshape(local_rows, HEADS * head_width).astype(bf16)
    residual = tokens_float + jnp.dot(attended, out_all, preferred_element_type=f32)
    inv_two = inverse_rms(residual)
    normed_two = (residual * inv_two * gain_two.astype(f32)).astype(bf16)
    gate_values = jnp.dot(normed_two, gate_all, preferred_element_type=f32)
    up_values = jnp.dot(normed_two, lift_all, preferred_element_type=f32)
    sigmoid_gate = jax.nn.sigmoid(gate_values)
    hidden = (gate_values * sigmoid_gate * up_values).astype(bf16)
    layer_sum = residual + jnp.dot(hidden, fall_all, preferred_element_type=f32)
    layer_out = layer_sum.astype(bf16)
    late = lax.optimization_barrier(
        (
            (
                first_gain,
                query_down,
                key_proj,
                value_proj,
                query_gain,
                query_up,
                out_proj,
                second_gain,
                gate_proj,
                up_proj,
                down_proj,
            ),
            layer_sum,
        )
    )[0]
    (
        gain_one,
        down_all,
        key_all,
        value_all,
        gain_query,
        up_all,
        out_all,
        gain_two,
        gate_all,
        lift_all,
        fall_all,
    ) = (
        lax.all_gather(late[0], "seq", axis=0, tiled=True),
        lax.all_gather(late[1], "seq", axis=0, tiled=True),
        lax.all_gather(late[2], "seq", axis=0, tiled=True),
        lax.all_gather(late[3], "seq", axis=0, tiled=True),
        lax.all_gather(late[4], "seq", axis=0, tiled=True),
        lax.all_gather(late[5], "seq", axis=0, tiled=True),
        lax.all_gather(late[6], "seq", axis=0, tiled=True),
        lax.all_gather(late[7], "seq", axis=0, tiled=True),
        lax.all_gather(late[8], "seq", axis=0, tiled=True),
        lax.all_gather(late[9], "seq", axis=0, tiled=True),
        lax.all_gather(late[10], "seq", axis=0, tiled=True),
    )
    late_keys = lax.optimization_barrier((key_rot, value_low, layer_sum))
    keys_back, values_back = (
        lax.all_gather(late_keys[0], "seq", axis=0, tiled=True),
        lax.all_gather(late_keys[1], "seq", axis=0, tiled=True),
    )
    grad_out = cotangent.astype(f32)
    grad_hidden = jnp.einsum("td,fd->tf", cotangent, fall_all, preferred_element_type=f32)
    grad_gate = (
        grad_hidden * up_values * sigmoid_gate * (1.0 + gate_values * (1.0 - sigmoid_gate))
    ).astype(bf16)
    grad_up = (grad_hidden * gate_values * sigmoid_gate).astype(bf16)
    grad_normed_two = jnp.einsum(
        "tf,df->td", grad_gate, gate_all, preferred_element_type=f32
    ) + jnp.einsum("tf,df->td", grad_up, lift_all, preferred_element_type=f32)
    grad_two, second_grad = rms_back(residual, inv_two, gain_two.astype(f32), grad_normed_two)
    grad_residual = grad_out + grad_two
    down_grad = jnp.einsum("tf,td->fd", hidden, cotangent, preferred_element_type=f32)
    gate_grad = jnp.einsum("td,tf->df", normed_two, grad_gate, preferred_element_type=f32)
    lift_grad = jnp.einsum("td,tf->df", normed_two, grad_up, preferred_element_type=f32)
    feed_sums = (
        lax.psum_scatter(
            second_grad.astype(jnp.bfloat16), "seq", scatter_dimension=0, tiled=True
        ).astype(jnp.float32),
        lax.psum_scatter(
            gate_grad.astype(jnp.bfloat16), "seq", scatter_dimension=0, tiled=True
        ).astype(jnp.float32),
        lax.psum_scatter(
            lift_grad.astype(jnp.bfloat16), "seq", scatter_dimension=0, tiled=True
        ).astype(jnp.float32),
        lax.psum_scatter(
            down_grad.astype(jnp.bfloat16), "seq", scatter_dimension=0, tiled=True
        ).astype(jnp.float32),
    )
    grad_branch = grad_residual.astype(bf16)
    out_grad = jnp.einsum("tk,td->kd", attended, grad_branch, preferred_element_type=f32)
    grad_attended = jnp.einsum("td,kd->tk", grad_branch, out_all, preferred_element_type=f32)
    grad_attended = grad_attended.astype(bf16).reshape(local_rows, HEADS, head_width)
    row_dot = jnp.transpose(jnp.sum(grad_attended.astype(f32) * attended_pre, axis=-1), (1, 0))[
        :, :, None
    ]

    def backward_block(block, carry):
        grad_query_acc, key_grad_acc, value_grad_acc = carry
        scores, allowed, key_block, start = block_scores(block, keys_back)
        value_block = lax.dynamic_slice_in_dim(values_back, start, local_rows, 0)
        probs = jnp.exp(scores - log_total)
        grad_probs = jnp.einsum(
            "qhd,kd->hqk", grad_attended, value_block, preferred_element_type=f32
        )
        value_piece = jnp.einsum(
            "hqk,qhd->kd", probs.astype(bf16), grad_attended, preferred_element_type=f32
        )
        grad_scores = (probs * (grad_probs - row_dot) * score_scale).astype(bf16)
        grad_query_acc = grad_query_acc + jnp.einsum(
            "hqk,kd->qhd", grad_scores, key_block, preferred_element_type=f32
        )
        key_piece = jnp.einsum("hqk,qhd->kd", grad_scores, query_rot, preferred_element_type=f32)
        key_grad_acc = lax.dynamic_update_slice_in_dim(key_grad_acc, key_piece, start, 0)
        value_grad_acc = lax.dynamic_update_slice_in_dim(value_grad_acc, value_piece, start, 0)
        return (grad_query_acc, key_grad_acc, value_grad_acc)

    empty_keys = jnp.zeros((group_size, head_width), f32)
    grad_qrot, key_grad_sum, value_grad_sum = lax.fori_loop(
        0,
        block_count,
        backward_block,
        (jnp.zeros((local_rows, HEADS, head_width), f32), empty_keys, empty_keys),
    )
    key_grad_local, value_grad_local = (
        lax.psum_scatter(
            key_grad_sum.astype(jnp.bfloat16), "seq", scatter_dimension=0, tiled=True
        ).astype(jnp.float32),
        lax.psum_scatter(
            value_grad_sum.astype(jnp.bfloat16), "seq", scatter_dimension=0, tiled=True
        ).astype(jnp.float32),
    )
    grad_keys = rotate_back(key_grad_local, cosine, sine_table).astype(bf16)
    grad_values = value_grad_local.astype(bf16)
    grad_queries = rotate_back(grad_qrot, cosine[:, None, :], sine_table[:, None, :])
    grad_queries = grad_queries.astype(bf16).reshape(local_rows, HEADS * head_width)
    query_up_grad = jnp.einsum("tc,tk->ck", latent_n, grad_queries, preferred_element_type=f32)
    grad_latent_n = jnp.einsum("tk,ck->tc", grad_queries, up_all, preferred_element_type=f32)
    grad_latent, query_gain_grad = rms_back(
        latent, inv_latent, gain_query.astype(f32), grad_latent_n
    )
    grad_latent = grad_latent.astype(bf16)
    query_down_grad = jnp.einsum("td,tc->dc", normed, grad_latent, preferred_element_type=f32)
    key_proj_grad = jnp.einsum("td,te->de", normed, grad_keys, preferred_element_type=f32)
    value_proj_grad = jnp.einsum("td,te->de", normed, grad_values, preferred_element_type=f32)
    grad_normed = (
        jnp.einsum("tc,dc->td", grad_latent, down_all, preferred_element_type=f32)
        + jnp.einsum("te,de->td", grad_keys, key_all, preferred_element_type=f32)
        + jnp.einsum("te,de->td", grad_values, value_all, preferred_element_type=f32)
    )
    grad_one, first_grad = rms_back(tokens_float, inv_one, gain_one.astype(f32), grad_normed)
    input_grad = grad_residual + grad_one
    summed = (
        lax.psum_scatter(
            first_grad.astype(jnp.bfloat16), "seq", scatter_dimension=0, tiled=True
        ).astype(jnp.float32),
        lax.psum_scatter(
            query_down_grad.astype(jnp.bfloat16), "seq", scatter_dimension=0, tiled=True
        ).astype(jnp.float32),
        lax.psum_scatter(
            key_proj_grad.astype(jnp.bfloat16), "seq", scatter_dimension=0, tiled=True
        ).astype(jnp.float32),
        lax.psum_scatter(
            value_proj_grad.astype(jnp.bfloat16), "seq", scatter_dimension=0, tiled=True
        ).astype(jnp.float32),
        lax.psum_scatter(
            query_gain_grad.astype(jnp.bfloat16), "seq", scatter_dimension=0, tiled=True
        ).astype(jnp.float32),
        lax.psum_scatter(
            query_up_grad.astype(jnp.bfloat16), "seq", scatter_dimension=0, tiled=True
        ).astype(jnp.float32),
        lax.psum_scatter(
            out_grad.astype(jnp.bfloat16), "seq", scatter_dimension=0, tiled=True
        ).astype(jnp.float32),
    )
    totals_all = (
        lax.psum(summed[0].astype(jnp.bfloat16), "dp").astype(jnp.float32),
        lax.psum(summed[1].astype(jnp.bfloat16), "dp").astype(jnp.float32),
        lax.psum(summed[2].astype(jnp.bfloat16), "dp").astype(jnp.float32),
        lax.psum(summed[3].astype(jnp.bfloat16), "dp").astype(jnp.float32),
        lax.psum(summed[4].astype(jnp.bfloat16), "dp").astype(jnp.float32),
        lax.psum(summed[5].astype(jnp.bfloat16), "dp").astype(jnp.float32),
        lax.psum(summed[6].astype(jnp.bfloat16), "dp").astype(jnp.float32),
        lax.psum(feed_sums[0].astype(jnp.bfloat16), "dp").astype(jnp.float32),
        lax.psum(feed_sums[1].astype(jnp.bfloat16), "dp").astype(jnp.float32),
        lax.psum(feed_sums[2].astype(jnp.bfloat16), "dp").astype(jnp.float32),
        lax.psum(feed_sums[3].astype(jnp.bfloat16), "dp").astype(jnp.float32),
    )
    return (
        layer_out,
        input_grad,
        totals_all[0],
        totals_all[1],
        totals_all[2],
        totals_all[3],
        totals_all[4],
        totals_all[5],
        totals_all[6],
        totals_all[7],
        totals_all[8],
        totals_all[9],
        totals_all[10],
    )


def solution(mesh):
    in_specs = (
        P(("dp", "seq"), None),
        P("dp", None),
        P("seq"),
        P("seq", None),
        P("seq", None),
        P("seq", None),
        P("seq"),
        P("seq", None),
        P("seq", None),
        P("seq"),
        P("seq", None),
        P("seq", None),
        P("seq", None),
        P(("dp", "seq"), None),
    )
    out_specs = (
        P(("dp", "seq"), None),
        P(("dp", "seq"), None),
        P("seq"),
        P("seq", None),
        P("seq", None),
        P("seq", None),
        P("seq"),
        P("seq", None),
        P("seq", None),
        P("seq"),
        P("seq", None),
        P("seq", None),
        P("seq", None),
    )
    return jax.shard_map(shards, mesh=mesh, in_specs=in_specs, out_specs=out_specs, check_vma=False)
```

profile of v0, /device:TPU:0, one launch (start us, length us, event | category | flops | bytes accessed | tf_op | source)
XLA Modules:
  0.0 2636.5 jit_solution(10451509798518191385)
XLA Ops:
  10.0 21.1 all-gather
  35.0 9.8 all-gather.25.cloned.1.call-done
  47.3 31.9 %all-gather.33.cloned.1.call-done = bf16[2048,256]{1,0:T(8,128)(2,1)} async-done(((bf16[128,256]{1,0:T(8,128)(2,1)}), bf16[2048,256]{1,0:T(8,128)(2,1)}) %all-gather.33.cloned.1.call-update) | async-done | bytes 1048592 | tf_op jit(solution)/shard_map/all_gather | solution.py:93
  85.8 29.1 %all-reduce = bf16[1024]{0:T(1024)(128)(2,1)S(1)} all-reduce(bf16[1024]{0:T(1024)(128)(2,1)S(1)} %dynamic-update-slice), channel_id=1, replica_groups=mesh['dp'=8,'seq'=16] {'seq'}, use_global_device_ids=true, to_apply=%add | all-reduce | flops 1024 | bytes 4096
  114.9 15.9 all-gather.1
  132.3 3.1 multiply_reduce_fusion.6
  136.1 36.2 %all-gather.31.cloned.1.call-done = bf16[1024,4096]{1,0:T(8,128)(2,1)} async-done(((bf16[64,4096]{1,0:T(8,128)(2,1)}), bf16[1024,4096]{1,0:T(8,128)(2,1)}) %all-gather.31.cloned.1.call-update) | async-done | bytes 8388624 | tf_op jit(solution)/shard_map/all_gather | solution.py:95
  172.2 6.8 fusion.61
  180.1 27.9 %all-gather.27.cloned.1.call-done = bf16[2048,256]{1,0:T(8,128)(2,1)} async-done(((bf16[128,256]{1,0:T(8,128)(2,1)}), bf16[2048,256]{1,0:T(8,128)(2,1)}) %all-gather.27.cloned.1.call-update) | async-done | bytes 1048592 | tf_op jit(solution)/shard_map/all_gather | solution.py:129
  207.9 34.7 %all-gather.35.cloned.1.call-done = bf16[2048,256]{1,0:T(8,128)(2,1)} async-done(((bf16[128,256]{1,0:T(8,128)(2,1)}), bf16[2048,256]{1,0:T(8,128)(2,1)}) %all-gather.35.cloned.1.call-update) | async-done | bytes 1048592 | tf_op jit(solution)/shard_map/all_gather | solution.py:130
  242.8 5.1 while.30
  249.2 86.7 %all-gather.37.cloned.1.call-done = bf16[4096,2048]{1,0:T(8,128)(2,1)} async-done(((bf16[256,2048]{1,0:T(8,128)(2,1)}), bf16[4096,2048]{1,0:T(8,128)(2,1)}) %all-gather.37.cloned.1.call-update) | async-done | bytes 16777232 | tf_op jit(solution)/shard_map/all_gather | solution.py:96
  336.0 8.6 multiply_reduce_fusion.3
  346.6 113.3 %all-gather.39.cloned.1.call-done = bf16[2048,5632]{1,0:T(8,128)(2,1)} async-done(((bf16[128,5632]{1,0:T(8,128)(2,1)}), bf16[2048,5632]{1,0:T(8,128)(2,1)}) %all-gather.39.cloned.1.call-update) | async-done | bytes 23068688 | tf_op jit(solution)/shard_map/all_gather | solution.py:98
  460.0 12.6 fusion.74
  472.6 111.4 %all-gather.41.cloned.1.call-done = bf16[2048,5632]{1,0:T(8,128)(2,1)} async-done(((bf16[128,5632]{1,0:T(8,128)(2,1)}), bf16[2048,5632]{1,0:T(8,128)(2,1)}) %all-gather.41.cloned.1.call-update) | async-done | bytes 23068688 | tf_op jit(solution)/shard_map/all_gather | solution.py:99
  584.0 14.5 multiply_convert_fusion.2
  598.5 109.4 %all-gather.43.cloned.1.call-done = bf16[5632,2048]{1,0:T(8,128)(2,1)} async-done(((bf16[352,2048]{1,0:T(8,128)(2,1)}), bf16[5632,2048]{1,0:T(8,128)(2,1)}) %all-gather.43.cloned.1.call-update) | async-done | bytes 23068688 | tf_op jit(solution)/shard_map/all_gather | solution.py:100
  707.8 12.6 convolution_add_fusion.2
  723.6 19.0 all-gather.2
  742.7 100.2 %all-gather.45.cloned.1.call-done = bf16[5632,2048]{1,0:T(8,128)(2,1)} async-done(((bf16[352,2048]{1,0:T(8,128)(2,1)}), bf16[5632,2048]{1,0:T(8,128)(2,1)}) %all-gather.45.cloned.1.call-update) | async-done | bytes 23068688 | tf_op jit(solution)/shard_map/all_gather | solution.py:220
  842.9 19.1 multiply_convert_fusion
  861.9 104.8 %all-gather.47.cloned.1.call-done = bf16[2048,5632]{1,0:T(8,128)(2,1)} async-done(((bf16[128,5632]{1,0:T(8,128)(2,1)}), bf16[2048,5632]{1,0:T(8,128)(2,1)}) %all-gather.47.cloned.1.call-update) | async-done | bytes 23068688 | tf_op jit(solution)/shard_map/all_gather | solution.py:218
  966.7 13.1 fusion.75
  979.8 110.9 %all-gather.49.cloned.1.call-done = bf16[2048,5632]{1,0:T(8,128)(2,1)} async-done(((bf16[128,5632]{1,0:T(8,128)(2,1)}), bf16[2048,5632]{1,0:T(8,128)(2,1)}) %all-gather.49.cloned.1.call-update) | async-done | bytes 23068688 | tf_op jit(solution)/shard_map/all_gather | solution.py:219
  1090.7 14.3 multiply_reduce_fusion.1
  1105.7 2.6 subtract_add_fusion
  1108.3 76.7 %all-gather.55.cloned.1.call-done = bf16[4096,2048]{1,0:T(8,128)(2,1)} async-done(((bf16[256,2048]{1,0:T(8,128)(2,1)}), bf16[4096,2048]{1,0:T(8,128)(2,1)}) %all-gather.55.cloned.1.call-update) | async-done | bytes 16777232 | tf_op jit(solution)/shard_map/all_gather | solution.py:216
  1185.0 12.7 convolution_convert_fusion.5
  1197.7 2.4 copy.77
  1200.1 2.7 copy.66
  1206.7 14.0 all-gather.51.cloned.1.call-done
  1220.7 34.7 %all-gather.53.cloned.1.call-done = bf16[2048,256]{1,0:T(8,128)(2,1)} async-done(((bf16[128,256]{1,0:T(8,128)(2,1)}), bf16[2048,256]{1,0:T(8,128)(2,1)}) %all-gather.53.cloned.1.call-update) | async-done | bytes 1048592 | tf_op jit(solution)/shard_map/all_gather | solution.py:225
  1257.7 7.6 while.31
  1266.6 12.5 convolution_convert_fusion
  1279.2 160.1 %reduce-scatter.11.cloned.1.call-done = bf16[128,256]{1,0:T(8,128)(2,1)} async-done(((bf16[2048,256]{1,0:T(8,128)(2,1)}), bf16[128,256]{1,0:T(8,128)(2,1)}) %reduce-scatter.11.cloned.1.call-update) | async-done | bytes 65552 | tf_op jit(solution)/shard_map/reduce_scatter | solution.py:291
  1442.9 27.2 %all-reduce.1 = bf16[1024]{0:T(1024)(128)(2,1)S(1)} all-reduce(bf16[1024]{0:T(1024)(128)(2,1)S(1)} %dynamic-update-slice.1), channel_id=1, replica_groups=mesh['dp'=8,'seq'=16] {'seq'}, use_global_device_ids=true, to_apply=%add.1 | all-reduce | flops 1024 | bytes 4096
  1470.2 32.0 %reduce-scatter.13.cloned.1.call-done = bf16[128,256]{1,0:T(8,128)(2,1)} async-done(((bf16[2048,256]{1,0:T(8,128)(2,1)}), bf16[128,256]{1,0:T(8,128)(2,1)}) %reduce-scatter.13.cloned.1.call-update) | async-done | bytes 65552 | tf_op jit(solution)/shard_map/reduce_scatter | solution.py:294
  1502.2 2.4 convolution_convert_fusion.7
  1506.2 48.2 %all-gather.57.cloned.1.call-done = bf16[1024,4096]{1,0:T(8,128)(2,1)} async-done(((bf16[64,4096]{1,0:T(8,128)(2,1)}), bf16[1024,4096]{1,0:T(8,128)(2,1)}) %all-gather.57.cloned.1.call-update) | async-done | bytes 8388624 | tf_op jit(solution)/shard_map/all_gather | solution.py:215
  1554.5 6.7 multiply_reduce_fusion.4
  1562.1 3.3 convolution_convert_fusion.6
  1566.9 5.7 convolution_convert_fusion.4
  1574.2 8.6 convolution_convert_fusion.3
  1584.3 11.2 convolution_convert_fusion.2
  1596.8 11.1 convolution_convert_fusion.1
  1610.1 77.9 %reduce-scatter.29.cloned.1.call-done = bf16[352,2048]{1,0:T(8,128)(2,1)} async-done(((bf16[5632,2048]{1,0:T(8,128)(2,1)}), bf16[352,2048]{1,0:T(8,128)(2,1)}) %reduce-scatter.29.cloned.1.call-update) | async-done | bytes 1441808 | tf_op jit(solution)/shard_map/reduce_scatter | solution.py:251
  1688.0 63.3 %reduce-scatter.17.cloned.1.call-done = bf16[128,256]{1,0:T(8,128)(2,1)} async-done(((bf16[2048,256]{1,0:T(8,128)(2,1)}), bf16[128,256]{1,0:T(8,128)(2,1)}) %reduce-scatter.17.cloned.1.call-update) | async-done | bytes 65552 | tf_op jit(solution)/shard_map/reduce_scatter | solution.py:325
  1751.3 63.0 %reduce-scatter.19.cloned.1.call-done = bf16[128,256]{1,0:T(8,128)(2,1)} async-done(((bf16[2048,256]{1,0:T(8,128)(2,1)}), bf16[128,256]{1,0:T(8,128)(2,1)}) %reduce-scatter.19.cloned.1.call-update) | async-done | bytes 65552 | tf_op jit(solution)/shard_map/reduce_scatter | solution.py:328
  1814.3 67.7 %reduce-scatter.15.cloned.1.call-done = bf16[128,1024]{1,0:T(8,128)(2,1)} async-done(((bf16[2048,1024]{1,0:T(8,128)(2,1)}), bf16[128,1024]{1,0:T(8,128)(2,1)}) %reduce-scatter.15.cloned.1.call-update) | async-done | bytes 262160 | tf_op jit(solution)/shard_map/reduce_scatter | solution.py:322
  1882.1 75.6 %reduce-scatter.21.cloned.1.call-done = bf16[64,4096]{1,0:T(8,128)(2,1)} async-done(((bf16[1024,4096]{1,0:T(8,128)(2,1)}), bf16[64,4096]{1,0:T(8,128)(2,1)}) %reduce-scatter.21.cloned.1.call-update) | async-done | bytes 524304 | tf_op jit(solution)/shard_map/reduce_scatter | solution.py:334
  1957.6 99.2 %reduce-scatter.23.cloned.1.call-done = bf16[256,2048]{1,0:T(8,128)(2,1)} async-done(((bf16[4096,2048]{1,0:T(8,128)(2,1)}), bf16[256,2048]{1,0:T(8,128)(2,1)}) %reduce-scatter.23.cloned.1.call-update) | async-done | bytes 1048592 | tf_op jit(solution)/shard_map/reduce_scatter | solution.py:337
  2056.9 131.2 %reduce-scatter.25.cloned.1.call-done = bf16[128,5632]{1,0:T(8,128)(2,1)} async-done(((bf16[2048,5632]{1,0:T(8,128)(2,1)}), bf16[128,5632]{1,0:T(8,128)(2,1)}) %reduce-scatter.25.cloned.1.call-update) | async-done | bytes 1441808 | tf_op jit(solution)/shard_map/reduce_scatter | solution.py:245
  2188.1 131.1 %reduce-scatter.27.cloned.1.call-done = bf16[128,5632]{1,0:T(8,128)(2,1)} async-done(((bf16[2048,5632]{1,0:T(8,128)(2,1)}), bf16[128,5632]{1,0:T(8,128)(2,1)}) %reduce-scatter.27.cloned.1.call-update) | async-done | bytes 1441808 | tf_op jit(solution)/shard_map/reduce_scatter | solution.py:248
  2320.5 16.6 all-gather.3
  2337.1 14.9 all-gather.61.cloned.1.call-done
  2352.1 2.7 fusion.76
  2354.7 31.6 %all-gather.63.cloned.1.call-done = bf16[2048,256]{1,0:T(8,128)(2,1)} async-done(((bf16[128,256]{1,0:T(8,128)(2,1)}), bf16[2048,256]{1,0:T(8,128)(2,1)}) %all-gather.63.cloned.1.call-update) | async-done | bytes 1048592 | tf_op jit(solution)/shard_map/all_gather | solution.py:213
  2386.3 2.7 fusion.77
  2389.0 36.3 %all-gather.59.cloned.1.call-done = bf16[2048,1024]{1,0:T(8,128)(2,1)} async-done(((bf16[128,1024]{1,0:T(8,128)(2,1)}), bf16[2048,1024]{1,0:T(8,128)(2,1)}) %all-gather.59.cloned.1.call-update) | async-done | bytes 4194320 | tf_op jit(solution)/shard_map/all_gather | solution.py:211
  2425.3 4.6 fusion.52
  2429.9 160.7 %all-reduce.5 = (bf16[2048]{0:T(1024)(128)(2,1)S(1)}, bf16[1024]{0:T(1024)(128)(2,1)S(1)}, bf16[2048]{0:T(1024)(128)(2,1)S(1)}) all-reduce(bf16[2048]{0:T(1024)(128)(2,1)S(1)} %get-tuple-element.315, bf16[1024]{0:T(1024)(128)(2,1)S(1)} %get-tuple-element.317, ...), channel_id=4, replica_groups=mesh['dp'=8,'seq'=16] {'seq'}, use_global_device_ids=true, to_apply=%region_20.21.clone | all-reduce | flops 5120 | bytes 20480
  2590.8 23.5 all-reduce.6
  2617.2 3.3 convert_element_type.248
  (250 shorter events, 71.2 us)
Async XLA Ops:
  7.2 72.0 %copy-start.1 = (bf16[128,2048]{1,0:T(8,128)(2,1)S(1)}, bf16[128,2048]{1,0:T(8,128)(2,1)}, u32[]{:S(2)}) copy-start(bf16[128,2048]{1,0:T(8,128)(2,1)} %param.18) | copy-start | bytes 1572868
  7.2 37.6 %all-gather.25.cloned.1.call-start = ((), (), s32[]{:S(2)}) async-start(), calls=%async_computation.10 | async-start | bytes 1114112 | tf_op jit(solution)/shard_map/all_gather | solution.py:92
  7.9 71.3 %all-gather.33.cloned.1.call-start = ((), (), s32[]{:S(2)}) async-start(), calls=%async_computation.14 | async-start | bytes 1114112 | tf_op jit(solution)/shard_map/all_gather | solution.py:93
  8.7 123.6 %all-gather.29.cloned.1.call-start = ((), (), s32[]{:S(2)}) async-start(), calls=%async_computation.12 | async-start | bytes 4456448 | tf_op jit(solution)/shard_map/all_gather | solution.py:91
  9.4 162.8 %all-gather.31.cloned.1.call-start = ((), (), s32[]{:S(2)}) async-start(), calls=%async_computation.13 | async-start | bytes 8912896 | tf_op jit(solution)/shard_map/all_gather | solution.py:95
  10.0 197.9 %all-gather.27.cloned.1.call-start = ((), (), s32[]{:S(2)}) async-start(), calls=%async_computation.11 | async-start | bytes 1114112 | tf_op jit(solution)/shard_map/all_gather | solution.py:129
  31.2 101.1 %copy-start.23 = (f32[16,1,128]{2,1,0:T(1,128)}, f32[16,1,128]{2,1,0:T(1,128)S(1)}, u32[]{:S(2)}) copy-start(f32[16,1,128]{2,1,0:T(1,128)S(1)} %convert_element_type.253) | copy-start | bytes 24580
  32.1 14.5 copy-start.32
  34.7 97.6 %copy-start.34 = (f32[128]{0:T(128)}, f32[128]{0:T(128)S(1)}, u32[]{:S(2)}) copy-start(f32[128]{0:T(128)S(1)} %get-tuple-element.409) | copy-start | bytes 1540
  47.3 195.3 %all-gather.35.cloned.1.call-start = ((), (), s32[]{:S(2)}) async-start(), calls=%async_computation.15 | async-start | bytes 1114112 | tf_op jit(solution)/shard_map/all_gather | solution.py:130
  81.4 4.2 copy-start.48
  81.4 33.5 %copy-start.42 = (bf16[128]{0:T(256)(128)(2,1)S(1)}, bf16[128]{0:T(256)(128)(2,1)}, u32[]{:S(2)}) copy-start(bf16[128]{0:T(256)(128)(2,1)} %param.27) | copy-start | bytes 772
  81.4 254.5 %all-gather.37.cloned.1.call-start = ((), (), s32[]{:S(2)}) async-start(), calls=%async_computation.16 | async-start | bytes 17825792 | tf_op jit(solution)/shard_map/all_gather | solution.py:96
  82.2 377.8 %all-gather.39.cloned.1.call-start = ((), (), s32[]{:S(2)}) async-start(), calls=%async_computation.17 | async-start | bytes 24510464 | tf_op jit(solution)/shard_map/all_gather | solution.py:98
  82.9 501.0 %all-gather.41.cloned.1.call-start = ((), (), s32[]{:S(2)}) async-start(), calls=%async_computation.18 | async-start | bytes 24510464 | tf_op jit(solution)/shard_map/all_gather | solution.py:99
  83.7 624.2 %all-gather.43.cloned.1.call-start = ((), (), s32[]{:S(2)}) async-start(), calls=%async_computation.19 | async-start | bytes 24510464 | tf_op jit(solution)/shard_map/all_gather | solution.py:100
  84.3 758.6 %all-gather.45.cloned.1.call-start = ((), (), s32[]{:S(2)}) async-start(), calls=%async_computation.20 | async-start | bytes 24510464 | tf_op jit(solution)/shard_map/all_gather | solution.py:220
  114.9 57.3 %copy-start.28 = (f32[1024]{0:T(1024)}, f32[1024]{0:T(1024)S(1)}, u32[]{:S(2)}) copy-start(f32[1024]{0:T(1024)S(1)} %convert_element_type.206) | copy-start | bytes 12292
  135.4 43.6 %copy-start.6 = (f32[128,1024]{1,0:T(8,128)}, f32[128,1024]{1,0:T(8,128)S(1)}, u32[]{:S(2)}) copy-start(f32[128,1024]{1,0:T(8,128)S(1)} %get-tuple-element.415) | copy-start | bytes 1572868
  136.1 43.0 %copy-start.38 = (f32[128]{0:T(128)}, f32[128]{0:T(128)S(1)}, u32[]{:S(2)}) copy-start(f32[128]{0:T(128)S(1)} %get-tuple-element.411) | copy-start | bytes 1540
  336.0 9.7 copy-start.33
  720.4 246.3 %all-gather.47.cloned.1.call-start = ((), (), s32[]{:S(2)}) async-start(), calls=%async_computation.21 | async-start | bytes 24510464 | tf_op jit(solution)/shard_map/all_gather | solution.py:218
  721.0 369.7 %all-gather.49.cloned.1.call-start = ((), (), s32[]{:S(2)}) async-start(), calls=%async_computation.22 | async-start | bytes 24510464 | tf_op jit(solution)/shard_map/all_gather | solution.py:219
  721.8 463.2 %all-gather.55.cloned.1.call-start = ((), (), s32[]{:S(2)}) async-start(), calls=%async_computation.25 | async-start | bytes 17825792 | tf_op jit(solution)/shard_map/all_gather | solution.py:216
  722.3 498.4 %all-gather.51.cloned.1.call-start = ((), (), s32[]{:S(2)}) async-start(), calls=%async_computation.23 | async-start | bytes 1114112 | tf_op jit(solution)/shard_map/all_gather | solution.py:224
  722.9 532.5 %all-gather.53.cloned.1.call-start = ((), (), s32[]{:S(2)}) async-start(), calls=%async_computation.24 | async-start | bytes 1114112 | tf_op jit(solution)/shard_map/all_gather | solution.py:225
  742.7 696.6 %reduce-scatter.11.cloned.1.call-start = ((), (), s32[]{:S(2)}) async-start(), calls=%async_computation.28 | async-start | bytes 1114112 | tf_op jit(solution)/shard_map/reduce_scatter | solution.py:291
  1090.7 15.0 copy-start.4
  1090.7 15.0 copy-start.15
  1090.7 15.0 copy-start.41
  1090.7 15.0 copy-start.47
  1206.7 51.0 %copy-start.25 = (f32[16,128,1]{1,0,2:T(8,128)S(1)}, f32[16,128,1]{1,0,2:T(8,128)}, u32[]{:S(2)}) copy-start(f32[16,128,1]{1,0,2:T(8,128)} %log_add_fusion) | copy-start | bytes 24580
  1265.3 236.9 %reduce-scatter.13.cloned.1.call-start = ((), (), s32[]{:S(2)}) async-start(), calls=%async_computation.30 | async-start | bytes 1114112 | tf_op jit(solution)/shard_map/reduce_scatter | solution.py:294
  1265.8 288.6 %all-gather.57.cloned.1.call-start = ((), (), s32[]{:S(2)}) async-start(), calls=%async_computation.26 | async-start | bytes 8912896 | tf_op jit(solution)/shard_map/all_gather | solution.py:215
  1266.6 421.5 %reduce-scatter.29.cloned.1.call-start = ((), (), s32[]{:S(2)}) async-start(), calls=%async_computation.39 | async-start | bytes 24510464 | tf_op jit(solution)/shard_map/reduce_scatter | solution.py:251
  1279.1 161.9 %copy-start.2 = (bf16[128,2048]{1,0:T(8,128)(2,1)S(1)}, bf16[128,2048]{1,0:T(8,128)(2,1)}, u32[]{:S(2)}) copy-start(bf16[128,2048]{1,0:T(8,128)(2,1)} %param.18) | copy-start | bytes 1572868
  1279.1 161.9 %copy-start.24 = (f32[16,1,128]{2,1,0:T(1,128)S(1)}, f32[16,1,128]{2,1,0:T(1,128)}, u32[]{:S(2)}) copy-start(f32[16,1,128]{2,1,0:T(1,128)} %copy-done.23) | copy-start | bytes 24580
  1279.1 161.9 %copy-start.35 = (f32[128]{0:T(128)S(1)}, f32[128]{0:T(128)}, u32[]{:S(2)}) copy-start(f32[128]{0:T(128)} %copy-done.34) | copy-start | bytes 1540
  1279.2 163.5 %copy-start.49 = (bf16[64]{0:T(256)(128)(2,1)S(1)}, bf16[64]{0:T(256)(128)(2,1)}, u32[]{:S(2)}) copy-start(bf16[64]{0:T(256)(128)(2,1)} %param.24) | copy-start | bytes 388
  1279.2 472.2 %reduce-scatter.17.cloned.1.call-start = ((), (), s32[]{:S(2)}) async-start(), calls=%async_computation.33 | async-start | bytes 1114112 | tf_op jit(solution)/shard_map/reduce_scatter | solution.py:325
  1441.1 63.7 %copy-start.20 = (bf16[128,256]{1,0:T(8,128)(2,1)}, bf16[128,256]{1,0:T(8,128)(2,1)S(1)}, u32[]{:S(2)}) copy-start(bf16[128,256]{1,0:T(8,128)(2,1)S(1)} %fusion.57) | copy-start | bytes 196612
  1442.6 371.7 %reduce-scatter.19.cloned.1.call-start = ((), (), s32[]{:S(2)}) async-start(), calls=%async_computation.34 | async-start | bytes 1114112 | tf_op jit(solution)/shard_map/reduce_scatter | solution.py:328
  1504.6 377.5 %reduce-scatter.15.cloned.1.call-start = ((), (), s32[]{:S(2)}) async-start(), calls=%async_computation.32 | async-start | bytes 4456448 | tf_op jit(solution)/shard_map/reduce_scatter | solution.py:322
  1504.9 49.5 %copy-start.7 = (f32[128,1024]{1,0:T(8,128)S(1)}, f32[128,1024]{1,0:T(8,128)}, u32[]{:S(2)}) copy-start(f32[128,1024]{1,0:T(8,128)} %copy-done.6) | copy-start | bytes 1572868
  1504.9 49.5 %copy-start.39 = (f32[128]{0:T(128)S(1)}, f32[128]{0:T(128)}, u32[]{:S(2)}) copy-start(f32[128]{0:T(128)} %copy-done.38) | copy-start | bytes 1540
  1554.5 6.7 copy-start.46
  1565.4 392.2 %reduce-scatter.21.cloned.1.call-start = ((), (), s32[]{:S(2)}) async-start(), calls=%async_computation.35 | async-start | bytes 8912896 | tf_op jit(solution)/shard_map/reduce_scatter | solution.py:334
  1572.6 484.2 %reduce-scatter.23.cloned.1.call-start = ((), (), s32[]{:S(2)}) async-start(), calls=%async_computation.36 | async-start | bytes 17825792 | tf_op jit(solution)/shard_map/reduce_scatter | solution.py:337
  1582.8 605.3 %reduce-scatter.25.cloned.1.call-start = ((), (), s32[]{:S(2)}) async-start(), calls=%async_computation.37 | async-start | bytes 24510464 | tf_op jit(solution)/shard_map/reduce_scatter | solution.py:245
  1595.5 723.7 %reduce-scatter.27.cloned.1.call-start = ((), (), s32[]{:S(2)}) async-start(), calls=%async_computation.38 | async-start | bytes 24510464 | tf_op jit(solution)/shard_map/reduce_scatter | solution.py:248
  1608.0 744.1 %all-gather.61.cloned.1.call-start = ((), (), s32[]{:S(2)}) async-start(), calls=%async_computation.29 | async-start | bytes 1114112 | tf_op jit(solution)/shard_map/all_gather | solution.py:212
  1608.7 777.6 %all-gather.63.cloned.1.call-start = ((), (), s32[]{:S(2)}) async-start(), calls=%async_computation.31 | async-start | bytes 1114112 | tf_op jit(solution)/shard_map/all_gather | solution.py:213
  1609.5 815.8 %all-gather.59.cloned.1.call-start = ((), (), s32[]{:S(2)}) async-start(), calls=%async_computation.27 | async-start | bytes 4456448 | tf_op jit(solution)/shard_map/all_gather | solution.py:211
  1610.1 1007.2 %all-reduce.10.cloned.1.call-start = ((), (), s32[]{:S(2)}) async-start(), calls=%async_computation.40 | async-start | bytes 12582912 | tf_op jit(solution)/shard_map/psum | solution.py:343
  2319.2 32.8 %copy-start.21 = (bf16[128,256]{1,0:T(8,128)(2,1)S(1)}, bf16[128,256]{1,0:T(8,128)(2,1)}, u32[]{:S(2)}) copy-start(bf16[128,256]{1,0:T(8,128)(2,1)} %copy-done.20) | copy-start | bytes 196612
  2319.2 67.1 %copy-start.27 = (bf16[128,256]{1,0:T(8,128)(2,1)S(1)}, bf16[128,256]{1,0:T(8,128)(2,1)}, u32[]{:S(2)}) copy-start(bf16[128,256]{1,0:T(8,128)(2,1)} %reduce-scatter.13.cloned.1.call-done) | copy-start | bytes 196612
  2319.2 106.0 %copy-start.14 = (bf16[128,1024]{1,0:T(8,128)(2,1)S(1)}, bf16[128,1024]{1,0:T(8,128)(2,1)}, u32[]{:S(2)}) copy-start(bf16[128,1024]{1,0:T(8,128)(2,1)} %copy-done.13) | copy-start | bytes 786436
  2319.3 106.0 %copy-start.36 = (f32[128]{0:T(128)S(1)}, f32[128]{0:T(128)}, u32[]{:S(2)}) copy-start(f32[128]{0:T(128)} %copy-done.34) | copy-start | bytes 1540
  2425.3 4.6 copy-start.37
  2425.3 190.5 %copy-start.45 = (f32[128]{0:T(128)S(1)}, f32[128]{0:T(128)}, u32[]{:S(2)}) copy-start(f32[128]{0:T(128)} %get-tuple-element.408) | copy-start | bytes 1540
  2617.2 3.3 copy-start.18
  2622.5 3.5 copy-start.22
  2624.4 3.5 copy-start.31
  2624.4 4.1 copy-start.30
  (17 other events, 27.2 us)
Sparse Core Ops, SparseCore 0:
  9.7 35.0 all-gather.24
  46.5 32.6 all-gather.32
  80.9 37.6 all-gather.28
  120.1 52.0 all-gather.30
  174.3 33.5 all-gather.26
  210.1 32.5 all-gather.34
  244.3 91.5 all-gather.36
  337.7 122.2 all-gather.38
  461.7 122.2 all-gather.40
  585.5 122.2 all-gather.42
  720.5 122.2 all-gather.44
  844.4 122.2 all-gather.46
  968.4 122.2 all-gather.48
  1092.3 92.6 all-gather.54
  1187.1 33.5 all-gather.50
  1222.8 32.5 all-gather.52
  1265.4 173.8 reduce-scatter.10
  1442.2 59.9 reduce-scatter.12
  1503.9 50.5 all-gather.56
  1556.7 131.2 reduce-scatter.28
  1691.0 60.2 reduce-scatter.16
  1754.4 59.8 reduce-scatter.18
  1816.7 65.2 reduce-scatter.14
  1884.3 73.2 reduce-scatter.20
  1960.0 96.7 reduce-scatter.22
  2059.1 128.8 reduce-scatter.24
  2190.3 128.8 reduce-scatter.26
  2320.9 31.0 all-gather.60
  2353.8 32.5 all-gather.62
  2387.9 37.3 all-gather.58
  2428.4 148.8 all-reduce.9
where the time goes:
time: 2650 us; the launch traced here: 2640 us
  waiting for transfers between devices  2050 us (77%)
  blocking collectives  313 us (12%)
  matrix products  203 us (8%)
  other arithmetic  35 us (1%)
    unnamed x3, blocking collectives  217 us
    reduce_scatter x1, waiting for transfers between devices, shards(): lax.psum_scatter(key_grad_sum.astype(jnp.bfloat16), 'seq', scatter_dimens...  160 us
    reduce_scatter x1, waiting for transfers between devices, shards(): lax.psum_scatter(gate_grad.astype(jnp.bfloat16), 'seq', scatter_dimension...  131 us
    reduce_scatter x1, waiting for transfers between devices, shards(): lax.psum_scatter(lift_grad.astype(jnp.bfloat16), 'seq', scatter_dimension...  131 us
    all_gather x1, waiting for transfers between devices, shards(): lax.all_gather(gate_proj, 'seq', axis=0, tiled=True)  113 us
    all_gather x1, waiting for transfers between devices, shards(): lax.all_gather(up_proj, 'seq', axis=0, tiled=True)  111 us
    all_gather x1, waiting for transfers between devices, shards(): lax.all_gather(late[9], 'seq', axis=0, tiled=True)  111 us
    all_gather x1, waiting for transfers between devices, shards(): lax.all_gather(down_proj, 'seq', axis=0, tiled=True)  109 us
  transfers between devices with their start and end apart: 31, of which 29 were waited for; matrix products, arithmetic and copies ran while one was open for 8% of the time, Pallas kernels for 0%

commit v1 on v0

v1 whole, which is shorter than its diff:
```python
import functools

import jax
import jax.numpy as jnp
from jax import lax
from jax.experimental import pallas as pl
from jax.experimental.pallas import tpu as pltpu
from jax.sharding import PartitionSpec as P

HEADS = 16
NORM_EPSILON = 1e-05
F32 = jnp.float32
BF16 = jnp.bfloat16

Y, Z, CORES = 2, 4, 2
CHIPS = Y * Z
X, V = 4, 2
OFFSETS = ((0, 0), (0, 1), (0, 3), (1, 0), (0, 2), (1, 1), (1, 3), (1, 2))
WAVES = ((0, 4), (4, 7), (7, 8))
KEY_CHUNK = 512


def shift(value, dy, dz, dc=0):
    pairs = []
    for y in range(Y):
        for z in range(Z):
            for c in range(CORES):
                target = (((y + dy) % Y) * Z + (z + dz) % Z) * CORES + (c + dc) % CORES
                pairs.append(((y * Z + z) * CORES + c, target))
    return lax.ppermute(value, "seq", pairs)


def fetch(value, dy, dz):
    return shift(value, -dy, -dz)


def sibling(value):
    return shift(value, 0, 0, 1)


def dp_shift(value, dv, dx):
    pairs = []
    for v in range(V):
        for x in range(X):
            pairs.append((v * X + x, ((v + dv) % V) * X + (x + dx) % X))
    return lax.ppermute(value, "dp", pairs)


def rows(value, start, stop):
    return lax.slice_in_dim(value, start, stop, axis=0)


def gather_lane(block):
    half = block.shape[0] // 2
    cut_a = block.shape[0] // 4
    cut_b = cut_a + (block.shape[0] - cut_a) // 2
    z_next, z_back, across = fetch(block, 0, 1), fetch(block, 0, -1), fetch(block, 1, 0)
    from_next = fetch(jnp.concatenate([rows(z_next, 0, half), rows(across, half, 2 * half)]), 0, 1)
    from_back = fetch(
        jnp.concatenate([rows(z_back, half, 2 * half), rows(across, half, 2 * half)]), 0, -1
    )
    from_across = fetch(jnp.concatenate([rows(z_next, 0, half), rows(z_back, 0, half)]), 1, 0)
    z_far = jnp.concatenate([rows(from_next, 0, half), rows(from_back, 0, half)])
    across_next = jnp.concatenate([rows(from_across, 0, half), rows(from_next, half, 2 * half)])
    across_back = jnp.concatenate(
        [rows(from_across, half, 2 * half), rows(from_back, half, 2 * half)]
    )
    far_a = fetch(rows(z_far, 0, cut_a), 1, 0)
    far_b = fetch(rows(across_next, cut_a, cut_b), 0, 1)
    far_c = fetch(rows(across_back, cut_b, 2 * half), 0, -1)
    across_far = jnp.concatenate([far_a, far_b, far_c])
    return (block, z_next, z_back, across, z_far, across_next, across_back, across_far)


def scatter_lane(parts):
    own, z_next, z_back, across, z_far, across_next, across_back, across_far = parts
    count = own.shape[0]
    half = count // 2
    cut_a = count // 4
    cut_b = cut_a + (count - cut_a) // 2
    far = across_far.astype(BF16)
    got_a = shift(rows(far, 0, cut_a), 1, 0).astype(F32)
    got_b = shift(rows(far, cut_a, cut_b), 0, 1).astype(F32)
    got_c = shift(rows(far, cut_b, count), 0, -1).astype(F32)
    z_far = jnp.concatenate([rows(z_far, 0, cut_a) + got_a, rows(z_far, cut_a, count)])
    across_next = jnp.concatenate(
        [
            rows(across_next, 0, cut_a),
            rows(across_next, cut_a, cut_b) + got_b,
            rows(across_next, cut_b, count),
        ]
    )
    across_back = jnp.concatenate(
        [rows(across_back, 0, cut_b), rows(across_back, cut_b, count) + got_c]
    )
    to_next = jnp.concatenate([rows(z_far, 0, half), rows(across_next, half, count)])
    to_back = jnp.concatenate([rows(z_far, half, count), rows(across_back, half, count)])
    to_across = jnp.concatenate([rows(across_next, 0, half), rows(across_back, 0, half)])
    got_next = shift(to_next.astype(BF16), 0, 1).astype(F32)
    got_back = shift(to_back.astype(BF16), 0, -1).astype(F32)
    got_across = shift(to_across.astype(BF16), 1, 0).astype(F32)
    z_next = jnp.concatenate(
        [
            rows(z_next, 0, half) + rows(got_next, 0, half) + rows(got_across, 0, half),
            rows(z_next, half, count),
        ]
    )
    z_back = jnp.concatenate(
        [
            rows(z_back, 0, half) + rows(got_across, half, count),
            rows(z_back, half, count) + rows(got_back, 0, half),
        ]
    )
    across = jnp.concatenate(
        [
            rows(across, 0, half),
            rows(across, half, count) + rows(got_next, half, count) + rows(got_back, half, count),
        ]
    )
    return (
        own
        + shift(z_next.astype(BF16), 0, 1).astype(F32)
        + shift(z_back.astype(BF16), 0, -1).astype(F32)
        + shift(across.astype(BF16), 1, 0).astype(F32)
    )


def dp_sum(value):
    x = lax.axis_index("dp") % X
    count = value.shape[0] // X

    def piece(offset):
        return lax.dynamic_slice_in_dim(value, ((x + offset) % X) * count, count, 0)

    total = (
        piece(0).astype(F32)
        + dp_shift(piece(1).astype(BF16), 0, 1).astype(F32)
        + dp_shift(piece(3).astype(BF16), 0, -1).astype(F32)
        + dp_shift(piece(2).astype(BF16), 0, 2).astype(F32)
    )
    total = total + dp_shift(total.astype(BF16), 1, 0).astype(F32)
    low = total.astype(BF16)
    result = jnp.zeros(value.shape, F32)
    parts = (total, dp_shift(low, 0, -1), dp_shift(low, 0, 1), dp_shift(low, 0, 2))
    for offset, part in zip((0, 1, 3, 2), parts):
        result = lax.dynamic_update_slice_in_dim(
            result, part.astype(F32), ((x + offset) % X) * count, 0
        )
    return result


def inverse_rms(values):
    return lax.rsqrt(jnp.mean(values * values, axis=-1, keepdims=True) + NORM_EPSILON)


def rms_back(values, inv_root, gain_row, grad_normed):
    scaled = grad_normed * gain_row
    gain_grad = jnp.sum(grad_normed * values * inv_root, axis=0)
    grad_values = inv_root * scaled - values * inv_root**3 * jnp.mean(
        scaled * values, axis=-1, keepdims=True
    )
    return (grad_values, gain_grad)


def layout(lengths, token_index):
    doc_ends = jnp.cumsum(lengths)
    starts = doc_ends - lengths
    doc_id = jnp.sum((token_index[:, None] >= doc_ends[None, :]).astype(jnp.int32), axis=1)
    numbers = jnp.arange(lengths.shape[0], dtype=jnp.int32)
    doc_start = jnp.sum(jnp.where(doc_id[:, None] == numbers[None, :], starts[None, :], 0), axis=1)
    return doc_start


def rope_tables(position, head_width):
    half_width = head_width // 2
    frequency = 10000.0 ** (-(2.0 * jnp.arange(half_width, dtype=F32)) / head_width)
    angles = position.astype(F32)[:, None] * frequency[None, :]
    return (jnp.cos(angles), jnp.sin(angles))


def rotate(values, cosine, sine):
    half_width = cosine.shape[-1]
    low, high = values[..., :half_width], values[..., half_width:]
    return jnp.concatenate([low * cosine - high * sine, high * cosine + low * sine], axis=-1)


def rotate_back(grads, cosine, sine):
    return rotate(grads, cosine, -sine)


def dot(left, right):
    return jnp.dot(left, right, preferred_element_type=F32)


def dot_nt(left, right):
    return lax.dot_general(left, right, (((1,), (1,)), ((), ())), preferred_element_type=F32)


def dot_tn(left, right):
    return lax.dot_general(left, right, (((0,), (0,)), ((), ())), preferred_element_type=F32)


def order_keys(source_own, source_sib, target, slots, own_lane, width):
    for chip in range(CHIPS):
        slot = slots[chip]
        target[pl.ds(chip * 2 * width + own_lane * width, width), :] = source_own[slot]
        target[pl.ds(chip * 2 * width + (1 - own_lane) * width, width), :] = source_sib[slot]


def masked(scores, first_key, place, begin):
    key = first_key + lax.broadcasted_iota(jnp.int32, scores.shape, 0)
    return jnp.where((key >= begin) & (key <= place), scores, -1e30)


def attend_kernel(
    meta, q_ref, ko_ref, ks_ref, vo_ref, vs_ref, place_ref, begin_ref, out_ref, log_ref, keys, values
):
    width = q_ref.shape[1]
    own_lane = meta[16]
    order_keys(ko_ref, ks_ref, keys, meta, own_lane, width)
    order_keys(vo_ref, vs_ref, values, meta, own_lane, width)
    head = keys.shape[1]

    @pl.loop(0, CHIPS)
    def per_block(block):
        query = jnp.concatenate([q_ref[block, :, :head], q_ref[block, :, head:]], axis=0)
        place, begin = place_ref[block], begin_ref[block]
        last = (meta[8 + block] * 2 + own_lane + 1) * width

        def chunk(step, carry):
            top, total, mixed = carry
            start = pl.multiple_of(step * KEY_CHUNK, KEY_CHUNK)
            key_chunk = keys[pl.ds(start, KEY_CHUNK), :]
            scores = masked(dot_nt(key_chunk, query), start, place, begin)
            new_top = jnp.maximum(top, jnp.max(scores, axis=0, keepdims=True))
            factor = jnp.exp(top - new_top)
            weights = jnp.exp(scores - new_top)
            total = total * factor + jnp.sum(weights, axis=0, keepdims=True)
            mixed = mixed * factor + dot_tn(
                values[pl.ds(start, KEY_CHUNK), :], weights.astype(BF16)
            )
            return (new_top, total, mixed)

        rows_all = query.shape[0]
        top, total, mixed = lax.fori_loop(
            0,
            (last + KEY_CHUNK - 1) // KEY_CHUNK,
            chunk,
            (
                jnp.full((1, rows_all), -1e30, F32),
                jnp.zeros((1, rows_all), F32),
                jnp.zeros((head, rows_all), F32),
            ),
        )
        result = (mixed / total).T.astype(BF16)
        out_ref[block, :, :head] = result[:width]
        out_ref[block, :, head:] = result[width:]
        log_ref[block] = top + jnp.log(total)


def attend_back_kernel(
    meta,
    q_ref,
    ko_ref,
    ks_ref,
    vo_ref,
    vs_ref,
    place_ref,
    begin_ref,
    log_ref,
    out_ref,
    grad_ref,
    gq_ref,
    own_ref,
    sib_ref,
    keys,
    values,
    key_grad,
    value_grad,
):
    width = q_ref.shape[1]
    own_lane = meta[16]
    order_keys(ko_ref, ks_ref, keys, meta, own_lane, width)
    order_keys(vo_ref, vs_ref, values, meta, own_lane, width)
    head = keys.shape[1]
    key_grad[...] = jnp.zeros_like(key_grad)
    value_grad[...] = jnp.zeros_like(value_grad)

    @pl.loop(0, CHIPS)
    def per_block(block):
        query = jnp.concatenate([q_ref[block, :, :head], q_ref[block, :, head:]], axis=0)
        grad = jnp.concatenate([grad_ref[block, :, :head], grad_ref[block, :, head:]], axis=0)
        out = jnp.concatenate([out_ref[block, :, :head], out_ref[block, :, head:]], axis=0)
        row_dot = jnp.sum((grad.astype(F32) * out.astype(F32)).T, axis=0, keepdims=True)
        place, begin, log_total = place_ref[block], begin_ref[block], log_ref[block]
        last = (meta[8 + block] * 2 + own_lane + 1) * width

        def chunk(step, acc):
            start = pl.multiple_of(step * KEY_CHUNK, KEY_CHUNK)
            span = pl.ds(start, KEY_CHUNK)
            key_chunk = keys[span, :]
            scores = masked(dot_nt(key_chunk, query), start, place, begin)
            probs = jnp.exp(scores - log_total)
            grad_probs = dot_nt(values[span, :], grad)
            grad_scores = (probs * (grad_probs - row_dot)).astype(BF16)
            value_grad[span, :] += dot(probs.astype(BF16), grad)
            key_grad[span, :] += dot(grad_scores, query)
            return acc + dot_tn(grad_scores, key_chunk)

        acc = lax.fori_loop(
            0,
            (last + KEY_CHUNK - 1) // KEY_CHUNK,
            chunk,
            jnp.zeros((query.shape[0], head), F32),
        )
        acc = acc * (head**-0.5)
        gq_ref[block, :, :head] = acc[:width]
        gq_ref[block, :, head:] = acc[width:]

    for chip in range(CHIPS):
        slot = meta[chip]
        own_rows = pl.ds(chip * 2 * width + own_lane * width, width)
        sib_rows = pl.ds(chip * 2 * width + (1 - own_lane) * width, width)
        own_ref[slot, :, :head] = key_grad[own_rows, :]
        own_ref[slot, :, head:] = value_grad[own_rows, :]
        sib_ref[slot, :, :head] = key_grad[sib_rows, :].astype(BF16)
        sib_ref[slot, :, head:] = value_grad[sib_rows, :].astype(BF16)


def kernel_specs(count):
    smem = pl.BlockSpec(memory_space=pltpu.SMEM)
    vmem = pl.BlockSpec(memory_space=pltpu.VMEM)
    return [smem] + [vmem] * count


def attend(meta, queries, key_own, key_sib, value_own, value_sib, place, begin):
    width, head = queries.shape[1], key_own.shape[2]
    group = CHIPS * CORES * width
    return pl.pallas_call(
        attend_kernel,
        out_shape=(
            jax.ShapeDtypeStruct(queries.shape, BF16),
            jax.ShapeDtypeStruct(place.shape, F32),
        ),
        in_specs=kernel_specs(7),
        out_specs=tuple(kernel_specs(2)[1:]),
        scratch_shapes=[pltpu.VMEM((group, head), BF16)] * 2,
        compiler_params=pltpu.CompilerParams(vmem_limit_bytes=40 * 2**20),
        cost_estimate=pl.CostEstimate(
            flops=2_600_000_000, bytes_accessed=5_000_000, transcendentals=2_600_000
        ),
        name="attend",
    )(meta, queries, key_own, key_sib, value_own, value_sib, place, begin)


def attend_back(meta, queries, key_own, key_sib, value_own, value_sib, place, begin, log, out, grad):
    width, head = queries.shape[1], key_own.shape[2]
    group = CHIPS * CORES * width
    return pl.pallas_call(
        attend_back_kernel,
        out_shape=(
            jax.ShapeDtypeStruct(queries.shape, F32),
            jax.ShapeDtypeStruct((CHIPS, width, 2 * head), F32),
            jax.ShapeDtypeStruct((CHIPS, width, 2 * head), BF16),
        ),
        in_specs=kernel_specs(10),
        out_specs=tuple(kernel_specs(3)[1:]),
        scratch_shapes=[pltpu.VMEM((group, head), BF16)] * 2 + [pltpu.VMEM((group, head), F32)] * 2,
        compiler_params=pltpu.CompilerParams(vmem_limit_bytes=48 * 2**20),
        cost_estimate=pl.CostEstimate(
            flops=6_500_000_000, bytes_accessed=10_000_000, transcendentals=2_600_000
        ),
        name="attend_back",
    )(meta, queries, key_own, key_sib, value_own, value_sib, place, begin, log, out, grad)


def shards(
    tokens,
    doc_lengths,
    first_gain,
    query_down,
    key_proj,
    value_proj,
    query_gain,
    query_up,
    out_proj,
    second_gain,
    gate_proj,
    up_proj,
    down_proj,
    cotangent,
):
    width, model = tokens.shape
    latent_width = query_down.shape[1]
    head = key_proj.shape[1]
    hidden_width = gate_proj.shape[1] // (CHIPS * CORES)
    small_width = 128
    lane_width = latent_width + 2 * head

    me = lax.axis_index("seq")
    core = me % CORES
    chip = me // CORES
    z, y = chip % Z, chip // Z
    chip_at = [((y + dy) % Y) * Z + (z + dz) % Z for dy, dz in OFFSETS]

    gains = jnp.stack(
        [first_gain, second_gain, jnp.pad(query_gain, (0, width - query_gain.shape[0]))], axis=1
    )
    packed = jnp.concatenate(
        [query_down, key_proj, value_proj, jnp.pad(gains, ((0, 0), (0, small_width - 3)))], axis=1
    )
    weights = lax.all_gather(packed, "seq", axis=0, tiled=True)

    def swap(weight):
        depth = weight.shape[0]
        parts = weight.reshape(depth, CHIPS * CORES, -1).transpose(1, 0, 2)
        return lax.all_to_all(parts, "seq", 0, 0).reshape(CHIPS * CORES * depth, -1)

    up_own = swap(query_up)
    gate_lift_own = swap(
        jnp.concatenate(
            [
                gate_proj.reshape(width, CHIPS * CORES, hidden_width),
                up_proj.reshape(width, CHIPS * CORES, hidden_width),
            ],
            axis=2,
        )
    )
    query_up_chip = jnp.concatenate([up_own, sibling(up_own)], axis=1)
    out_chip = jnp.concatenate([out_proj, sibling(out_proj)], axis=0)
    gate_lift_sib = sibling(gate_lift_own)
    gate_chip = jnp.concatenate(
        [gate_lift_own[:, :hidden_width], gate_lift_sib[:, :hidden_width]], axis=1
    )
    lift_chip = jnp.concatenate(
        [gate_lift_own[:, hidden_width:], gate_lift_sib[:, hidden_width:]], axis=1
    )
    down_chip = jnp.concatenate([down_proj, sibling(down_proj)], axis=0)

    lengths = doc_lengths[0]
    blocks = jnp.stack([place * CORES + core for place in chip_at])
    token_index = blocks[:, None] * width + jnp.arange(width, dtype=jnp.int32)[None, :]
    doc_start = layout(lengths, token_index.reshape(-1)).reshape(token_index.shape)
    cosine, sine = rope_tables((token_index - doc_start).reshape(-1), head)
    slot_of = [
        sum(jnp.where(chip_at[slot] == number, slot, 0) for slot in range(CHIPS))
        for number in range(CHIPS)
    ]
    meta = jnp.stack(slot_of + chip_at + [core]).astype(jnp.int32)
    place_row = jnp.tile(token_index, (1, 2))[:, None, :]
    begin_row = jnp.tile(doc_start, (1, 2))[:, None, :]

    tokens_float = tokens.astype(F32)
    inv_one = inverse_rms(tokens_float)
    gain_rows = weights[:, lane_width : lane_width + 3].astype(F32).T
    gain_one, gain_two = gain_rows[0:1], gain_rows[1:2]
    gain_query = gain_rows[2].reshape(-1, width)[:, : query_gain.shape[0]].reshape(1, -1)
    normed = (tokens_float * inv_one * gain_one).astype(BF16)
    first = dot(normed, weights)
    latent = first[:, :latent_width]
    inv_latent = inverse_rms(latent)
    latent_n = (latent * inv_latent * gain_query).astype(BF16)
    cos_own, sin_own = cosine[:width], sine[:width]
    key_rot = rotate(first[:, latent_width : latent_width + head], cos_own, sin_own).astype(BF16)
    value_low = first[:, latent_width + head : lane_width].astype(BF16)

    lane = gather_lane(jnp.concatenate([latent_n, key_rot, value_low], axis=1))
    lane_all = jnp.concatenate(lane, axis=0)
    latent_lane = lane_all[:, :latent_width]
    key_value_own = lane_all[:, latent_width:]
    key_value_sib = sibling(key_value_own).reshape(CHIPS, width, 2 * head)
    key_value_own = key_value_own.reshape(CHIPS, width, 2 * head)
    key_own, value_own = key_value_own[..., :head], key_value_own[..., head:]
    key_sib, value_sib = key_value_sib[..., :head], key_value_sib[..., head:]

    queries = dot(latent_lane, query_up_chip).reshape(CHIPS * width, 2, head)
    query_rot = rotate(queries, cosine[:, None, :], sine[:, None, :]) * head**-0.5
    query_rot = query_rot.astype(BF16).reshape(CHIPS, width, 2 * head)
    attended, log_total = attend(
        meta, query_rot, key_own, key_sib, value_own, value_sib, place_row, begin_row
    )
    attended_rows = attended.reshape(CHIPS * width, 2 * head)
    mixed = dot(attended_rows, out_chip).reshape(CHIPS, width, model)
    residual = tokens_float + scatter_lane([mixed[i] for i in range(CHIPS)])
    inv_two = inverse_rms(residual)
    normed_two = (residual * inv_two * gain_two).astype(BF16)

    cot_lane = gather_lane(cotangent)
    normed_lane = gather_lane(normed_two)
    wave_values = []
    fed, back = [], []
    for first_block, last_block in WAVES:
        normed_wave = jnp.concatenate(normed_lane[first_block:last_block], axis=0)
        cot_wave = jnp.concatenate(cot_lane[first_block:last_block], axis=0)
        gate_values = dot(normed_wave, gate_chip)
        up_values = dot(normed_wave, lift_chip)
        grad_hidden = dot_nt(cot_wave, down_chip)
        sigmoid = jax.nn.sigmoid(gate_values)
        hidden = (gate_values * sigmoid * up_values).astype(BF16)
        grad_gate = (
            grad_hidden * up_values * sigmoid * (1.0 + gate_values * (1.0 - sigmoid))
        ).astype(BF16)
        grad_up = (grad_hidden * gate_values * sigmoid).astype(BF16)
        wave_values.append((normed_wave, cot_wave, hidden, grad_gate, grad_up))
        back_wave = dot_nt(grad_gate, gate_chip) + dot_nt(grad_up, lift_chip)
        fed_wave = dot(hidden, down_chip)
        for block in range(last_block - first_block):
            back.append(rows(back_wave, block * width, (block + 1) * width))
            fed.append(rows(fed_wave, block * width, (block + 1) * width))
    grad_normed_two = scatter_lane(back)
    layer_out = (residual + scatter_lane(fed)).astype(BF16)
    normed_two_all, cot_all, hidden_all, grad_gate_all, grad_up_all = (
        jnp.concatenate([wave[i] for wave in wave_values], axis=0) for i in range(5)
    )
    gate_grad = dot_tn(normed_two_all, grad_gate_all)
    lift_grad = dot_tn(normed_two_all, grad_up_all)
    down_grad = dot_tn(hidden_all, cot_all)

    grad_two, second_grad = rms_back(residual, inv_two, gain_two, grad_normed_two)
    grad_residual = cotangent.astype(F32) + grad_two

    branch_all = jnp.concatenate(gather_lane(grad_residual.astype(BF16)), axis=0)
    grad_attended = dot_nt(branch_all, out_chip).astype(BF16).reshape(CHIPS, width, 2 * head)
    out_grad = dot_tn(attended_rows, branch_all)
    grad_qrot, key_value_grad, key_value_grad_sib = attend_back(
        meta,
        query_rot,
        key_own,
        key_sib,
        value_own,
        value_sib,
        place_row,
        begin_row,
        log_total,
        attended,
        grad_attended,
    )
    key_value_grad = key_value_grad + sibling(key_value_grad_sib).astype(F32)
    grad_queries = rotate_back(
        grad_qrot.reshape(CHIPS * width, 2, head), cosine[:, None, :], sine[:, None, :]
    )
    grad_queries = grad_queries.astype(BF16).reshape(CHIPS * width, 2 * head)
    up_grad = dot_tn(latent_lane, grad_queries)
    latent_parts = dot_nt(grad_queries, query_up_chip).reshape(CHIPS, width, latent_width)
    summed = scatter_lane(
        [jnp.concatenate([latent_parts[i], key_value_grad[i]], axis=1) for i in range(CHIPS)]
    )
    grad_keys = rotate_back(
        summed[:, latent_width : latent_width + head], cos_own, sin_own
    ).astype(BF16)
    grad_values = summed[:, latent_width + head :].astype(BF16)
    grad_latent, query_gain_grad = rms_back(
        latent, inv_latent, gain_query, summed[:, :latent_width]
    )
    grad_first = jnp.concatenate([grad_latent.astype(BF16), grad_keys, grad_values], axis=1)
    grad_normed = dot_nt(jnp.pad(grad_first, ((0, 0), (0, small_width))), weights)
    grad_one, first_grad = rms_back(tokens_float, inv_one, gain_one, grad_normed)
    input_grad = grad_residual + grad_one

    count = CHIPS * CORES
    gain_grads = jnp.concatenate(
        [
            first_grad.reshape(count, -1),
            second_grad.reshape(count, -1),
            query_gain_grad.reshape(count, -1),
        ],
        axis=1,
    )
    gain_cols = gain_grads.size // width
    gain_grads = gain_grads.reshape(width, gain_cols).astype(BF16)
    first_lane = jnp.concatenate(
        gather_lane(
            jnp.concatenate(
                [grad_first, jnp.pad(gain_grads, ((0, 0), (0, small_width - gain_cols)))], axis=1
            )
        ),
        axis=0,
    )
    columns = []
    for dy, dz in OFFSETS:
        wanted = ((y - dy) % Y) * Z + (z - dz) % Z
        part = lax.dynamic_slice_in_dim(normed, wanted * 2 * width, 2 * width, 1)
        columns.append(part if (dy, dz) == (0, 0) else fetch(part, dy, dz))
    first_weights = dot_tn(jnp.concatenate(columns, axis=0), first_lane)
    gain_sums = jnp.sum(
        first_lane[:, lane_width : lane_width + gain_cols]
        .astype(F32)
        .reshape(CHIPS, width, gain_cols),
        axis=0,
    )
    gain_sums = gain_sums + sibling(gain_sums)
    own_first = lax.dynamic_slice_in_dim(first_weights, core * width, width, 0)
    sib_first = lax.dynamic_slice_in_dim(first_weights, (1 - core) * width, width, 0)
    own_first = own_first + sibling(sib_first.astype(BF16)).astype(F32)
    own_gains = lax.dynamic_slice_in_dim(gain_sums, me * (width // count), width // count, 0)
    tail = dp_sum(
        jnp.concatenate(
            [
                own_first[:, :lane_width],
                jnp.pad(
                    own_gains, ((0, width - width // count), (0, small_width - gain_cols))
                ),
            ],
            axis=1,
        )
    )
    own_gains = tail[: width // count, lane_width : lane_width + gain_cols].reshape(-1)

    def combine(grad, axis):
        size = grad.shape[axis] // 2
        own = lax.slice_in_dim(grad, 0, size, axis=axis)
        other = lax.slice_in_dim(grad, size, 2 * size, axis=axis)
        return own + sibling(other.astype(BF16)).astype(F32)

    def swap_back(grad):
        depth = grad.shape[0] // count
        parts = lax.all_to_all(grad.astype(BF16).reshape(count, depth, -1), "seq", 0, 0)
        return parts

    gate_lift_grad = jnp.concatenate([combine(gate_grad, 1), combine(lift_grad, 1)], axis=1)
    gate_lift_grad = swap_back(gate_lift_grad)
    gate_own = gate_lift_grad[..., :hidden_width].transpose(1, 0, 2).reshape(width, -1)
    lift_own = gate_lift_grad[..., hidden_width:].transpose(1, 0, 2).reshape(width, -1)
    up_own_grad = swap_back(combine(up_grad, 1))
    up_own_grad = up_own_grad.transpose(1, 0, 2).reshape(query_up.shape)
    gate_sum, lift_sum, down_sum = lax.psum(
        (gate_own, lift_own, combine(down_grad, 0).astype(BF16)), "dp"
    )
    out_sum, up_sum = lax.psum((combine(out_grad, 0).astype(BF16), up_own_grad), "dp")

    def wide(value):
        return value.astype(F32)

    return (
        layer_out,
        input_grad,
        own_gains[:width],
        tail[:, :latent_width],
        tail[:, latent_width : latent_width + head],
        tail[:, latent_width + head : lane_width],
        own_gains[2 * width :],
        wide(up_sum),
        wide(out_sum),
        own_gains[width : 2 * width],
        wide(gate_sum),
        wide(lift_sum),
        wide(down_sum),
    )


def solution(mesh):
    split = P(("dp", "seq"), None)
    matrix, vector = P("seq", None), P("seq")
    in_specs = (
        split,
        P("dp", None),
        vector,
        matrix,
        matrix,
        matrix,
        vector,
        matrix,
        matrix,
        vector,
        matrix,
        matrix,
        matrix,
        split,
    )
    out_specs = (
        split,
        split,
        vector,
        matrix,
        matrix,
        matrix,
        vector,
        matrix,
        matrix,
        vector,
        matrix,
        matrix,
        matrix,
    )
    return jax.shard_map(shards, mesh=mesh, in_specs=in_specs, out_specs=out_specs, check_vma=False)
```

time: 2650 us -> 803 us (0.30)
  waiting for transfers between devices: 2050 us -> 350 us
  blocking collectives: 313 us -> 0 us
  starting transfers between devices: 1.23 us -> 155 us
  matrix products: 203 us -> 70.1 us
  local copies, waits for them, and re-layouts: 20.6 us -> 100 us
  Pallas kernels: 0 us -> 34.3 us
  other arithmetic: 35 us -> 66.7 us
    all_gather x20 -> x1, waiting for transfers between devices: 1130 us -> 0.01 us  [shards(): weights = lax.all_gather(packed, 'seq', axis=0, tiled=True)]
    reduce_scatter x10 -> x0, waiting for transfers between devices: 901 us -> none  [the longest x1 160 us: shards(): lax.psum_scatter(key_grad_sum.astype(jnp.bfloat16), 'seq', scatter_dimens...]
    ppermute x0 -> x108, waiting for transfers between devices: none -> 328 us  [the longest x101 313 us: shift(): return lax.ppermute(value, 'seq', pairs)]
    unnamed x3 -> x0, blocking collectives: 217 us -> none
    ppermute x0 -> x108, starting transfers between devices: none -> 138 us  [the longest x101 128 us: shift(): return lax.ppermute(value, 'seq', pairs)]
    dot_general x30, matrix products: 196 us -> 70.1 us  [the longest x12 27.7 us: dot_nt(): lax.dot_general(left, right, (((1,), (1,)), ((), ())), preferred_element_...]
    all_gather x4 -> x0, blocking collectives: 72.6 us -> none  [the longest x1 21.1 us: shards(): lax.all_gather(first_gain, 'seq', axis=0, tiled=True)]
    unnamed x108 -> x276, local copies, waits for them, and re-layouts: 11.3 us -> 52.1 us
  transfers between devices with their start and end apart: 31 -> 114, of which waited for: 29 -> 55; matrix products, arithmetic and copies ran while one was open for 8% -> 24% of each run, Pallas kernels for 0% -> 2%
where the time goes in v1:
time: 803 us; the launch traced here: 795 us
  waiting for transfers between devices  350 us (44%)
  starting transfers between devices  155 us (19%)
  local copies, waits for them, and re-layouts  100 us (12%)
  matrix products  70.1 us (9%)
  other arithmetic  66.7 us (8%)
  Pallas kernels  34.3 us (4%)
  between operations  17.6 us (2%)
    ppermute x101, waiting for transfers between devices, shift(): return lax.ppermute(value, 'seq', pairs)  313 us
    ppermute x101, starting transfers between devices, shift(): return lax.ppermute(value, 'seq', pairs)  128 us
    unnamed x276, local copies, waits for them, and re-layouts  52.1 us
    dot_general x12, matrix products, dot_nt(): lax.dot_general(left, right, (((1,), (1,)), ((), ())), preferred_element_...  27.7 us
    dot_general x12, matrix products, dot(): return jnp.dot(left, right, preferred_element_type=F32)  23.8 us
    pallas_call x1, Pallas kernels, attend_back(): pl.pallas_call(attend_back_kernel, out_shape=(jax.ShapeDtypeStruct(querie...  18.9 us
    dot_general x6, matrix products, dot_tn(): lax.dot_general(left, right, (((0,), (0,)), ((), ())), preferred_element_...  18.6 us
  transfers between devices with their start and end apart: 114, of which 55 were waited for; matrix products, arithmetic and copies ran while one was open for 24% of the time, Pallas kernels for 2%

profile of v1, /device:TPU:0, one launch (start us, length us, event | category | flops | bytes accessed | tf_op | source)
XLA Modules:
  0.0 794.6 jit_solution(5301479826620248277)
XLA Ops:
  10.7 4.2 collective-permute-start.41
  18.5 4.7 all-to-all-start
  39.2 8.8 %all-to-all-done = bf16[16,64,256]{2,1,0:T(8,128)(2,1)} async-done(((bf16[16,64,256]{2,1,0:T(8,128)(2,1)}), bf16[16,64,256]{2,1,0:T(8,128)(2,1)}, u32[]{:S(2)}, u32[]{:S(2)}) %all-to-all-start) | async-done | bytes 524320 | tf_op jit(solution)/shard_map/all_to_all | solution.py:417
  47.9 4.0 all-to-all-start.1
  64.3 41.4 %collective-permute-done.44 = bf16[128,2048]{1,0:T(8,128)(2,1)S(1)} collective-permute-done((bf16[128,2048]{1,0:T(8,128)(2,1)S(1)}, bf16[128,2048]{1,0:T(8,128)(2,1)S(1)}, u32[]{:S(2)}, u32[]{:S(2)}) %collective-permute-start.44) | collective-permute-done | bytes 524320 | tf_op jit(solution)/shard_map/ppermute | solution.py:30
  109.6 10.7 %collective-permute-done.46 = bf16[128,2048]{1,0:T(8,128)(2,1)S(1)} collective-permute-done((bf16[128,2048]{1,0:T(8,128)(2,1)S(1)}, bf16[128,2048]{1,0:T(8,128)(2,1)S(1)}, u32[]{:S(2)}, u32[]{:S(2)}) %collective-permute-start.46) | collective-permute-done | bytes 524320 | tf_op jit(solution)/shard_map/ppermute | solution.py:30
  122.7 3.4 collective-permute-start.48
  138.4 4.2 fusion.6
  147.1 4.3 fusion.238
  154.2 3.2 collective-permute-start
  171.3 3.3 collective-permute-start.3
  178.4 4.5 collective-permute-done.3
  182.8 3.4 collective-permute-done.4
  192.9 3.4 collective-permute-done.8
  211.9 15.4 %attend.1 = (bf16[8,128,512]{2,1,0:T(8,128)(2,1)S(1)}, f32[8,1,256]{2,1,0:T(1,128)S(1)}) custom-call(s32[17]{0:T(128)S(1)} %stack.110.meta, bf16[8,128,512]{2,1,0:T(8,128)(2,1)S(1)} %convert_element_type.333.q_ref, bf16[8,128,256]{2,1,0:T(8,128)(2,1)S(1)} %get-tuple-element.180.ko_ref, bf16[8,128,256]{2,1,0:T(8,128)(2,1)S(1)} %get-tuple-element.178.ks_ref, ...), custom_call_target="tpu_custom_call" | custom-call | flops 2600000000 | bytes 5000000 | tf_op jit(solution)/shard_map/attend/pallas_call | solution.py:339
  230.4 3.2 collective-permute-start.17
  245.8 3.2 collective-permute-start.78
  249.0 3.8 collective-permute-done.18
  256.6 3.3 collective-permute-start.19
  264.3 6.5 collective-permute-done.79
  278.4 3.8 collective-permute-start.84
  282.6 3.3 collective-permute-done.84
  288.0 3.6 collective-permute-done.22
  298.5 3.2 multiply_convert_fusion.1
  337.3 4.0 collective-permute-done.31
  346.1 7.3 fusion.26
  353.4 3.2 fusion.20
  357.8 3.2 collective-permute-start.37
  361.1 3.2 collective-permute-start.55
  366.0 3.5 collective-permute-done.50
  375.0 9.6 %collective-permute-done.38 = bf16[128,2048]{1,0:T(8,128)(2,1)S(1)} collective-permute-done((bf16[128,2048]{1,0:T(8,128)(2,1)S(1)}, bf16[128,2048]{1,0:T(8,128)(2,1)S(1)}, u32[]{:S(2)}, u32[]{:S(2)}) %collective-permute-start.38) | collective-permute-done | bytes 524320 | tf_op jit(solution)/shard_map/ppermute | solution.py:30
  388.8 6.6 collective-permute-done.56
  405.7 6.2 collective-permute-done.36
  414.2 3.2 fusion.32
  418.1 3.4 collective-permute-done.54
  424.2 3.2 multiply_reduce_fusion
  447.2 7.1 collective-permute-done.62
  456.8 3.2 collective-permute-start.66
  461.6 3.4 collective-permute-done.65
  465.1 3.3 collective-permute-done.67
  468.5 3.3 convolution_convert_fusion.1
  471.8 18.9 %attend_back.1 = (f32[8,128,512]{2,1,0:T(8,128)}, f32[8,128,512]{2,1,0:T(8,128)}, bf16[8,128,512]{2,1,0:T(8,128)(2,1)S(1)}) custom-call(s32[17]{0:T(128)S(1)} %stack.110.meta, bf16[8,128,512]{2,1,0:T(8,128)(2,1)S(1)} %convert_element_type.333.q_ref, bf16[8,128,256]{2,1,0:T(8,128)(2,1)S(1)} %get-tuple-element.180.ko_ref, ...), custom_call_target="tpu_custom_call" | custom-call | flops 6499999744 | bytes 10000000 | tf_op jit(solution)/shard_map/attend_back/pallas_call | solution.py:359
  490.8 3.6 reshape.428
  505.6 4.2 all-to-all-start.2
  521.6 3.6 collective-permute-start.75
  526.5 6.7 collective-permute-done.75
  533.2 3.8 collective-permute-done.71
  537.7 3.3 collective-permute-start.76
  548.1 4.6 all-to-all-start.3
  561.1 5.4 fusion.46
  577.0 13.2 %all-to-all-done.3 = bf16[16,128,704]{1,2,0:T(8,128)(2,1)} async-done(((bf16[16,128,704]{1,2,0:T(8,128)(2,1)}), bf16[16,128,704]{1,2,0:T(8,128)(2,1)}, u32[]{:S(2)}, u32[]{:S(2)}) %all-to-all-start.3) | async-done | bytes 2883616 | tf_op jit(solution)/shard_map/all_to_all | solution.py:617
  590.2 3.6 fusion.208
  594.0 5.3 collective-permute-done.85
  599.4 5.9 collective-permute-done.87
  605.5 8.3 %collective-permute-start.88 = (bf16[128,1664]{1,0:T(8,128)(2,1)S(1)}, bf16[128,1664]{1,0:T(8,128)(2,1)S(1)}, u32[]{:S(2)}, u32[]{:S(2)}) collective-permute-start(bf16[128,1664]{1,0:T(8,128)(2,1)S(1)} %get-tuple-element.259), channel_id=1, source_target_pairs={{0,6},{1,7},{2,0},{3,1},{4,2},{5,3},{6,4},{7,5},{8,14},{9,15},{10,... | collective-permute-start | bytes 1277960 | tf_op jit(solution)/shard_map/ppermute | solution.py:30
  614.4 8.1 %collective-permute-done.88 = bf16[128,1664]{1,0:T(8,128)(2,1)S(1)} collective-permute-done((bf16[128,1664]{1,0:T(8,128)(2,1)S(1)}, bf16[128,1664]{1,0:T(8,128)(2,1)S(1)}, u32[]{:S(2)}, u32[]{:S(2)}) %collective-permute-start.88) | collective-permute-done | bytes 426016 | tf_op jit(solution)/shard_map/ppermute | solution.py:30
  622.5 3.4 collective-permute-done.89
  625.9 50.8 %collective-permute-done.90 = bf16[128,1664]{1,0:T(8,128)(2,1)S(1)} collective-permute-done((bf16[128,1664]{1,0:T(8,128)(2,1)S(1)}, bf16[128,1664]{1,0:T(8,128)(2,1)S(1)}, u32[]{:S(2)}, u32[]{:S(2)}) %collective-permute-start.90) | collective-permute-done | bytes 426016 | tf_op jit(solution)/shard_map/ppermute | solution.py:30
  680.9 60.2 %collective-permute-done.91 = bf16[32,1664]{1,0:T(8,128)(2,1)S(1)} collective-permute-done((bf16[32,1664]{1,0:T(8,128)(2,1)S(1)}, bf16[32,1664]{1,0:T(8,128)(2,1)S(1)}, u32[]{:S(2)}, u32[]{:S(2)}) %collective-permute-start.91) | collective-permute-done | bytes 106528 | tf_op jit(solution)/shard_map/ppermute | solution.py:30
  746.9 3.2 collective-permute-start.97
  750.1 3.3 collective-permute-done.96
  760.5 3.5 collective-permute-done.99
  769.1 5.5 collective-permute-done.101
  777.4 3.4 convert_element_type.416
  (707 shorter events, 315.5 us)
Async XLA Ops:
  7.2 137.1 %all-gather.2.cloned.1.call-start = ((), (), s32[]{:S(2)}) async-start(), calls=%async_computation.4 | async-start | bytes 7241728 | tf_op jit(solution)/shard_map/all_gather | solution.py:412
  10.7 41.3 %collective-permute-start.41 = (bf16[128,2048]{1,0:T(8,128)(2,1)}, bf16[128,2048]{1,0:T(8,128)(2,1)}, u32[]{:S(2)}, u32[]{:S(2)}) collective-permute-start(bf16[128,2048]{1,0:T(8,128)(2,1)} %param.27), channel_id=1, source_target_pairs={{0,6},{1,7},{2,0},{3,1},{4,2},{5,3},{6,4},{7,5},{8,14},{9,15},{10,... | collective-permute-start | bytes 1572872 | tf_op jit(solution)/shard_map/ppermute | solution.py:30
  14.9 39.5 %collective-permute-start.42 = (bf16[128,2048]{1,0:T(8,128)(2,1)}, bf16[128,2048]{1,0:T(8,128)(2,1)}, u32[]{:S(2)}, u32[]{:S(2)}) collective-permute-start(bf16[128,2048]{1,0:T(8,128)(2,1)} %param.27), channel_id=1, source_target_pairs={{0,2},{1,3},{2,4},{3,5},{4,6},{5,7},{6,0},{7,1},{8,10},{9,11},{10,... | collective-permute-start | bytes 1572872 | tf_op jit(solution)/shard_map/ppermute | solution.py:30
  14.9 38.5 %collective-permute-start.43 = (bf16[128,2048]{1,0:T(8,128)(2,1)}, bf16[128,2048]{1,0:T(8,128)(2,1)}, u32[]{:S(2)}, u32[]{:S(2)}) collective-permute-start(bf16[128,2048]{1,0:T(8,128)(2,1)} %param.27), channel_id=1, source_target_pairs={{0,8},{1,9},{2,10},{3,11},{4,12},{5,13},{6,14},{7,15},{8,0},{9,1},... | collective-permute-start | bytes 1572872 | tf_op jit(solution)/shard_map/ppermute | solution.py:30
  18.5 29.4 %all-to-all-start = ((bf16[16,64,256]{2,1,0:T(8,128)(2,1)}), bf16[16,64,256]{2,1,0:T(8,128)(2,1)}, u32[]{:S(2)}, u32[]{:S(2)}) async-start(bf16[16,64,256]{2,1,0:T(8,128)(2,1)} %copy.101), calls=%async_computation | async-start | bytes 1048576 | tf_op jit(solution)/shard_map/all_to_all | solution.py:417
  23.2 103.8 %collective-permute-start.11 = (bf16[256,2048]{1,0:T(8,128)(2,1)}, bf16[256,2048]{1,0:T(8,128)(2,1)}, u32[]{:S(2)}, u32[]{:S(2)}) collective-permute-start(bf16[256,2048]{1,0:T(8,128)(2,1)} %param.22), channel_id=1, source_target_pairs={{0,1},{1,0},{2,3},{3,2},{4,5},{5,4},{6,7},{7,6},{8,9},{9,8},{10,11... | collective-permute-start | bytes 3145736 | tf_op jit(solution)/shard_map/ppermute | solution.py:30
  23.6 110.7 %collective-permute-start.25 = (bf16[352,2048]{1,0:T(8,128)(2,1)}, bf16[352,2048]{1,0:T(8,128)(2,1)}, u32[]{:S(2)}, u32[]{:S(2)}) collective-permute-start(bf16[352,2048]{1,0:T(8,128)(2,1)} %param.26), channel_id=1, source_target_pairs={{0,1},{1,0},{2,3},{3,2},{4,5},{5,4},{6,7},{7,6},{8,9},{9,8},{10,11... | collective-permute-start | bytes 4325384 | tf_op jit(solution)/shard_map/ppermute | solution.py:30
  47.9 109.5 %all-to-all-start.1 = ((bf16[16,128,704]{1,2,0:T(8,128)(2,1)}), bf16[16,128,704]{1,2,0:T(8,128)(2,1)S(1)}, u32[]{:S(2)}, u32[]{:S(2)}) async-start(bf16[16,128,704]{1,2,0:T(8,128)(2,1)} %maximum_bitcast_fusion), calls=%async_computation.1 | async-start | bytes 5767168 | tf_op jit(solution)/shard_map/all_to_all | solution.py:417
  51.9 146.0 %collective-permute-start.9 = (bf16[1024,256]{1,0:T(8,128)(2,1)}, bf16[1024,256]{1,0:T(8,128)(2,1)}, u32[]{:S(2)}, u32[]{:S(2)}) collective-permute-start(bf16[1024,256]{1,0:T(8,128)(2,1)} %bitcast.35), channel_id=1, source_target_pairs={{0,1},{1,0},{2,3},{3,2},{4,5},{5,4},{6,7},{7,6},{8,9},{9,8},{10,11... | collective-permute-start | bytes 1572872 | tf_op jit(solution)/shard_map/ppermute | solution.py:30
  55.7 50.0 %collective-permute-start.44 = (bf16[128,2048]{1,0:T(8,128)(2,1)S(1)}, bf16[128,2048]{1,0:T(8,128)(2,1)S(1)}, u32[]{:S(2)}, u32[]{:S(2)}) collective-permute-start(bf16[128,2048]{1,0:T(8,128)(2,1)S(1)} %get-tuple-element.253), channel_id=1, source_target_pairs={{0,6},{1,7},{2,0},{3,1},{4,2},{5,3},{6,4},{7,5},{8,14},{9,15},{10,... | collective-permute-start | bytes 1572872 | tf_op jit(solution)/shard_map/ppermute | solution.py:30
  58.6 50.3 %collective-permute-start.45 = (bf16[128,2048]{1,0:T(8,128)(2,1)S(1)}, bf16[128,2048]{1,0:T(8,128)(2,1)S(1)}, u32[]{:S(2)}, u32[]{:S(2)}) collective-permute-start(bf16[128,2048]{1,0:T(8,128)(2,1)S(1)} %get-tuple-element.254), channel_id=1, source_target_pairs={{0,2},{1,3},{2,4},{3,5},{4,6},{5,7},{6,0},{7,1},{8,10},{9,11},{10,... | collective-permute-start | bytes 1572872 | tf_op jit(solution)/shard_map/ppermute | solution.py:30
  105.7 14.7 %collective-permute-start.46 = (bf16[128,2048]{1,0:T(8,128)(2,1)S(1)}, bf16[128,2048]{1,0:T(8,128)(2,1)S(1)}, u32[]{:S(2)}, u32[]{:S(2)}) collective-permute-start(bf16[128,2048]{1,0:T(8,128)(2,1)S(1)} %get-tuple-element.252), channel_id=1, source_target_pairs={{0,8},{1,9},{2,10},{3,11},{4,12},{5,13},{6,14},{7,15},{8,0},{9,1},... | collective-permute-start | bytes 1572872 | tf_op jit(solution)/shard_map/ppermute | solution.py:30
  159.4 102.2 %collective-permute-start.24 = (bf16[2048,704]{0,1:T(8,128)(2,1)}, bf16[2048,704]{0,1:T(8,128)(2,1)}, u32[]{:S(2)}, u32[]{:S(2)}) collective-permute-start(bf16[2048,704]{0,1:T(8,128)(2,1)} %copy_bitcast_fusion), channel_id=1, source_target_pairs={{0,1},{1,0},{2,3},{3,2},{4,5},{5,4},{6,7},{7,6},{8,9},{9,8},{10,11... | collective-permute-start | bytes 8650760 | tf_op jit(solution)/shard_map/ppermute | solution.py:30
  159.4 11.8 %collective-permute-start.2 = (bf16[128,1536]{1,0:T(8,128)(2,1)}, bf16[128,1536]{1,0:T(8,128)(2,1)S(1)}, u32[]{:S(2)}, u32[]{:S(2)}) collective-permute-start(bf16[128,1536]{1,0:T(8,128)(2,1)} %get-tuple-element.245), channel_id=1, source_target_pairs={{0,8},{1,9},{2,10},{3,11},{4,12},{5,13},{6,14},{7,15},{8,0},{9,1},... | collective-permute-start | bytes 1179656 | tf_op jit(solution)/shard_map/ppermute | solution.py:30
  197.4 13.1 %collective-permute-start.10 = (bf16[1024,512]{1,0:T(8,128)(2,1)}, bf16[1024,512]{1,0:T(8,128)(2,1)}, u32[]{:S(2)}, u32[]{:S(2)}) collective-permute-start(bf16[1024,512]{1,0:T(8,128)(2,1)} %slice.1193), channel_id=1, source_target_pairs={{0,1},{1,0},{2,3},{3,2},{4,5},{5,4},{6,7},{7,6},{8,9},{9,8},{10,11... | collective-permute-start | bytes 3145736 | tf_op jit(solution)/shard_map/ppermute | solution.py:30
  238.7 14.1 %collective-permute-start.18 = (bf16[128,2048]{1,0:T(8,128)(2,1)S(1)}, bf16[128,2048]{1,0:T(8,128)(2,1)S(1)}, u32[]{:S(2)}, u32[]{:S(2)}) collective-permute-start(bf16[128,2048]{1,0:T(8,128)(2,1)S(1)} %fusion.97), channel_id=1, source_target_pairs={{0,6},{1,7},{2,0},{3,1},{4,2},{5,3},{6,4},{7,5},{8,14},{9,15},{10,... | collective-permute-start | bytes 1572872 | tf_op jit(solution)/shard_map/ppermute | solution.py:30
  241.8 13.9 %collective-permute-start.14 = (bf16[128,2048]{1,0:T(8,128)(2,1)S(1)}, bf16[128,2048]{1,0:T(8,128)(2,1)S(1)}, u32[]{:S(2)}, u32[]{:S(2)}) collective-permute-start(bf16[128,2048]{1,0:T(8,128)(2,1)S(1)} %get-tuple-element.270), channel_id=1, source_target_pairs={{0,2},{1,3},{2,4},{3,5},{4,6},{5,7},{6,0},{7,1},{8,10},{9,11},{10,... | collective-permute-start | bytes 1572872 | tf_op jit(solution)/shard_map/ppermute | solution.py:30
  241.9 13.9 %collective-permute-start.15 = (bf16[128,2048]{1,0:T(8,128)(2,1)S(1)}, bf16[128,2048]{1,0:T(8,128)(2,1)S(1)}, u32[]{:S(2)}, u32[]{:S(2)}) collective-permute-start(bf16[128,2048]{1,0:T(8,128)(2,1)S(1)} %get-tuple-element.269), channel_id=1, source_target_pairs={{0,8},{1,9},{2,10},{3,11},{4,12},{5,13},{6,14},{7,15},{8,0},{9,1},... | collective-permute-start | bytes 1572872 | tf_op jit(solution)/shard_map/ppermute | solution.py:30
  245.8 18.0 %collective-permute-start.78 = (bf16[128,256]{1,0:T(8,128)(2,1)S(1)}, bf16[128,256]{1,0:T(8,128)(2,1)S(1)}, u32[]{:S(2)}, u32[]{:S(2)}) collective-permute-start(bf16[128,256]{1,0:T(8,128)(2,1)S(1)} %get-tuple-element.215), channel_id=1, source_target_pairs={{0,6},{1,7},{2,0},{3,1},{4,2},{5,3},{6,4},{7,5},{8,14},{9,15},{10,... | collective-permute-start | bytes 196616 | tf_op jit(solution)/shard_map/ppermute | solution.py:30
  256.5 14.4 %collective-permute-start.16 = (bf16[128,2048]{1,0:T(8,128)(2,1)S(1)}, bf16[128,2048]{1,0:T(8,128)(2,1)S(1)}, u32[]{:S(2)}, u32[]{:S(2)}) collective-permute-start(bf16[128,2048]{1,0:T(8,128)(2,1)S(1)} %pad_maximum_fusion.20), channel_id=1, source_target_pairs={{0,2},{1,3},{2,4},{3,5},{4,6},{5,7},{6,0},{7,1},{8,10},{9,11},{10,... | collective-permute-start | bytes 1572872 | tf_op jit(solution)/shard_map/ppermute | solution.py:30
  256.6 17.2 %collective-permute-start.19 = (bf16[128,2048]{1,0:T(8,128)(2,1)S(1)}, bf16[128,2048]{1,0:T(8,128)(2,1)S(1)}, u32[]{:S(2)}, u32[]{:S(2)}) collective-permute-start(bf16[128,2048]{1,0:T(8,128)(2,1)S(1)} %pad_maximum_fusion.21), channel_id=1, source_target_pairs={{0,6},{1,7},{2,0},{3,1},{4,2},{5,3},{6,4},{7,5},{8,14},{9,15},{10,... | collective-permute-start | bytes 1572872 | tf_op jit(solution)/shard_map/ppermute | solution.py:30
  259.9 13.9 %collective-permute-start.20 = (bf16[128,2048]{1,0:T(8,128)(2,1)S(1)}, bf16[128,2048]{1,0:T(8,128)(2,1)S(1)}, u32[]{:S(2)}, u32[]{:S(2)}) collective-permute-start(bf16[128,2048]{1,0:T(8,128)(2,1)S(1)} %pad_maximum_fusion.22), channel_id=1, source_target_pairs={{0,8},{1,9},{2,10},{3,11},{4,12},{5,13},{6,14},{7,15},{8,0},{9,1},... | collective-permute-start | bytes 1572872 | tf_op jit(solution)/shard_map/ppermute | solution.py:30
  263.8 14.5 %collective-permute-start.80 = (bf16[128,256]{1,0:T(8,128)(2,1)S(1)}, bf16[128,256]{1,0:T(8,128)(2,1)S(1)}, u32[]{:S(2)}, u32[]{:S(2)}) collective-permute-start(bf16[128,256]{1,0:T(8,128)(2,1)S(1)} %get-tuple-element.213), channel_id=1, source_target_pairs={{0,8},{1,9},{2,10},{3,11},{4,12},{5,13},{6,14},{7,15},{8,0},{9,1},... | collective-permute-start | bytes 196616 | tf_op jit(solution)/shard_map/ppermute | solution.py:30
  275.4 12.6 %collective-permute-start.21 = (bf16[128,2048]{1,0:T(8,128)(2,1)S(1)}, bf16[128,2048]{1,0:T(8,128)(2,1)S(1)}, u32[]{:S(2)}, u32[]{:S(2)}) collective-permute-start(bf16[128,2048]{1,0:T(8,128)(2,1)S(1)} %get-tuple-element.90), channel_id=1, source_target_pairs={{0,6},{1,7},{2,0},{3,1},{4,2},{5,3},{6,4},{7,5},{8,14},{9,15},{10,... | collective-permute-start | bytes 1572872 | tf_op jit(solution)/shard_map/ppermute | solution.py:30
  278.3 13.2 %collective-permute-start.22 = (bf16[128,2048]{1,0:T(8,128)(2,1)S(1)}, bf16[128,2048]{1,0:T(8,128)(2,1)S(1)}, u32[]{:S(2)}, u32[]{:S(2)}) collective-permute-start(bf16[128,2048]{1,0:T(8,128)(2,1)S(1)} %get-tuple-element.90), channel_id=1, source_target_pairs={{0,2},{1,3},{2,4},{3,5},{4,6},{5,7},{6,0},{7,1},{8,10},{9,11},{10,... | collective-permute-start | bytes 1572872 | tf_op jit(solution)/shard_map/ppermute | solution.py:30
  293.4 18.3 %collective-permute-start.26 = (bf16[128,2048]{1,0:T(8,128)(2,1)}, bf16[128,2048]{1,0:T(8,128)(2,1)S(1)}, u32[]{:S(2)}, u32[]{:S(2)}) collective-permute-start(bf16[128,2048]{1,0:T(8,128)(2,1)} %get-tuple-element.256), channel_id=1, source_target_pairs={{0,6},{1,7},{2,0},{3,1},{4,2},{5,3},{6,4},{7,5},{8,14},{9,15},{10,... | collective-permute-start | bytes 1572872 | tf_op jit(solution)/shard_map/ppermute | solution.py:30
  294.7 17.7 %collective-permute-start.27 = (bf16[128,2048]{1,0:T(8,128)(2,1)}, bf16[128,2048]{1,0:T(8,128)(2,1)}, u32[]{:S(2)}, u32[]{:S(2)}) collective-permute-start(bf16[128,2048]{1,0:T(8,128)(2,1)} %get-tuple-element.257), channel_id=1, source_target_pairs={{0,2},{1,3},{2,4},{3,5},{4,6},{5,7},{6,0},{7,1},{8,10},{9,11},{10,... | collective-permute-start | bytes 1572872 | tf_op jit(solution)/shard_map/ppermute | solution.py:30
  295.4 18.7 %collective-permute-start.28 = (bf16[128,2048]{1,0:T(8,128)(2,1)}, bf16[128,2048]{1,0:T(8,128)(2,1)S(1)}, u32[]{:S(2)}, u32[]{:S(2)}) collective-permute-start(bf16[128,2048]{1,0:T(8,128)(2,1)} %get-tuple-element.255), channel_id=1, source_target_pairs={{0,8},{1,9},{2,10},{3,11},{4,12},{5,13},{6,14},{7,15},{8,0},{9,1},... | collective-permute-start | bytes 1572872 | tf_op jit(solution)/shard_map/ppermute | solution.py:30
  344.7 19.8 %collective-permute-start.32 = (bf16[32,2048]{1,0:T(8,128)(2,1)S(1)}, bf16[32,2048]{1,0:T(8,128)(2,1)S(1)}, u32[]{:S(2)}, u32[]{:S(2)}) collective-permute-start(bf16[32,2048]{1,0:T(8,128)(2,1)S(1)} %slice.1243), channel_id=1, source_target_pairs={{0,8},{1,9},{2,10},{3,11},{4,12},{5,13},{6,14},{7,15},{8,0},{9,1},... | collective-permute-start | bytes 393224 | tf_op jit(solution)/shard_map/ppermute | solution.py:30
  357.3 12.3 %collective-permute-start.33 = (bf16[48,2048]{1,0:T(8,128)(2,1)S(1)}, bf16[48,2048]{1,0:T(8,128)(2,1)S(1)}, u32[]{:S(2)}, u32[]{:S(2)}) collective-permute-start(bf16[48,2048]{1,0:T(8,128)(2,1)S(1)} %get-tuple-element.227), channel_id=1, source_target_pairs={{0,2},{1,3},{2,4},{3,5},{4,6},{5,7},{6,0},{7,1},{8,10},{9,11},{10,... | collective-permute-start | bytes 589832 | tf_op jit(solution)/shard_map/ppermute | solution.py:30
  357.8 11.8 %collective-permute-start.37 = (bf16[48,2048]{1,0:T(8,128)(2,1)S(1)}, bf16[48,2048]{1,0:T(8,128)(2,1)S(1)}, u32[]{:S(2)}, u32[]{:S(2)}) collective-permute-start(bf16[48,2048]{1,0:T(8,128)(2,1)S(1)} %get-tuple-element.228), channel_id=1, source_target_pairs={{0,6},{1,7},{2,0},{3,1},{4,2},{5,3},{6,4},{7,5},{8,14},{9,15},{10,... | collective-permute-start | bytes 589832 | tf_op jit(solution)/shard_map/ppermute | solution.py:30
  361.1 12.4 %collective-permute-start.55 = (bf16[48,2048]{1,0:T(8,128)(2,1)S(1)}, bf16[48,2048]{1,0:T(8,128)(2,1)S(1)}, u32[]{:S(2)}, u32[]{:S(2)}) collective-permute-start(bf16[48,2048]{1,0:T(8,128)(2,1)S(1)} %get-tuple-element.224), channel_id=1, source_target_pairs={{0,6},{1,7},{2,0},{3,1},{4,2},{5,3},{6,4},{7,5},{8,14},{9,15},{10,... | collective-permute-start | bytes 589832 | tf_op jit(solution)/shard_map/ppermute | solution.py:30
  369.6 61.2 %collective-permute-start.105 = (bf16[2048,352]{0,1:T(8,128)(2,1)S(1)}, bf16[2048,352]{0,1:T(8,128)(2,1)}, u32[]{:S(2)}, u32[]{:S(2)}) collective-permute-start(bf16[2048,352]{0,1:T(8,128)(2,1)S(1)} %slice.1697), channel_id=1, source_target_pairs={{0,1},{1,0},{2,3},{3,2},{4,5},{5,4},{6,7},{7,6},{8,9},{9,8},{10,11... | collective-permute-start | bytes 4325384 | tf_op jit(solution)/shard_map/ppermute | solution.py:30
  369.8 14.8 %collective-permute-start.38 = (bf16[128,2048]{1,0:T(8,128)(2,1)S(1)}, bf16[128,2048]{1,0:T(8,128)(2,1)S(1)}, u32[]{:S(2)}, u32[]{:S(2)}) collective-permute-start(bf16[128,2048]{1,0:T(8,128)(2,1)S(1)} %fusion.103), channel_id=1, source_target_pairs={{0,6},{1,7},{2,0},{3,1},{4,2},{5,3},{6,4},{7,5},{8,14},{9,15},{10,... | collective-permute-start | bytes 1572872 | tf_op jit(solution)/shard_map/ppermute | solution.py:30
  370.0 15.6 %collective-permute-start.34 = (bf16[128,2048]{1,0:T(8,128)(2,1)S(1)}, bf16[128,2048]{1,0:T(8,128)(2,1)S(1)}, u32[]{:S(2)}, u32[]{:S(2)}) collective-permute-start(bf16[128,2048]{1,0:T(8,128)(2,1)S(1)} %get-tuple-element.268), channel_id=1, source_target_pairs={{0,2},{1,3},{2,4},{3,5},{4,6},{5,7},{6,0},{7,1},{8,10},{9,11},{10,... | collective-permute-start | bytes 1572872 | tf_op jit(solution)/shard_map/ppermute | solution.py:30
  372.1 15.0 %collective-permute-start.35 = (bf16[128,2048]{1,0:T(8,128)(2,1)S(1)}, bf16[128,2048]{1,0:T(8,128)(2,1)S(1)}, u32[]{:S(2)}, u32[]{:S(2)}) collective-permute-start(bf16[128,2048]{1,0:T(8,128)(2,1)S(1)} %get-tuple-element.267), channel_id=1, source_target_pairs={{0,8},{1,9},{2,10},{3,11},{4,12},{5,13},{6,14},{7,15},{8,0},{9,1},... | collective-permute-start | bytes 1572872 | tf_op jit(solution)/shard_map/ppermute | solution.py:30
  373.6 21.9 %collective-permute-start.56 = (bf16[128,2048]{1,0:T(8,128)(2,1)S(1)}, bf16[128,2048]{1,0:T(8,128)(2,1)S(1)}, u32[]{:S(2)}, u32[]{:S(2)}) collective-permute-start(bf16[128,2048]{1,0:T(8,128)(2,1)S(1)} %fusion.100), channel_id=1, source_target_pairs={{0,6},{1,7},{2,0},{3,1},{4,2},{5,3},{6,4},{7,5},{8,14},{9,15},{10,... | collective-permute-start | bytes 1572872 | tf_op jit(solution)/shard_map/ppermute | solution.py:30
  384.6 16.1 %collective-permute-start.52 = (bf16[128,2048]{1,0:T(8,128)(2,1)S(1)}, bf16[128,2048]{1,0:T(8,128)(2,1)S(1)}, u32[]{:S(2)}, u32[]{:S(2)}) collective-permute-start(bf16[128,2048]{1,0:T(8,128)(2,1)S(1)} %get-tuple-element.266), channel_id=1, source_target_pairs={{0,2},{1,3},{2,4},{3,5},{4,6},{5,7},{6,0},{7,1},{8,10},{9,11},{10,... | collective-permute-start | bytes 1572872 | tf_op jit(solution)/shard_map/ppermute | solution.py:30
  385.6 16.5 %collective-permute-start.53 = (bf16[128,2048]{1,0:T(8,128)(2,1)S(1)}, bf16[128,2048]{1,0:T(8,128)(2,1)S(1)}, u32[]{:S(2)}, u32[]{:S(2)}) collective-permute-start(bf16[128,2048]{1,0:T(8,128)(2,1)S(1)} %get-tuple-element.265), channel_id=1, source_target_pairs={{0,8},{1,9},{2,10},{3,11},{4,12},{5,13},{6,14},{7,15},{8,0},{9,1},... | collective-permute-start | bytes 1572872 | tf_op jit(solution)/shard_map/ppermute | solution.py:30
  388.2 23.7 %collective-permute-start.36 = (bf16[128,2048]{1,0:T(8,128)(2,1)S(1)}, bf16[128,2048]{1,0:T(8,128)(2,1)S(1)}, u32[]{:S(2)}, u32[]{:S(2)}) collective-permute-start(bf16[128,2048]{1,0:T(8,128)(2,1)S(1)} %pad_maximum_fusion.23), channel_id=1, source_target_pairs={{0,2},{1,3},{2,4},{3,5},{4,6},{5,7},{6,0},{7,1},{8,10},{9,11},{10,... | collective-permute-start | bytes 1572872 | tf_op jit(solution)/shard_map/ppermute | solution.py:30
  395.4 16.5 %collective-permute-start.39 = (bf16[128,2048]{1,0:T(8,128)(2,1)S(1)}, bf16[128,2048]{1,0:T(8,128)(2,1)S(1)}, u32[]{:S(2)}, u32[]{:S(2)}) collective-permute-start(bf16[128,2048]{1,0:T(8,128)(2,1)S(1)} %pad_maximum_fusion.24), channel_id=1, source_target_pairs={{0,6},{1,7},{2,0},{3,1},{4,2},{5,3},{6,4},{7,5},{8,14},{9,15},{10,... | collective-permute-start | bytes 1572872 | tf_op jit(solution)/shard_map/ppermute | solution.py:30
  400.7 17.3 %collective-permute-start.40 = (bf16[128,2048]{1,0:T(8,128)(2,1)}, bf16[128,2048]{1,0:T(8,128)(2,1)S(1)}, u32[]{:S(2)}, u32[]{:S(2)}) collective-permute-start(bf16[128,2048]{1,0:T(8,128)(2,1)} %pad_maximum_fusion.25), channel_id=1, source_target_pairs={{0,8},{1,9},{2,10},{3,11},{4,12},{5,13},{6,14},{7,15},{8,0},{9,1},... | collective-permute-start | bytes 1572872 | tf_op jit(solution)/shard_map/ppermute | solution.py:30
  404.0 17.4 %collective-permute-start.54 = (bf16[128,2048]{1,0:T(8,128)(2,1)}, bf16[128,2048]{1,0:T(8,128)(2,1)S(1)}, u32[]{:S(2)}, u32[]{:S(2)}) collective-permute-start(bf16[128,2048]{1,0:T(8,128)(2,1)} %pad_maximum_fusion.26), channel_id=1, source_target_pairs={{0,2},{1,3},{2,4},{3,5},{4,6},{5,7},{6,0},{7,1},{8,10},{9,11},{10,... | collective-permute-start | bytes 1572872 | tf_op jit(solution)/shard_map/ppermute | solution.py:30
  418.0 15.9 %collective-permute-start.107 = (bf16[352,2048]{1,0:T(8,128)(2,1)S(1)}, bf16[352,2048]{1,0:T(8,128)(2,1)}, u32[]{:S(2)}, u32[]{:S(2)}) collective-permute-start(bf16[352,2048]{1,0:T(8,128)(2,1)S(1)} %slice.1695), channel_id=1, source_target_pairs={{0,1},{1,0},{2,3},{3,2},{4,5},{5,4},{6,7},{7,6},{8,9},{9,8},{10,11... | collective-permute-start | bytes 4325384 | tf_op jit(solution)/shard_map/ppermute | solution.py:30
  421.4 15.3 %collective-permute-start.106 = (bf16[2048,352]{0,1:T(8,128)(2,1)S(1)}, bf16[2048,352]{0,1:T(8,128)(2,1)}, u32[]{:S(2)}, u32[]{:S(2)}) collective-permute-start(bf16[2048,352]{0,1:T(8,128)(2,1)S(1)} %slice.1696), channel_id=1, source_target_pairs={{0,1},{1,0},{2,3},{3,2},{4,5},{5,4},{6,7},{7,6},{8,9},{9,8},{10,11... | collective-permute-start | bytes 4325384 | tf_op jit(solution)/shard_map/ppermute | solution.py:30
  428.8 11.7 %collective-permute-start.59 = (bf16[128,2048]{1,0:T(8,128)(2,1)S(1)}, bf16[128,2048]{1,0:T(8,128)(2,1)S(1)}, u32[]{:S(2)}, u32[]{:S(2)}) collective-permute-start(bf16[128,2048]{1,0:T(8,128)(2,1)S(1)} %get-tuple-element.102), channel_id=1, source_target_pairs={{0,6},{1,7},{2,0},{3,1},{4,2},{5,3},{6,4},{7,5},{8,14},{9,15},{10,... | collective-permute-start | bytes 1572872 | tf_op jit(solution)/shard_map/ppermute | solution.py:30
  430.5 12.8 %collective-permute-start.60 = (bf16[128,2048]{1,0:T(8,128)(2,1)S(1)}, bf16[128,2048]{1,0:T(8,128)(2,1)S(1)}, u32[]{:S(2)}, u32[]{:S(2)}) collective-permute-start(bf16[128,2048]{1,0:T(8,128)(2,1)S(1)} %get-tuple-element.102), channel_id=1, source_target_pairs={{0,2},{1,3},{2,4},{3,5},{4,6},{5,7},{6,0},{7,1},{8,10},{9,11},{10,... | collective-permute-start | bytes 1572872 | tf_op jit(solution)/shard_map/ppermute | solution.py:30
  430.8 12.5 %collective-permute-start.61 = (bf16[128,2048]{1,0:T(8,128)(2,1)S(1)}, bf16[128,2048]{1,0:T(8,128)(2,1)S(1)}, u32[]{:S(2)}, u32[]{:S(2)}) collective-permute-start(bf16[128,2048]{1,0:T(8,128)(2,1)S(1)} %get-tuple-element.102), channel_id=1, source_target_pairs={{0,8},{1,9},{2,10},{3,11},{4,12},{5,13},{6,14},{7,15},{8,0},{9,1},... | collective-permute-start | bytes 1572872 | tf_op jit(solution)/shard_map/ppermute | solution.py:30
  498.1 11.7 %collective-permute-start.68 = (bf16[8,128,512]{2,1,0:T(8,128)(2,1)S(1)}, bf16[8,128,512]{2,1,0:T(8,128)(2,1)}, u32[]{:S(2)}, u32[]{:S(2)}) collective-permute-start(bf16[8,128,512]{2,1,0:T(8,128)(2,1)S(1)} %get-tuple-element.22), channel_id=1, source_target_pairs={{0,1},{1,0},{2,3},{3,2},{4,5},{5,4},{6,7},{7,6},{8,9},{9,8},{10,11... | collective-permute-start | bytes 3145736 | tf_op jit(solution)/shard_map/ppermute | solution.py:30
  505.6 42.6 %all-to-all-start.2 = ((bf16[16,64,256]{2,1,0:T(8,128)(2,1)}), bf16[16,64,256]{2,1,0:T(8,128)(2,1)}, u32[]{:S(2)}, u32[]{:S(2)}) async-start(bf16[16,64,256]{2,1,0:T(8,128)(2,1)} %bitcast.169), calls=%async_computation.2 | async-start | bytes 1048576 | tf_op jit(solution)/shard_map/all_to_all | solution.py:617
  537.6 17.2 %collective-permute-start.73 = (bf16[128,1536]{1,0:T(8,128)(2,1)S(1)}, bf16[128,1536]{1,0:T(8,128)(2,1)}, u32[]{:S(2)}, u32[]{:S(2)}) collective-permute-start(bf16[128,1536]{1,0:T(8,128)(2,1)S(1)} %pad_maximum_fusion.39), channel_id=1, source_target_pairs={{0,2},{1,3},{2,4},{3,5},{4,6},{5,7},{6,0},{7,1},{8,10},{9,11},{10,... | collective-permute-start | bytes 1179656 | tf_op jit(solution)/shard_map/ppermute | solution.py:30
  537.7 17.1 %collective-permute-start.76 = (bf16[128,1536]{1,0:T(8,128)(2,1)S(1)}, bf16[128,1536]{1,0:T(8,128)(2,1)}, u32[]{:S(2)}, u32[]{:S(2)}) collective-permute-start(bf16[128,1536]{1,0:T(8,128)(2,1)S(1)} %pad_maximum_fusion.40), channel_id=1, source_target_pairs={{0,6},{1,7},{2,0},{3,1},{4,2},{5,3},{6,4},{7,5},{8,14},{9,15},{10,... | collective-permute-start | bytes 1179656 | tf_op jit(solution)/shard_map/ppermute | solution.py:30
  541.7 13.1 %collective-permute-start.77 = (bf16[128,1536]{1,0:T(8,128)(2,1)}, bf16[128,1536]{1,0:T(8,128)(2,1)}, u32[]{:S(2)}, u32[]{:S(2)}) collective-permute-start(bf16[128,1536]{1,0:T(8,128)(2,1)} %pad_maximum_fusion.41), channel_id=1, source_target_pairs={{0,8},{1,9},{2,10},{3,11},{4,12},{5,13},{6,14},{7,15},{8,0},{9,1},... | collective-permute-start | bytes 1179656 | tf_op jit(solution)/shard_map/ppermute | solution.py:30
  548.1 25.7 %collective-permute-start.104 = (bf16[256,2048]{1,0:T(8,128)(2,1)}, bf16[256,2048]{1,0:T(8,128)(2,1)}, u32[]{:S(2)}, u32[]{:S(2)}) collective-permute-start(bf16[256,2048]{1,0:T(8,128)(2,1)} %slice.1698), channel_id=1, source_target_pairs={{0,1},{1,0},{2,3},{3,2},{4,5},{5,4},{6,7},{7,6},{8,9},{9,8},{10,11... | collective-permute-start | bytes 3145736 | tf_op jit(solution)/shard_map/ppermute | solution.py:30
  548.1 42.0 %all-to-all-start.3 = ((bf16[16,128,704]{1,2,0:T(8,128)(2,1)}), bf16[16,128,704]{1,2,0:T(8,128)(2,1)}, u32[]{:S(2)}, u32[]{:S(2)}) async-start(bf16[16,128,704]{1,2,0:T(8,128)(2,1)} %pad_maximum_fusion.2), calls=%async_computation.3 | async-start | bytes 5767168 | tf_op jit(solution)/shard_map/all_to_all | solution.py:617
  552.8 224.6 %all-reduce.8.cloned.1.call-start = ((), (), s32[]{:S(2)}) async-start(), calls=%async_computation.5 | async-start | bytes 11796480 | tf_op jit(solution)/shard_map/psum | solution.py:626
  570.9 28.5 %collective-permute-start.85 = (bf16[128,1664]{1,0:T(8,128)(2,1)}, bf16[128,1664]{1,0:T(8,128)(2,1)S(1)}, u32[]{:S(2)}, u32[]{:S(2)}) collective-permute-start(bf16[128,1664]{1,0:T(8,128)(2,1)} %get-tuple-element.278), channel_id=1, source_target_pairs={{0,6},{1,7},{2,0},{3,1},{4,2},{5,3},{6,4},{7,5},{8,14},{9,15},{10,... | collective-permute-start | bytes 1277960 | tf_op jit(solution)/shard_map/ppermute | solution.py:30
  573.8 25.5 %collective-permute-start.86 = (bf16[128,1664]{1,0:T(8,128)(2,1)}, bf16[128,1664]{1,0:T(8,128)(2,1)S(1)}, u32[]{:S(2)}, u32[]{:S(2)}) collective-permute-start(bf16[128,1664]{1,0:T(8,128)(2,1)} %get-tuple-element.278), channel_id=1, source_target_pairs={{0,2},{1,3},{2,4},{3,5},{4,6},{5,7},{6,0},{7,1},{8,10},{9,11},{10,... | collective-permute-start | bytes 1277960 | tf_op jit(solution)/shard_map/ppermute | solution.py:30
  605.5 17.0 %collective-permute-start.88 = (bf16[128,1664]{1,0:T(8,128)(2,1)S(1)}, bf16[128,1664]{1,0:T(8,128)(2,1)S(1)}, u32[]{:S(2)}, u32[]{:S(2)}) collective-permute-start(bf16[128,1664]{1,0:T(8,128)(2,1)S(1)} %get-tuple-element.259), channel_id=1, source_target_pairs={{0,6},{1,7},{2,0},{3,1},{4,2},{5,3},{6,4},{7,5},{8,14},{9,15},{10,... | collective-permute-start | bytes 1277960 | tf_op jit(solution)/shard_map/ppermute | solution.py:30
  613.8 12.1 %collective-permute-start.89 = (bf16[128,1664]{1,0:T(8,128)(2,1)S(1)}, bf16[128,1664]{1,0:T(8,128)(2,1)S(1)}, u32[]{:S(2)}, u32[]{:S(2)}) collective-permute-start(bf16[128,1664]{1,0:T(8,128)(2,1)S(1)} %get-tuple-element.260), channel_id=1, source_target_pairs={{0,2},{1,3},{2,4},{3,5},{4,6},{5,7},{6,0},{7,1},{8,10},{9,11},{10,... | collective-permute-start | bytes 1277960 | tf_op jit(solution)/shard_map/ppermute | solution.py:30
  613.8 63.0 %collective-permute-start.90 = (bf16[128,1664]{1,0:T(8,128)(2,1)S(1)}, bf16[128,1664]{1,0:T(8,128)(2,1)S(1)}, u32[]{:S(2)}, u32[]{:S(2)}) collective-permute-start(bf16[128,1664]{1,0:T(8,128)(2,1)S(1)} %get-tuple-element.258), channel_id=1, source_target_pairs={{0,8},{1,9},{2,10},{3,11},{4,12},{5,13},{6,14},{7,15},{8,0},{9,1},... | collective-permute-start | bytes 1277960 | tf_op jit(solution)/shard_map/ppermute | solution.py:30
  676.8 64.2 %collective-permute-start.92 = (bf16[48,1664]{1,0:T(8,128)(2,1)S(1)}, bf16[48,1664]{1,0:T(8,128)(2,1)S(1)}, u32[]{:S(2)}, u32[]{:S(2)}) collective-permute-start(bf16[48,1664]{1,0:T(8,128)(2,1)S(1)} %pad_maximum_fusion.47), channel_id=1, source_target_pairs={{0,6},{1,7},{2,0},{3,1},{4,2},{5,3},{6,4},{7,5},{8,14},{9,15},{10,... | collective-permute-start | bytes 479240 | tf_op jit(solution)/shard_map/ppermute | solution.py:30
  679.9 61.2 %collective-permute-start.91 = (bf16[32,1664]{1,0:T(8,128)(2,1)S(1)}, bf16[32,1664]{1,0:T(8,128)(2,1)S(1)}, u32[]{:S(2)}, u32[]{:S(2)}) collective-permute-start(bf16[32,1664]{1,0:T(8,128)(2,1)S(1)} %slice.1370), channel_id=1, source_target_pairs={{0,8},{1,9},{2,10},{3,11},{4,12},{5,13},{6,14},{7,15},{8,0},{9,1},... | collective-permute-start | bytes 319496 | tf_op jit(solution)/shard_map/ppermute | solution.py:30
  680.5 60.6 %collective-permute-start.93 = (bf16[48,1664]{1,0:T(8,128)(2,1)S(1)}, bf16[48,1664]{1,0:T(8,128)(2,1)S(1)}, u32[]{:S(2)}, u32[]{:S(2)}) collective-permute-start(bf16[48,1664]{1,0:T(8,128)(2,1)S(1)} %slice.1371), channel_id=1, source_target_pairs={{0,2},{1,3},{2,4},{3,5},{4,6},{5,7},{6,0},{7,1},{8,10},{9,11},{10,... | collective-permute-start | bytes 479240 | tf_op jit(solution)/shard_map/ppermute | solution.py:30
  (151 other events, 1346.1 us)
Sparse Core Ops, SparseCore 0:
  10.8 83.4 all-gather.1
  593.9 147.6 all-reduce.7

commit v2 on v1

v2 whole, which is shorter than its diff:
```python
import jax
import jax.numpy as jnp
from jax import lax
from jax.experimental import pallas as pl
from jax.experimental.pallas import tpu as pltpu
from jax.sharding import Mesh, PartitionSpec as P

NORM_EPSILON = 1e-05
F32 = jnp.float32
BF16 = jnp.bfloat16

AXES = ("v", "x", "y", "z", "c")
SIZES = (2, 4, 2, 4, 2)
DP, SEQ, ACROSS = ("v", "x"), ("y", "z", "c"), ("v", "x", "y")
SLOT = 384
KEY_CHUNK = 512


def turn(value, axis, step):
    size = SIZES[AXES.index(axis)]
    return lax.ppermute(value, axis, [(i, (i + step) % size) for i in range(size)])


def sibling(value):
    return turn(value, "c", 1)


def after(value, other):
    first = other[(0,) * other.ndim] if other.ndim else other
    return value + (first * 0).astype(value.dtype)


def rows(value, start, stop):
    return lax.slice_in_dim(value, start, stop, axis=0)


def exchange(parts, axes):
    return lax.all_to_all(parts, axes, 0, 0)


def spread(value, axes):
    count = 1
    for axis in axes:
        count *= SIZES[AXES.index(axis)]
    return exchange(jnp.broadcast_to(value[None], (count,) + value.shape), axes)


def total_of(parts):
    return jnp.sum(parts.astype(F32), axis=0)


def ring_gather(block, axis="z"):
    half = block.shape[0] // 2
    after_it, before_it = turn(block, axis, -1), turn(block, axis, 1)
    far_low = turn(rows(after_it, 0, half), axis, -1)
    far_high = turn(rows(before_it, half, 2 * half), axis, 1)
    return (block, far_low, far_high, after_it, before_it)


def ring_merge_kernel(part_ref, low_ref, high_ref, next_ref, back_ref):
    half = low_ref.shape[0]
    next_ref[half:, :] = part_ref[0, half:, :]
    next_ref[:half, :] = (part_ref[0, :half, :].astype(F32) + low_ref[...].astype(F32)).astype(BF16)
    back_ref[:half, :] = part_ref[1, :half, :]
    back_ref[half:, :] = (part_ref[1, half:, :].astype(F32) + high_ref[...].astype(F32)).astype(
        BF16
    )


def ring_scatter(parts, other=None):
    _, width, size = parts.shape
    half = width // 2
    got_low = turn(parts[1, :half], "z", 1)
    got_high = turn(parts[1, half:], "z", -1)
    if other is not None:
        got_low = after(got_low, other)
    half_spec = pl.BlockSpec((half, size), lambda i: (0, 0))
    full_spec = pl.BlockSpec((width, size), lambda i: (0, 0))
    to_next, to_back = pl.pallas_call(
        ring_merge_kernel,
        grid=(1,),
        out_shape=(jax.ShapeDtypeStruct((width, size), BF16),) * 2,
        in_specs=[pl.BlockSpec((2, width, size), lambda i: (1, 0, 0)), half_spec, half_spec],
        out_specs=(full_spec, full_spec),
        name="ring_merge",
    )(parts, got_low, got_high)
    return (
        parts[0].astype(F32)
        + turn(to_next, "z", 1).astype(F32)
        + turn(to_back, "z", -1).astype(F32)
    )


def inverse_rms(values):
    return lax.rsqrt(jnp.mean(values * values, axis=-1, keepdims=True) + NORM_EPSILON)


def rms_back(values, inv_root, gain_row, grad_normed):
    scaled = grad_normed * gain_row
    return inv_root * scaled - values * inv_root**3 * jnp.mean(
        scaled * values, axis=-1, keepdims=True
    )


def layout(lengths, token_index):
    doc_ends = jnp.cumsum(lengths)
    starts = doc_ends - lengths
    doc_id = jnp.sum((token_index[:, None] >= doc_ends[None, :]).astype(jnp.int32), axis=1)
    numbers = jnp.arange(lengths.shape[0], dtype=jnp.int32)
    doc_start = jnp.sum(jnp.where(doc_id[:, None] == numbers[None, :], starts[None, :], 0), axis=1)
    return doc_start


def rope_tables(position, head_width):
    half_width = head_width // 2
    frequency = 10000.0 ** (-(2.0 * jnp.arange(half_width, dtype=F32)) / head_width)
    angles = position.astype(F32)[:, None] * frequency[None, :]
    return (jnp.cos(angles), jnp.sin(angles))


def rotate(values, cosine, sine):
    half_width = cosine.shape[-1]
    low, high = values[..., :half_width], values[..., half_width:]
    return jnp.concatenate([low * cosine - high * sine, high * cosine + low * sine], axis=-1)


def rotate_back(grads, cosine, sine):
    return rotate(grads, cosine, -sine)


def dot(left, right):
    return jnp.dot(left, right, preferred_element_type=F32)


def dot_nt(left, right):
    return lax.dot_general(left, right, (((1,), (1,)), ((), ())), preferred_element_type=F32)


def dot_tn(left, right):
    return lax.dot_general(left, right, (((0,), (0,)), ((), ())), preferred_element_type=F32)


def masked(scores, first_key, place, begin):
    key = first_key + lax.broadcasted_iota(jnp.int32, scores.shape, 0)
    return jnp.where((key >= begin) & (key <= place), scores, -1e30)


def chunk_bounds(meta, block, width):
    number = meta[6 + block]
    count = ((number + 1) * width + KEY_CHUNK - 1) // KEY_CHUNK
    clear_from = jnp.minimum((meta[2 + block] + KEY_CHUNK - 1) // KEY_CHUNK, count)
    clear_to = jnp.maximum((number * width + 1) // KEY_CHUNK, clear_from)
    return clear_from, clear_to, count


def stack_lane(refs):
    return jnp.concatenate([ref[...] for ref in refs], axis=0)


def stack_heads(ref, block, first, head):
    return jnp.concatenate(
        [ref[block, :, first : first + head], ref[block, :, first + head : first + 2 * head]],
        axis=0,
    )


def query_kernel(lane_a, lane_b, lane_c, lane_d, lane_e, up_ref, cos_ref, sin_ref, q_ref):
    blocks, width, size = q_ref.shape
    half = cos_ref.shape[1]
    head = 2 * half
    latent = stack_lane((lane_a, lane_b, lane_c, lane_d, lane_e))
    cosine, sine = cos_ref[...], sin_ref[...]
    for start in range(0, size, head):
        query = dot(latent, up_ref[:, start : start + head])
        low, high = query[:, :half], query[:, half:]
        turned = ((low * cosine - high * sine), (high * cosine + low * sine))
        for part, value in enumerate(turned):
            q_ref[:, :, start + part * half : start + (part + 1) * half] = (
                (value * head**-0.5).astype(BF16).reshape(blocks, width, half)
            )


def attend_kernel(meta, q_ref, kv_ref, place_ref, begin_ref, out_ref, log_ref):
    blocks, width, size = q_ref.shape
    head = kv_ref.shape[1] // 2
    pairs = range(size // head // 2)

    @pl.loop(0, blocks)
    def per_block(block):
        clear_from, clear_to, count = chunk_bounds(meta, block, width)
        place, begin = place_ref[block], begin_ref[block]
        queries = [stack_heads(q_ref, block, pair * 2 * head, head) for pair in pairs]

        def chunk(step, carries, clear):
            start = pl.multiple_of(step * KEY_CHUNK, KEY_CHUNK)
            key_chunk = kv_ref[pl.ds(start, KEY_CHUNK), :head]
            value_chunk = kv_ref[pl.ds(start, KEY_CHUNK), head:]
            result = []
            for query, (top, total, mixed) in zip(queries, carries):
                scores = dot_nt(key_chunk, query)
                if not clear:
                    scores = masked(scores, start, place, begin)
                new_top = jnp.maximum(top, jnp.max(scores, axis=0, keepdims=True))
                factor = jnp.exp(top - new_top)
                weights = jnp.exp(scores - new_top)
                total = total * factor + jnp.sum(weights, axis=0, keepdims=True)
                mixed = mixed * factor + dot_tn(value_chunk, weights.astype(BF16))
                result.append((new_top, total, mixed))
            return tuple(result)

        carry = tuple(
            (
                jnp.full((1, 2 * width), -1e30, F32),
                jnp.zeros((1, 2 * width), F32),
                jnp.zeros((head, 2 * width), F32),
            )
            for _ in pairs
        )
        carry = lax.fori_loop(0, clear_from, lambda s, w: chunk(s, w, False), carry)
        carry = lax.fori_loop(clear_from, clear_to, lambda s, w: chunk(s, w, True), carry)
        carry = lax.fori_loop(clear_to, count, lambda s, w: chunk(s, w, False), carry)
        for pair, (top, total, mixed) in zip(pairs, carry):
            first = pair * 2 * head
            result = (mixed / total).T.astype(BF16)
            out_ref[block, :, first : first + head] = result[:width]
            out_ref[block, :, first + head : first + 2 * head] = result[width:]
            log_ref[block, pair] = top + jnp.log(total)


def attend_back_kernel(
    meta,
    branch_a,
    branch_b,
    branch_c,
    branch_d,
    branch_e,
    kv_ref,
    up_ref,
    proj_a,
    proj_b,
    proj_c,
    proj_d,
    cos_ref,
    sin_ref,
    place_ref,
    begin_ref,
    q_ref,
    out_ref,
    log_ref,
    lane_a,
    lane_b,
    lane_c,
    lane_d,
    lane_e,
    gq_ref,
    latent_ref,
    kv_own,
    kv_sib,
    out_own,
    out_sib,
    up_own,
    up_sib,
    grads,
    key_grad,
    value_grad,
):
    blocks, width, _ = q_ref.shape
    head = kv_ref.shape[1] // 2
    half = head // 2
    heads = q_ref.shape[2] // head
    branch = stack_lane((branch_a, branch_b, branch_c, branch_d, branch_e))
    y = meta[0]
    for at, (ref, yy) in enumerate(
        ((proj_a, y), (proj_b, 1 - y), (proj_c, y), (proj_d, 1 - y))
    ):
        first = pl.multiple_of((at // 2 * 2 + yy) * head, head)
        value = dot_nt(branch, ref[...])
        grads[:, :, pl.ds(first, head)] = value.astype(BF16).reshape(blocks, width, head)
    key_grad[...] = jnp.zeros_like(key_grad)
    value_grad[...] = jnp.zeros_like(value_grad)

    pairs = range(heads // 2)

    @pl.loop(0, blocks)
    def per_block(block):
        clear_from, clear_to, count = chunk_bounds(meta, block, width)
        place, begin = place_ref[block], begin_ref[block]
        token = pl.ds(pl.multiple_of(block * width, width), width)
        cosine, sine = cos_ref[token, :], sin_ref[token, :]
        fixed = []
        for pair in pairs:
            query, grad, out = (
                stack_heads(ref, block, pair * 2 * head, head) for ref in (q_ref, grads, out_ref)
            )
            row_dot = jnp.sum((grad.astype(F32) * out.astype(F32)).T, axis=0, keepdims=True)
            fixed.append((query, grad, row_dot, log_ref[block, pair]))

        def chunk(step, accs, clear):
            start = pl.multiple_of(step * KEY_CHUNK, KEY_CHUNK)
            span = pl.ds(start, KEY_CHUNK)
            key_chunk, value_chunk = kv_ref[span, :head], kv_ref[span, head:]
            key_sum, value_sum = key_grad[span, :], value_grad[span, :]
            result = []
            for (query, grad, row_dot, log_total), acc in zip(fixed, accs):
                scores = dot_nt(key_chunk, query)
                if not clear:
                    scores = masked(scores, start, place, begin)
                probs = jnp.exp(scores - log_total)
                grad_probs = dot_nt(value_chunk, grad)
                grad_scores = (probs * (grad_probs - row_dot)).astype(BF16)
                value_sum += dot(probs.astype(BF16), grad)
                key_sum += dot(grad_scores, query)
                result.append(acc + dot_tn(grad_scores, key_chunk))
            key_grad[span, :] = key_sum
            value_grad[span, :] = value_sum
            return tuple(result)

        accs = tuple(jnp.zeros((2 * width, head), F32) for _ in pairs)
        accs = lax.fori_loop(0, clear_from, lambda s, w: chunk(s, w, False), accs)
        accs = lax.fori_loop(clear_from, clear_to, lambda s, w: chunk(s, w, True), accs)
        accs = lax.fori_loop(clear_to, count, lambda s, w: chunk(s, w, False), accs)
        for pair, acc in zip(pairs, accs):
            acc = acc * (head**-0.5)
            for h in range(2):
                value = acc[h * width : (h + 1) * width]
                low, high = value[:, :half], value[:, half:]
                start = (pair * 2 + h) * head
                gq_ref[block, :, start : start + half] = (low * cosine + high * sine).astype(BF16)
                gq_ref[block, :, start + half : start + head] = (
                    high * cosine - low * sine
                ).astype(BF16)

    grad_query = gq_ref[...].reshape(blocks * width, heads * head)
    size = latent_ref.shape[2]
    piece = 256
    for start in range(0, size, piece):
        value = dot_nt(grad_query, up_ref[start : start + piece, :])
        latent_ref[:, :, start : start + piece] = value.astype(BF16).reshape(blocks, width, piece)
    mixed = out_ref[...].reshape(blocks * width, heads * head)
    latent = stack_lane((lane_a, lane_b, lane_c, lane_d, lane_e))
    for h in range(heads):
        span = slice(h * head, (h + 1) * head)
        at = slice((h % 2) * head, (h % 2 + 1) * head)
        target = (out_own, out_sib)[h // 2]
        target[at, :] = dot_tn(mixed[:, span], branch).astype(BF16)
        target = (up_own, up_sib)[h // 2]
        target[:, at] = dot_tn(latent, grad_query[:, span]).astype(BF16)
    c = meta[1]
    for chip in range(2 * blocks):
        for target, cc in ((kv_own, c), (kv_sib, 1 - c)):
            span = pl.ds(pl.multiple_of((chip * 2 + cc) * width, width), width)
            target[chip, :, :head] = key_grad[span, :].astype(BF16)
            target[chip, :, head:] = value_grad[span, :].astype(BF16)


def kernel_specs(count):
    smem = pl.BlockSpec(memory_space=pltpu.SMEM)
    vmem = pl.BlockSpec(memory_space=pltpu.VMEM)
    return [smem] + [vmem] * count


def column_kernel(meta, normed_ref, *targets):
    width = targets[0].shape[0]
    z, c = meta[0], meta[1]
    for step, target in zip((0, 2, 1, 3), targets):
        place = (z + 4 - step) % 4
        for at, (cc, y) in enumerate(((c, 0), (c, 1), (1 - c, 0), (1 - c, 1))):
            start = pl.multiple_of(((y * 4 + place) * 2 + cc) * width, width)
            target[:, at * width : (at + 1) * width] = normed_ref[:, pl.ds(start, width)]


def first_kernel(col_a, col_b, col_c, col_d, g_a, g_b, g_c, g_d, g_e, own_ref, other_ref):
    columns = stack_lane((col_a, col_b, col_c, col_d))
    grads = stack_lane((g_a, g_b, g_c, g_d, g_e))
    half = own_ref.shape[0]
    own_ref[...] = dot_tn(columns[:, :half], grads)
    other_ref[...] = dot_tn(columns[:, half:], grads).astype(BF16)


def first_weights(columns, lane):
    half, size = columns[0].shape[1] // 2, lane[0].shape[1]
    return pl.pallas_call(
        first_kernel,
        out_shape=(
            jax.ShapeDtypeStruct((half, size), F32),
            jax.ShapeDtypeStruct((half, size), BF16),
        ),
        in_specs=kernel_specs(9)[1:],
        out_specs=tuple(kernel_specs(2)[1:]),
        compiler_params=pltpu.CompilerParams(vmem_limit_bytes=16 * 2**20),
        cost_estimate=pl.CostEstimate(
            flops=800_000_000, bytes_accessed=5_000_000, transcendentals=0
        ),
        name="first_weights",
    )(*columns, *lane)


def pick_columns(normed, z, c):
    width = normed.shape[0]
    return pl.pallas_call(
        column_kernel,
        out_shape=(jax.ShapeDtypeStruct((width, 4 * width), BF16),) * 4,
        in_specs=kernel_specs(1),
        out_specs=tuple(kernel_specs(4)[1:]),
        name="pick_columns",
    )(jnp.stack([z, c]).astype(jnp.int32), normed)


def make_queries(lane, up, cosine, sine, blocks):
    width = lane[0].shape[0]
    return pl.pallas_call(
        query_kernel,
        out_shape=jax.ShapeDtypeStruct((blocks, width, up.shape[1]), BF16),
        in_specs=kernel_specs(8)[1:],
        out_specs=kernel_specs(1)[1],
        compiler_params=pltpu.CompilerParams(vmem_limit_bytes=24 * 2**20),
        cost_estimate=pl.CostEstimate(
            flops=1_100_000_000, bytes_accessed=5_000_000, transcendentals=0
        ),
        name="make_queries",
    )(*lane, up, cosine, sine)


def attend(meta, query, kv, place, begin):
    blocks, width, size = query.shape
    head = kv.shape[1] // 2
    shape = jax.ShapeDtypeStruct
    return pl.pallas_call(
        attend_kernel,
        out_shape=(
            shape(query.shape, BF16),
            shape((blocks, size // head // 2, 1, 2 * width), F32),
        ),
        in_specs=kernel_specs(4),
        out_specs=tuple(kernel_specs(2)[1:]),
        compiler_params=pltpu.CompilerParams(vmem_limit_bytes=32 * 2**20),
        cost_estimate=pl.CostEstimate(
            flops=20_000_000_000, bytes_accessed=5_000_000, transcendentals=3_400_000
        ),
        name="attend",
    )(meta, query, kv, place, begin)


def project_kernel(meta, mixed_ref, own_ref, across_ref, sib_ref, across_sib_ref, part_ref):
    blocks, width, model = part_ref.shape
    head = own_ref.shape[0]
    y = meta[0]
    piece = 512
    for start in range(0, model, piece):
        total = None
        for at, (ref, yy) in enumerate(
            ((own_ref, y), (across_ref, 1 - y), (sib_ref, y), (across_sib_ref, 1 - y))
        ):
            first = pl.multiple_of((at // 2 * 2 + yy) * head, head)
            left = mixed_ref[:, :, pl.ds(first, head)].reshape(blocks * width, head)
            value = dot(left, ref[:, start : start + piece])
            total = value if total is None else total + value
        part_ref[:, :, start : start + piece] = total.astype(BF16).reshape(blocks, width, piece)


def project(meta, mixed, pieces):
    blocks, width, _ = mixed.shape
    model = pieces[0].shape[1]
    return pl.pallas_call(
        project_kernel,
        out_shape=jax.ShapeDtypeStruct((blocks, width, model), BF16),
        in_specs=kernel_specs(5),
        out_specs=kernel_specs(1)[1],
        compiler_params=pltpu.CompilerParams(vmem_limit_bytes=24 * 2**20),
        cost_estimate=pl.CostEstimate(
            flops=2_200_000_000, bytes_accessed=7_500_000, transcendentals=0
        ),
        name="project",
    )(meta, mixed, *pieces)


def feed_kernel(n_ref, cot_ref, own_ref, sib_ref, down_ref, hid_ref, go_ref, gs_ref, back_ref):
    slot = down_ref.shape[0] // 2
    blocks, _, size = own_ref.shape
    normed = n_ref[...]
    grad_hidden = dot_nt(cot_ref[...], down_ref[...])
    back = None
    for at, (weight, grad_ref) in enumerate(((own_ref, go_ref), (sib_ref, gs_ref))):
        span = slice(at * slot, (at + 1) * slot)
        both = jnp.concatenate([dot(normed, weight[i]) for i in range(blocks)], axis=1)
        gate, lift = both[:, :slot], both[:, slot:]
        grad = grad_hidden[:, span]
        sigmoid = jax.nn.sigmoid(gate)
        active = gate * sigmoid
        hid_ref[:, span] = (active * lift).astype(BF16)
        grad_ref[:, :slot] = (grad * lift * sigmoid * (1.0 + gate * (1.0 - sigmoid))).astype(BF16)
        grad_ref[:, slot:] = (grad * active).astype(BF16)
        for i in range(blocks):
            part = dot_nt(grad_ref[:, i * size : (i + 1) * size], weight[i])
            back = part if back is None else back + part
    back_ref[...] = back.astype(BF16)


def combine_kernel(feed_ref, feed_got, down_ref, down_got, out_ref):
    parts, owners, quarter, _ = out_ref.shape
    wide = feed_ref.shape[1]
    for owner in range(owners):
        for x in range(parts):
            span = slice((owner * parts + x) * quarter, (owner * parts + x + 1) * quarter)
            feed = feed_ref[span, :].astype(F32) + feed_got[span, :].astype(F32)
            down = down_ref[span, :].astype(F32) + down_got[span, :].astype(F32)
            out_ref[x, owner, :, :wide] = feed.astype(BF16)
            out_ref[x, owner, :, wide:] = down.astype(BF16)


def combine(feed, feed_got, down, down_got):
    model, wide = feed.shape
    parts, owners, steps = 4, 16, 4
    share = model // (parts * owners)
    total = wide + down.shape[1]

    def row(value):
        return pl.BlockSpec((model // steps, value.shape[1]), lambda i: (i, 0))

    result = pl.pallas_call(
        combine_kernel,
        out_shape=jax.ShapeDtypeStruct((parts, owners, share, total), BF16),
        grid=(steps,),
        in_specs=[row(feed), row(feed_got), row(down), row(down_got)],
        out_specs=pl.BlockSpec((parts, owners // steps, share, total), lambda i: (0, i, 0, 0)),
        compiler_params=pltpu.CompilerParams(vmem_limit_bytes=24 * 2**20),
        cost_estimate=pl.CostEstimate(flops=5_000_000, bytes_accessed=15_000_000, transcendentals=0),
        name="combine",
    )(feed, feed_got, down, down_got)
    return result.reshape(model, total)


def spill_kernel(sum_ref, gate_weight, lift_weight, gate_ref, lift_ref, down_ref, gain_ref):
    parts, owners, quarter, _ = sum_ref.shape
    hidden = down_ref.shape[0]
    width = parts * quarter
    for owner in range(owners):
        for x in range(parts):
            span = slice(x * quarter, (x + 1) * quarter)
            at = slice(owner * hidden, (owner + 1) * hidden)
            gate_ref[span, at] = sum_ref[x, owner, :, :hidden].astype(F32)
            lift_ref[span, at] = sum_ref[x, owner, :, SLOT : SLOT + hidden].astype(F32)
        block = sum_ref[:, owner, :, 2 * SLOT :].astype(F32).reshape(width, SLOT)
        down_ref[:, owner * width : (owner + 1) * width] = block.T[:hidden]
    gain_ref[...] = jnp.sum(
        gate_ref[...] * gate_weight[...].astype(F32) + lift_ref[...] * lift_weight[...].astype(F32),
        axis=1,
        keepdims=True,
    )


def spill(summed, gate_weight, lift_weight, hidden):
    parts, owners, quarter, _ = summed.shape
    shape = jax.ShapeDtypeStruct
    return pl.pallas_call(
        spill_kernel,
        out_shape=(shape((parts * quarter, owners * hidden), F32),) * 2
        + (shape((hidden, owners * parts * quarter), F32), shape((parts * quarter, 1), F32)),
        in_specs=kernel_specs(3)[1:],
        out_specs=tuple(kernel_specs(4)[1:]),
        compiler_params=pltpu.CompilerParams(vmem_limit_bytes=40 * 2**20),
        cost_estimate=pl.CostEstimate(flops=5_000_000, bytes_accessed=17_000_000, transcendentals=0),
        name="spill",
    )(summed, gate_weight, lift_weight)


def heads_kernel(fence, out_ref, out_got, up_ref, up_got, pack_ref):
    model = out_ref.shape[1]
    head = out_ref.shape[0] // 2
    share = head // 8
    owners = 16
    depth = up_ref.shape[0] // owners
    few = depth // 8
    for y in range(2):
        for part in range(8):
            at = part * 2 + y
            span = slice(y * head + part * share, y * head + (part + 1) * share)
            total = out_ref[span, :].astype(F32) + out_got[span, :].astype(F32)
            pack_ref[at, :share, :] = total.astype(BF16)
            cols = slice(y * head, (y + 1) * head)
            for pair in range(owners // 2):
                slabs = []
                for owner in (2 * pair, 2 * pair + 1):
                    rows_at = slice(owner * depth + part * few, owner * depth + (part + 1) * few)
                    slabs.append(
                        up_ref[rows_at, cols].astype(F32) + up_got[rows_at, cols].astype(F32)
                    )
                pack_ref[at, share:, pair * head : (pair + 1) * head] = jnp.concatenate(
                    slabs, axis=0
                ).astype(BF16)


def pack_heads(fence, out, out_got, up, up_got):
    head, model = out.shape[0] // 2, out.shape[1]
    return pl.pallas_call(
        heads_kernel,
        out_shape=jax.ShapeDtypeStruct((16, head // 8 + 16, model), BF16),
        in_specs=kernel_specs(4),
        out_specs=kernel_specs(1)[1],
        compiler_params=pltpu.CompilerParams(vmem_limit_bytes=24 * 2**20),
        cost_estimate=pl.CostEstimate(flops=2_000_000, bytes_accessed=9_500_000, transcendentals=0),
        name="pack_heads",
    )(fence, out, out_got, up, up_got)


def finish_kernel(
    last_ref,
    down_weight,
    key_weight,
    value_weight,
    up_weight,
    out_ref,
    up_ref,
    down_ref,
    key_ref,
    value_ref,
    first_ref,
    query_ref,
):
    parts, _, model = last_ref.shape
    out_rows, up_rows = out_ref.shape[0] // parts, up_ref.shape[0] // parts
    rows_each = down_ref.shape[0] // parts
    latent, head = down_ref.shape[1], key_ref.shape[1]
    for part in range(parts):
        out_ref[part * out_rows : (part + 1) * out_rows, :] = last_ref[part, :out_rows, :].astype(
            F32
        )
        up = last_ref[part, out_rows : out_rows + 2 * up_rows, :].astype(F32)
        span = slice(part * up_rows, (part + 1) * up_rows)
        up_ref[span, :model] = up[:up_rows]
        up_ref[span, model:] = up[up_rows:]
        first = last_ref[part, out_rows + 2 * up_rows :, :].astype(F32)
        span = slice(part * rows_each, (part + 1) * rows_each)
        down_ref[span, :] = first[:, :latent]
        key_ref[span, :] = first[:, latent : latent + head]
        value_ref[span, :] = first[:, latent + head : latent + 2 * head]
    total = None
    for grad, weight in ((down_ref, down_weight), (key_ref, key_weight), (value_ref, value_weight)):
        value = jnp.sum(grad[...] * weight[...].astype(F32), axis=1, keepdims=True)
        total = value if total is None else total + value
    first_ref[...] = total
    query_ref[...] = jnp.sum(up_ref[...] * up_weight[...].astype(F32), axis=1, keepdims=True)


def finish(last, down_weight, key_weight, value_weight, up_weight):
    parts, _, model = last.shape
    shape = jax.ShapeDtypeStruct
    width, depth, head = down_weight.shape[0], up_weight.shape[0], key_weight.shape[1]
    return pl.pallas_call(
        finish_kernel,
        out_shape=(
            shape((head, model), F32),
            shape(up_weight.shape, F32),
            shape(down_weight.shape, F32),
            shape(key_weight.shape, F32),
            shape(value_weight.shape, F32),
            shape((width, 1), F32),
            shape((depth, 1), F32),
        ),
        in_specs=kernel_specs(5)[1:],
        out_specs=tuple(kernel_specs(7)[1:]),
        compiler_params=pltpu.CompilerParams(vmem_limit_bytes=24 * 2**20),
        cost_estimate=pl.CostEstimate(flops=2_000_000, bytes_accessed=8_000_000, transcendentals=0),
        name="finish",
    )(last, down_weight, key_weight, value_weight, up_weight)


def feed_forward(normed, cotangent, own, sib, down):
    count, model = normed.shape
    tile, slots = 256, down.shape[0]
    row = pl.BlockSpec((tile, model), lambda i: (i, 0))
    slot_row = pl.BlockSpec((tile, slots), lambda i: (i, 0))

    def fixed(value):
        return pl.BlockSpec(value.shape, lambda i: (0,) * value.ndim)

    shape = jax.ShapeDtypeStruct
    return pl.pallas_call(
        feed_kernel,
        grid=(count // tile,),
        out_shape=(shape((count, slots), BF16),) * 3 + (shape((count, model), BF16),),
        in_specs=[row, row, fixed(own), fixed(sib), fixed(down)],
        out_specs=(slot_row,) * 3 + (row,),
        compiler_params=pltpu.CompilerParams(vmem_limit_bytes=52 * 2**20),
        cost_estimate=pl.CostEstimate(
            flops=19_000_000_000, bytes_accessed=32_000_000, transcendentals=800_000
        ),
        name="feed_forward",
    )(normed, cotangent, own, sib, down)


def attend_back(meta, branch, kv, up, proj, cosine, sine, place, begin, query, out, log, lane):
    blocks, _, rows_all = place.shape
    width, head = rows_all // 2, kv.shape[1] // 2
    shape = jax.ShapeDtypeStruct
    return pl.pallas_call(
        attend_back_kernel,
        out_shape=(
            shape(query.shape, BF16),
            shape((blocks, width, up.shape[0]), BF16),
            shape((2 * blocks, width, 2 * head), BF16),
            shape((2 * blocks, width, 2 * head), BF16),
            shape((2 * head, proj[0].shape[1]), BF16),
            shape((2 * head, proj[0].shape[1]), BF16),
            shape((up.shape[0], 2 * head), BF16),
            shape((up.shape[0], 2 * head), BF16),
        ),
        in_specs=kernel_specs(23),
        out_specs=tuple(kernel_specs(8)[1:]),
        scratch_shapes=[pltpu.VMEM(query.shape, BF16)]
        + [pltpu.VMEM((kv.shape[0], head), F32)] * 2,
        compiler_params=pltpu.CompilerParams(vmem_limit_bytes=48 * 2**20),
        cost_estimate=pl.CostEstimate(
            flops=24_000_000_000, bytes_accessed=20_000_000, transcendentals=3_400_000
        ),
        name="attend_back",
    )(meta, *branch, kv, up, *proj, cosine, sine, place, begin, query, out, log, *lane)


def shards(
    tokens,
    doc_lengths,
    first_gain,
    query_down,
    key_proj,
    value_proj,
    query_gain,
    query_up,
    out_proj,
    second_gain,
    gate_proj,
    up_proj,
    down_proj,
    cotangent,
):
    width, model = tokens.shape
    latent_width = query_down.shape[1]
    head = key_proj.shape[1]
    depth = query_up.shape[0]
    hidden_width = gate_proj.shape[1] // 16
    lane_width = latent_width + 2 * head

    v, x, y, z, c = (lax.axis_index(axis) for axis in AXES)

    weights = lax.all_gather(
        jnp.concatenate([query_down, key_proj, value_proj], axis=1), SEQ, axis=0, tiled=True
    )

    gain_rows = jnp.zeros((16, head), BF16)
    gain_rows = gain_rows.at[0, :width].set(first_gain).at[1, :width].set(second_gain)
    gain_rows = gain_rows.at[2, :depth].set(query_gain)
    heads = query_up.reshape(depth, 2, 8, head)
    quarter = width // 4
    feed_rows = [
        jnp.pad(
            lax.dynamic_slice_in_dim(weight, x * quarter, quarter, 0).reshape(
                quarter, 16, hidden_width
            ),
            ((0, 0), (0, 0), (0, SLOT - hidden_width)),
        )
        for weight in (gate_proj, up_proj)
    ]
    feed_rows = jnp.concatenate(feed_rows, axis=2)
    parts = [
        jnp.broadcast_to(heads[:, at].transpose(1, 0, 2)[None], (2, 8, depth, head)).reshape(
            16, depth, head
        )
        for at in range(2)
    ]
    parts = parts + [
        feed_rows[..., at * head : (at + 1) * head].transpose(1, 0, 2) for at in range(3)
    ]
    parts = parts + [jnp.broadcast_to(gain_rows[None], (16, 16, head))]
    swapped_weights = exchange(jnp.concatenate(parts, axis=1), SEQ)
    first_row = 2 * depth + 3 * quarter
    gain_one = swapped_weights[:, first_row, :width].reshape(1, model).astype(F32)
    gain_two = swapped_weights[:, first_row + 1, :width].reshape(1, model).astype(F32)
    gain_query = swapped_weights[:, first_row + 2, :depth].reshape(1, latent_width).astype(F32)
    up_pair = jnp.concatenate(
        [
            swapped_weights[:, at * depth : (at + 1) * depth].reshape(latent_width, head)
            for at in range(2)
        ],
        axis=1,
    )
    up_chip = jnp.concatenate([up_pair, sibling(up_pair)], axis=1)
    feed_parts = swapped_weights[:, 2 * depth : first_row].reshape(16 * 3 * quarter, head)

    lengths = doc_lengths[0]
    z_at = jnp.stack([z, (z + 2) % 4, (z + 1) % 4, (z + 3) % 4])
    blocks = (y * 4 + z_at) * 2 + c
    token_index = blocks[:, None] * width + jnp.arange(width, dtype=jnp.int32)[None, :]
    doc_start = layout(lengths, token_index.reshape(-1)).reshape(token_index.shape)
    cosine, sine = rope_tables((token_index - doc_start).reshape(-1), head)
    meta = jnp.concatenate([jnp.stack([y, c]), jnp.max(doc_start, axis=1), blocks])
    meta = meta.astype(jnp.int32)
    place_row = jnp.tile(token_index, (1, 2))[:, None, :]
    begin_row = jnp.tile(doc_start, (1, 2))[:, None, :]
    cos_own, sin_own = cosine[:width], sine[:width]

    tokens_float = tokens.astype(F32)
    inv_one = inverse_rms(tokens_float)
    with jax.named_scope("out_chip"):
        out_sib = sibling(out_proj)
    for piece in (up_chip, out_sib):
        gain_one = after(gain_one, piece)
    normed = (tokens_float * inv_one * gain_one).astype(BF16)
    first = dot(normed, weights)
    latent = first[:, :latent_width]
    inv_latent = inverse_rms(latent)
    latent_n = (latent * inv_latent * gain_query).astype(BF16)
    key_rot = rotate(first[:, latent_width : latent_width + head], cos_own, sin_own).astype(BF16)
    value_low = first[:, latent_width + head :].astype(BF16)

    kv = lax.all_gather(
        jnp.concatenate([key_rot, value_low], axis=1), SEQ, axis=0, tiled=True
    )
    with jax.named_scope("lane"):
        lane = ring_gather(latent_n)
    with jax.named_scope("out_chip"):
        out_across = turn(after(out_proj, first), "y", 1)
    lane = (lane[0], after(lane[1], out_across)) + lane[2:]
    query_rot = make_queries(lane, up_chip, cosine, sine, 4)
    with jax.named_scope("out_chip"):
        out_across_sib = sibling(after(out_across, query_rot))
    attended, log_total = attend(meta, query_rot, kv, place_row, begin_row)
    out_pieces = (out_proj, out_across, out_sib, out_across_sib)
    cot_all = lax.all_gather(after(after(cotangent, kv), query_rot), ("y", "z"), axis=0, tiled=True)
    attended_rows = attended.reshape(4 * width, 4 * head)
    mixed = project(meta, attended, out_pieces)
    with jax.named_scope("residual"):
        residual = tokens_float + ring_scatter(mixed)
    inv_two = inverse_rms(residual)
    normed_two = (residual * inv_two * gain_two).astype(BF16)

    normed_all = lax.all_gather(normed_two, ("y", "z"), axis=0, tiled=True)
    with jax.named_scope("feed_weights"):
        feed_ring = ring_gather(after(feed_parts, normed_two), "x")
        feed_own = jnp.zeros((3, 16, 4, quarter, head), BF16)
        for part, step, first_owner in zip(feed_ring, (0, 2, 2, 1, 3), (0, 0, 8, 0, 0)):
            part = part.reshape(-1, 3, quarter, head).transpose(1, 0, 2, 3)[:, :, None]
            feed_own = lax.dynamic_update_slice(
                feed_own, part, (0, first_owner, (x + step) % 4, 0, 0)
            )
        feed_own = feed_own.reshape(3, model, head)
        feed_sib = sibling(feed_own)
        down_own = jnp.pad(down_proj, ((0, SLOT - hidden_width), (0, 0)))
        down_chip = jnp.concatenate([down_own, sibling(after(down_own, kv))], axis=0)
    hidden, grad_own, grad_sib, back = feed_forward(
        normed_all, cot_all, feed_own, feed_sib, down_chip
    )
    grad_normed_two = lax.psum_scatter(back, ("y", "z"), scatter_dimension=0, tiled=True)
    grad_normed_two = grad_normed_two.astype(F32)

    with jax.named_scope("feed_grad"):
        feed_other = sibling(dot_tn(normed_all, grad_sib).astype(BF16))
        down_other = sibling(dot_tn(cot_all, hidden[:, SLOT:]).astype(BF16))
        feed_grad = dot_tn(normed_all, grad_own).astype(BF16)
        down_grad = dot_tn(cot_all, hidden[:, :SLOT]).astype(BF16)
    with jax.named_scope("feed_grad"):
        feed_grad = combine(feed_grad, feed_other, down_grad, down_other)
        feed_part = lax.psum_scatter(feed_grad, "x", scatter_dimension=0, tiled=True)
        fed = lax.optimization_barrier(dot(hidden, down_chip).astype(BF16))
    grad_normed_two = after(after(grad_normed_two, feed_grad), fed)
    grad_two = rms_back(residual, inv_two, gain_two, grad_normed_two)
    grad_residual = cotangent.astype(F32) + grad_two

    with jax.named_scope("branch"):
        branch = ring_gather(grad_residual.astype(BF16))
    with jax.named_scope("layer_out"):
        fed = fed.reshape(2, 4 * width, model)
        fed_own = lax.dynamic_index_in_dim(fed, y, 0, keepdims=False)
        fed_across = lax.dynamic_index_in_dim(fed, 1 - y, 0, keepdims=False)
        fed_across = turn(after(fed_across, branch[1]), "y", 1)
    grad_queries, latent_parts, kv_own, kv_sib, out_grad, out_grad_sib, up_grad, up_sib = attend_back(
        meta,
        branch,
        kv,
        up_chip,
        out_pieces,
        cosine,
        sine,
        place_row,
        begin_row,
        query_rot,
        attended,
        log_total,
        lane,
    )
    with jax.named_scope("feed_grad"):
        feed_part = feed_part.reshape(16, quarter, 3 * SLOT)
        swapped = exchange(feed_part[..., : 2 * SLOT], SEQ)
    with jax.named_scope("latent_grad"):
        grad_latent_n = ring_scatter(latent_parts)
    with jax.named_scope("heads_grad"):
        heads_parts = pack_heads(
            ((fed_across[0, 0] + grad_latent_n[0, 0] + swapped[0, 0, 0]) * 0).astype(jnp.int32).reshape(1),
            out_grad,
            sibling(out_grad_sib),
            up_grad,
            sibling(up_sib),
        )
        heads_got = exchange(heads_parts, ACROSS)
    with jax.named_scope("kv_grad"):
        kv_grad = kv_own.astype(F32) + sibling(kv_sib).astype(F32)
        kv_grad = after(kv_grad, heads_got).astype(BF16)
        kv_sum = total_of(exchange(kv_grad, ("y", "z")))
    grad_keys = rotate_back(kv_sum[:, :head], cos_own, sin_own).astype(BF16)
    grad_values = kv_sum[:, head:].astype(BF16)
    grad_latent = rms_back(latent, inv_latent, gain_query, grad_latent_n)
    grad_latent = grad_latent.astype(BF16)
    grad_first = jnp.concatenate([grad_latent, grad_keys, grad_values], axis=1)
    with jax.named_scope("first_lane"):
        first_lane = ring_gather(grad_first)
    with jax.named_scope("columns"):
        columns = pick_columns(normed, z + (kv_sum[0, 0] * 0).astype(jnp.int32), c)
        columns = (columns[0],) + tuple(
            turn(part, "z", -step) for part, step in zip(columns[1:], (2, 1, 3))
        )
    own_first, first_other = first_weights(columns, first_lane)
    own_first = own_first + sibling(first_other).astype(F32)
    with jax.named_scope("feed_grad"):
        feed_part = jnp.concatenate([swapped, feed_part[..., 2 * SLOT :]], axis=2)
        feed_across = after(turn(feed_part, "v", 1), kv_sum)
        feed_part = (feed_part.astype(F32) + feed_across.astype(F32)).astype(BF16)
        feed_sum = lax.all_gather(
            feed_part.reshape(16 * quarter, 3 * SLOT), "x", axis=0, tiled=True
        )
    with jax.named_scope("layer_out"):
        fed = fed_own.astype(F32) + after(fed_across.astype(F32), heads_parts)
        fed_part = lax.psum_scatter(fed.astype(BF16), "z", scatter_dimension=0, tiled=True)
        layer_out = (residual + fed_part.astype(F32)).astype(BF16)
    with jax.named_scope("heads_grad"):
        heads_part = total_of(heads_got).astype(BF16)
        out_part, up_part = heads_part[: head // 8], heads_part[head // 8 :]
        up_part = up_part.reshape(16, 8, head).transpose(1, 0, 2)
    with jax.named_scope("up_grad"):
        up_part = exchange(after(up_part, kv_sum).reshape(16, depth // 8, head), SEQ)
        up_part = up_part.reshape(2, 8, depth // 8, head).transpose(0, 2, 1, 3)
        up_part = up_part.reshape(-1, model)
    grad_normed = dot_nt(grad_latent, weights[:, :latent_width])
    grad_normed = grad_normed + dot_nt(grad_first[:, latent_width:], weights[:, latent_width:])
    grad_one = rms_back(tokens_float, inv_one, gain_one, grad_normed)
    input_grad = grad_residual + grad_one

    share = width // 8
    tail = own_first.reshape(2, 8, share, lane_width).transpose(1, 0, 2, 3)
    tail = total_of(exchange(tail.reshape(16, share, lane_width).astype(BF16), ACROSS))
    first_part = jnp.pad(tail.astype(BF16), ((0, 0), (0, model - lane_width)))
    last_sum = spread(jnp.concatenate([out_part, up_part, first_part], axis=0), DP)

    gate_sum, lift_sum, down_sum, second_gain_sum = spill(
        feed_sum.reshape(4, 16, quarter, 3 * SLOT), gate_proj, up_proj, hidden_width
    )
    out_sum, up_sum, down_first, key_sum, value_sum, first_gain_sum, query_gain_sum = finish(
        last_sum, query_down, after(key_proj, second_gain_sum), value_proj, query_up
    )
    first_gain_sum = first_gain_sum.reshape(-1) / first_gain.astype(F32)
    query_gain_sum = query_gain_sum.reshape(-1) / query_gain.astype(F32)
    second_gain_sum = second_gain_sum.reshape(-1) / second_gain.astype(F32)
    return (
        layer_out,
        input_grad,
        first_gain_sum,
        down_first,
        key_sum,
        value_sum,
        query_gain_sum,
        up_sum,
        out_sum,
        second_gain_sum,
        gate_sum,
        lift_sum,
        down_sum,
    )


def solution(mesh):
    fine = Mesh(mesh.devices.reshape(SIZES), AXES)
    split, groups = P(DP + SEQ, None), P(DP, None)
    matrix, vector = P(SEQ, None), P(SEQ)
    in_specs = (
        split,
        groups,
        vector,
        matrix,
        matrix,
        matrix,
        vector,
        matrix,
        matrix,
        vector,
        matrix,
        matrix,
        matrix,
        split,
    )
    out_specs = (
        split,
        split,
        vector,
        matrix,
        matrix,
        matrix,
        vector,
        matrix,
        matrix,
        vector,
        matrix,
        matrix,
        matrix,
    )
    return jax.shard_map(shards, mesh=fine, in_specs=in_specs, out_specs=out_specs, check_vma=False)
```

time: 803 us -> 668 us (0.83)
  starting transfers between devices: 155 us -> 88.6 us
  waiting for transfers between devices: 350 us -> 285 us
  Pallas kernels: 34.3 us -> 83.2 us
  local copies, waits for them, and re-layouts: 100 us -> 53.3 us
  matrix products: 70.1 us -> 31.6 us
  blocking collectives: 0 us -> 30.3 us
  between operations: 17.6 us -> 27.4 us
  other arithmetic: 66.7 us -> 57.3 us
    ppermute x108 -> x41, waiting for transfers between devices: 328 us -> 159 us  [turn(): lax.ppermute(value, axis, [(i, (i + step) % size) for i in range(size)])]
    ppermute x108 -> x41, starting transfers between devices: 138 us -> 45 us  [turn(): lax.ppermute(value, axis, [(i, (i + step) % size) for i in range(size)])]
    all_to_all x4 -> x6, waiting for transfers between devices: 22 us -> 94.1 us  [exchange(): return lax.all_to_all(parts, axes, 0, 0)]
    pallas_call x2 -> x13, Pallas kernels: 34.3 us -> 83.2 us  [the longest x1 25.5 us: feed_forward(): pl.pallas_call(feed_kernel, grid=(count // tile,), out_shape=(shape((coun...]
    all_to_all x0 -> x1, blocking collectives: none -> 30.3 us  [exchange(): return lax.all_to_all(parts, axes, 0, 0)]
    unnamed x276 -> x169, local copies, waits for them, and re-layouts: 52.1 us -> 22.8 us
    all_to_all x4 -> x6, starting transfers between devices: 17.5 us -> 43.2 us  [exchange(): return lax.all_to_all(parts, axes, 0, 0)]
    reduce_scatter x0 -> x3, waiting for transfers between devices: none -> 21.9 us  [the longest x1 21.9 us: shards(): lax.psum_scatter(back, ('y', 'z'), scatter_dimension=0, tiled=True)]
  transfers between devices with their start and end apart: 114 -> 55, of which waited for: 55 -> 25; matrix products, arithmetic and copies ran while one was open for 24% -> 17% of each run, Pallas kernels for 2% -> 8%
where the time goes in v2:
time: 668 us; the launch traced here: 657 us
  waiting for transfers between devices  285 us (43%)
  starting transfers between devices  88.6 us (13%)
  Pallas kernels  83.2 us (12%)
  other arithmetic  57.3 us (9%)
  local copies, waits for them, and re-layouts  53.3 us (8%)
  matrix products  31.6 us (5%)
  blocking collectives  30.3 us (5%)
  between operations  27.4 us (4%)
    ppermute x41, waiting for transfers between devices, turn(): lax.ppermute(value, axis, [(i, (i + step) % size) for i in range(size)])  159 us
    all_to_all x6, waiting for transfers between devices, exchange(): return lax.all_to_all(parts, axes, 0, 0)  94.1 us
    ppermute x41, starting transfers between devices, turn(): lax.ppermute(value, axis, [(i, (i + step) % size) for i in range(size)])  45 us
    all_to_all x6, starting transfers between devices, exchange(): return lax.all_to_all(parts, axes, 0, 0)  43.2 us
    all_to_all x1, blocking collectives, exchange(): return lax.all_to_all(parts, axes, 0, 0)  30.3 us
    pallas_call x1, Pallas kernels, feed_forward(): pl.pallas_call(feed_kernel, grid=(count // tile,), out_shape=(shape((coun...  25.5 us
    pallas_call x1, Pallas kernels, attend_back(): pl.pallas_call(attend_back_kernel, out_shape=(shape(query.shape, BF16), s...  23.8 us
    unnamed x169, local copies, waits for them, and re-layouts  22.8 us
  transfers between devices with their start and end apart: 55, of which 25 were waited for; matrix products, arithmetic and copies ran while one was open for 17% of the time, Pallas kernels for 8%

profile of v2, /device:TPU:0, one launch (start us, length us, event | category | flops | bytes accessed | tf_op | source)
XLA Modules:
  0.0 656.8 jit_solution(8071683177235176492)
XLA Ops:
  17.4 6.6 all-to-all-start
  29.1 36.2 %all-to-all-done = bf16[16,240,256]{2,1,0:T(8,128)(2,1)} async-done(((bf16[16,240,256]{2,1,0:T(8,128)(2,1)}), bf16[16,240,256]{2,1,0:T(8,128)(2,1)}, u32[]{:S(2)}, u32[]{:S(2)}) %all-to-all-start) | async-done | bytes 1966112 | tf_op jit(solution)/shard_map/all_to_all | solution.py:38
  65.3 2.1 fusion.37
  71.2 5.5 all-gather.6.cloned.1.call-done
  76.7 4.0 fusion.39
  81.6 2.2 pad_maximum_fusion.3
  92.6 9.7 %collective-permute-done.1.lane_d = bf16[128,1024]{1,0:T(8,128)(2,1)S(1)} collective-permute-done((bf16[128,1024]{1,0:T(8,128)(2,1)S(1)}, bf16[128,1024]{1,0:T(8,128)(2,1)S(1)}, u32[]{:S(2)}, u32[]{:S(2)}) %collective-permute-start.1) | collective-permute-done | bytes 262176 | tf_op jit(solution)/shard_map/lane/ppermute | solution.py:21
  106.0 15.7 %collective-permute-done.3.across_ref.proj_b = bf16[256,2048]{1,0:T(8,128)(2,1)S(1)} collective-permute-done((bf16[256,2048]{1,0:T(8,128)(2,1)}, bf16[256,2048]{1,0:T(8,128)(2,1)S(1)}, u32[]{:S(2)}, u32[]{:S(2)}) %collective-permute-start.3) | collective-permute-done | bytes 1048608 | tf_op jit(solution)/shard_map/out_chip/ppermute | solution.py:21
  131.4 9.3 %attend.1 = (bf16[4,128,1024]{2,1,0:T(8,128)(2,1)S(1)}, f32[4,2,1,256]{3,2,1,0:T(1,128)S(1)}) custom-call(s32[10]{0:T(128)S(1)} %pad_add_fusion.meta, bf16[4,128,1024]{2,1,0:T(8,128)(2,1)S(1)} %make_queries.1.q_ref, bf16[2048,512]{1,0:T(8,128)(2,1)S(1)} %copy-done.23, s32[4,1,256]{2,1,0:T(1,128)S(1)} %bitcast.159, s32[4,1,256]{2,1,0:T(1,128)S(1)} %bitcast.157), custom_call_target="tpu_custom_call" | custom-call | flops 20000000000 | bytes 5000000 | tf_op jit(solution)/shard_map/attend/pallas_call | solution.py:428
  140.8 2.9 project.1.part_ref
  143.9 3.2 collective-permute-start.9
  147.1 40.5 %collective-permute-done.8.low_ref = bf16[64,2048]{1,0:T(8,128)(2,1)} collective-permute-done((bf16[64,2048]{1,0:T(8,128)(2,1)S(1)}, bf16[64,2048]{1,0:T(8,128)(2,1)}, u32[]{:S(2)}, u32[]{:S(2)}) %collective-permute-start.8) | collective-permute-done | bytes 262176 | tf_op jit(solution)/shard_map/residual/ppermute | solution.py:21
  187.6 2.4 ring_merge.2
  190.0 3.2 collective-permute-start.11
  194.0 11.3 %collective-permute-done.10 = bf16[128,2048]{1,0:T(8,128)(2,1)S(1)} collective-permute-done((bf16[128,2048]{1,0:T(8,128)(2,1)}, bf16[128,2048]{1,0:T(8,128)(2,1)S(1)}, u32[]{:S(2)}, u32[]{:S(2)}) %collective-permute-start.10) | collective-permute-done | bytes 524320 | tf_op jit(solution)/shard_map/residual/ppermute | solution.py:21
  212.1 2.8 collective-permute-start.12
  214.8 16.2 %collective-permute-done.12 = bf16[1536,256]{1,0:T(8,128)(2,1)S(1)} collective-permute-done((bf16[1536,256]{1,0:T(8,128)(2,1)S(1)}, bf16[1536,256]{1,0:T(8,128)(2,1)S(1)}, u32[]{:S(2)}, u32[]{:S(2)}) %collective-permute-start.12) | collective-permute-done | bytes 786464 | tf_op jit(solution)/shard_map/feed_weights/ppermute | solution.py:21
  231.1 3.8 collective-permute-start.13
  236.4 5.4 collective-permute-done.13
  242.8 3.5 collective-permute-done.15
  249.7 5.9 collective-permute-done.17
  255.6 2.3 pad_maximum_fusion.down_ref
  257.9 4.8 all-gather.10.cloned.1.call-done.n_ref
  262.7 25.5 %feed_forward.1 = (bf16[1024,768]{1,0:T(8,128)(2,1)S(1)}, bf16[1024,768]{1,0:T(8,128)(2,1)}, bf16[1024,768]{1,0:T(8,128)(2,1)}, bf16[1024,2048]{1,0:T(8,128)(2,1)}) custom-call(bf16[1024,2048]{1,0:T(8,128)(2,1)} %all-gather.10.cloned.1.call-done.n_ref, bf16[1024,2048]{1,0:T(8,128)(2,1)} %all-gather.12.cloned.1.call-done.cot_ref, ...), custom_call_target="tpu_custom_call" | custom-call | flops 19000000512 | bytes 32000000 | tf_op jit(solution)/shard_map/feed_forward/pallas_call | solution.py:678
  288.3 6.4 convolution_convert_fusion.1
  294.8 2.4 convolution_convert_fusion.3
  298.0 2.4 convolution_convert_fusion.4.down_ref
  300.4 3.8 convolution_convert_fusion.2.feed_ref
  305.7 2.1 copy-done
  307.9 5.6 convolution_convert_fusion
  318.5 21.9 %reduce-scatter.4.cloned.1.call-done = bf16[128,2048]{1,0:T(8,128)(2,1)} async-done(((bf16[1024,2048]{1,0:T(8,128)(2,1)}), bf16[128,2048]{1,0:T(8,128)(2,1)}) %reduce-scatter.4.cloned.1.call-update) | async-done | bytes 524304 | tf_op jit(solution)/shard_map/reduce_scatter | solution.py:852
  345.7 11.7 %collective-permute-done.20.branch_d = bf16[128,2048]{1,0:T(8,128)(2,1)S(1)} collective-permute-done((bf16[128,2048]{1,0:T(8,128)(2,1)S(1)}, bf16[128,2048]{1,0:T(8,128)(2,1)S(1)}, u32[]{:S(2)}, u32[]{:S(2)}) %collective-permute-start.20) | collective-permute-done | bytes 524320 | tf_op jit(solution)/shard_map/branch/ppermute | solution.py:21
  359.6 5.2 collective-permute-done.21.branch_b
  366.0 3.1 add_bitcast_fusion
  371.9 23.8 %attend_back.1 = (bf16[4,128,1024]{2,1,0:T(8,128)(2,1)}, bf16[4,128,1024]{2,1,0:T(8,128)(2,1)S(1)}, bf16[8,128,512]{2,1,0:T(8,128)(2,1)}, bf16[8,128,512]{2,1,0:...) custom-call(s32[10]{0:T(128)S(1)} %pad_add_fusion.meta, ...), custom_call_target="tpu_custom_call" | custom-call | flops 24000000000 | bytes 20000000 | tf_op jit(solution)/shard_map/attend_back/pallas_call | solution.py:696
  396.3 2.1 slice.341
  398.3 13.6 %all-to-all-start.1 = ((bf16[16,32,768]{2,1,0:T(8,128)(2,1)}), bf16[16,32,768]{2,1,0:T(8,128)(2,1)}, u32[]{:S(2)}, u32[]{:S(2)}) async-start(bf16[16,32,768]{2,1,0:T(8,128)(2,1)} %slice.341), calls=%async_computation.3 | async-start | bytes 1572864 | tf_op jit(solution)/shard_map/feed_grad/all_to_all | solution.py:38
  415.3 12.2 %collective-permute-done.25.low_ref = bf16[64,1024]{1,0:T(8,128)(2,1)S(1)} collective-permute-done((bf16[64,1024]{1,0:T(8,128)(2,1)S(1)}, bf16[64,1024]{1,0:T(8,128)(2,1)S(1)}, u32[]{:S(2)}, u32[]{:S(2)}) %collective-permute-start.25) | collective-permute-done | bytes 131104 | tf_op jit(solution)/shard_map/latent_grad/ppermute | solution.py:21
  430.1 3.5 collective-permute-start.28
  433.5 6.0 collective-permute-done.27
  446.5 4.3 pack_heads.1
  450.8 5.8 all-to-all-start.2
  458.5 4.5 fusion.2
  464.2 2.4 pad_maximum_fusion.2
  466.6 3.4 collective-permute-start.40
  470.1 28.9 %all-to-all-done.2 = bf16[16,48,2048]{2,1,0:T(8,128)(2,1)S(1)} async-done(((bf16[16,48,2048]{2,1,0:T(8,128)(2,1)}), bf16[16,48,2048]{2,1,0:T(8,128)(2,1)S(1)}, u32[]{:S(2)}, u32[]{:S(2)}) %all-to-all-start.2) | async-done | bytes 3145760 | tf_op jit(solution)/shard_map/heads_grad/all_to_all | solution.py:38
  502.1 30.3 %all_to_all.35 = bf16[8,128,512]{2,1,0:T(8,128)(2,1)S(1)} all-to-all(bf16[8,128,512]{2,1,0:T(8,128)(2,1)S(1)} %add_convert_fusion.1), channel_id=1, replica_groups=mesh['v'=2,'x'=4,'y'=2,'z'=4,'c'=2] {'y','z'}, dimensions={0} | all-to-all | bytes 2097152 | tf_op jit(solution)/shard_map/kv_grad/all_to_all | solution.py:38
  533.9 3.0 add_convert_fusion
  540.9 7.2 %collective-permute-done.35.g_d = bf16[128,1536]{1,0:T(8,128)(2,1)S(1)} collective-permute-done((bf16[128,1536]{1,0:T(8,128)(2,1)S(1)}, bf16[128,1536]{1,0:T(8,128)(2,1)S(1)}, u32[]{:S(2)}, u32[]{:S(2)}) %collective-permute-start.35) | collective-permute-done | bytes 393248 | tf_op jit(solution)/shard_map/first_lane/ppermute | solution.py:21
  553.8 2.3 collective-permute-start.33
  556.4 3.2 collective-permute-done.32.col_b
  564.5 2.3 collective-permute-done.39
  567.9 7.3 %all-to-all-start.5 = ((bf16[16,16,1536]{2,1,0:T(8,128)(2,1)}), bf16[16,16,1536]{2,1,0:T(8,128)(2,1)}, u32[]{:S(2)}, u32[]{:S(2)}) async-start(bf16[16,16,1536]{2,1,0:T(8,128)(2,1)} %bitcast.172), calls=%async_computation.8 | async-start | bytes 1572864 | tf_op jit(solution)/shard_map/all_to_all | solution.py:38
  576.6 19.7 %all-to-all-done.5 = bf16[16,16,1536]{2,1,0:T(8,128)(2,1)} async-done(((bf16[16,16,1536]{2,1,0:T(8,128)(2,1)}), bf16[16,16,1536]{2,1,0:T(8,128)(2,1)}, u32[]{:S(2)}, u32[]{:S(2)}) %all-to-all-start.5) | async-done | bytes 786464 | tf_op jit(solution)/shard_map/all_to_all | solution.py:38
  596.3 3.5 all-to-all-start.4
  601.1 4.8 all-to-all-done.4
  607.5 6.5 all-to-all-start.6
  614.1 3.7 fusion
  617.9 3.4 fusion.11
  621.8 4.0 fusion.10
  625.9 2.3 copy-done.3
  629.6 5.0 spill.1
  638.3 4.4 all-to-all-done.6.last_ref
  645.5 2.1 finish.1
  (369 shorter events, 114.5 us)
Async XLA Ops:
  7.2 69.5 %all-gather.6.cloned.1.call-start = ((), (), s32[]{:S(2)}) async-start(), calls=%async_computation.10 | async-start | bytes 6684672 | tf_op jit(solution)/shard_map/all_gather | solution.py:745
  17.4 48.0 %all-to-all-start = ((bf16[16,240,256]{2,1,0:T(8,128)(2,1)}), bf16[16,240,256]{2,1,0:T(8,128)(2,1)}, u32[]{:S(2)}, u32[]{:S(2)}) async-start(bf16[16,240,256]{2,1,0:T(8,128)(2,1)} %broadcast_dynamic-update-slice_fusion), calls=%async_computation | async-start | bytes 3932160 | tf_op jit(solution)/shard_map/all_to_all | solution.py:38
  24.0 101.6 %all-gather.8.cloned.1.call-start = ((), (), s32[]{:S(2)}) async-start(), calls=%async_computation.11 | async-start | bytes 2228224 | tf_op jit(solution)/shard_map/all_gather | solution.py:815
  24.0 3.9 collective-permute-start
  26.8 53.9 %copy-start.65 = (f32[128]{0:T(128)}, f32[128]{0:T(128)S(1)}, u32[]{:S(2)}) copy-start(f32[128]{0:T(128)S(1)} %get-tuple-element.144) | copy-start | bytes 1540
  27.9 342.0 %copy-start.10 = (f32[512,128]{1,0:T(8,128)}, f32[512,128]{1,0:T(8,128)S(1)}, u32[]{:S(2)}) copy-start(f32[512,128]{1,0:T(8,128)S(1)} %get-tuple-element.142.cos_ref) | copy-start | bytes 786436
  27.9 52.8 %copy-start.24 = (bf16[256,2048]{1,0:T(8,128)(2,1)}, bf16[256,2048]{1,0:T(8,128)(2,1)S(1)}, u32[]{:S(2)}) copy-start(bf16[256,2048]{1,0:T(8,128)(2,1)S(1)} %collective-permute-done.sib_ref.proj_c) | copy-start | bytes 3145732
  81.6 176.4 %all-gather.12.cloned.1.call-start = ((), (), s32[]{:S(2)}) async-start(), calls=%async_computation.13 | async-start | bytes 4718592 | tf_op jit(solution)/shard_map/all_gather | solution.py:828
  83.9 19.8 %collective-permute-start.6 = (bf16[1024,512]{1,0:T(8,128)(2,1)}, bf16[1024,512]{1,0:T(8,128)(2,1)}, u32[]{:S(2)}, u32[]{:S(2)}) collective-permute-start(bf16[1024,512]{1,0:T(8,128)(2,1)} %pad_maximum_fusion.3), channel_id=1, source_target_pairs={{0,1},{1,0},{2,3},{3,2},{4,5},{5,4},{6,7},{7,6},{8,9},{9,8},{10,11... | collective-permute-start | bytes 3145736 | tf_op jit(solution)/shard_map/ppermute | solution.py:21
  86.3 35.4 %collective-permute-start.3 = (bf16[256,2048]{1,0:T(8,128)(2,1)}, bf16[256,2048]{1,0:T(8,128)(2,1)S(1)}, u32[]{:S(2)}, u32[]{:S(2)}) collective-permute-start(bf16[256,2048]{1,0:T(8,128)(2,1)} %broadcast_add_fusion.2), channel_id=1, source_target_pairs={{0,8},{8,0},{1,9},{9,1},{2,10},{10,2},{3,11},{11,3},{4,12},{12,4},... | collective-permute-start | bytes 3145736 | tf_op jit(solution)/shard_map/out_chip/ppermute | solution.py:21
  90.5 11.8 %collective-permute-start.1 = (bf16[128,1024]{1,0:T(8,128)(2,1)S(1)}, bf16[128,1024]{1,0:T(8,128)(2,1)S(1)}, u32[]{:S(2)}, u32[]{:S(2)}) collective-permute-start(bf16[128,1024]{1,0:T(8,128)(2,1)S(1)} %multiply_convert_fusion.1.lane_a), channel_id=1, source_target_pairs={{0,6},{2,0},{4,2},{6,4},{1,7},{3,1},{5,3},{7,5},{8,14},{10,8},{12,... | collective-permute-start | bytes 786440 | tf_op jit(solution)/shard_map/lane/ppermute | solution.py:21
  92.2 13.0 %collective-permute-start.4 = (bf16[128,1024]{1,0:T(8,128)(2,1)S(1)}, bf16[128,1024]{1,0:T(8,128)(2,1)S(1)}, u32[]{:S(2)}, u32[]{:S(2)}) collective-permute-start(bf16[128,1024]{1,0:T(8,128)(2,1)S(1)} %multiply_convert_fusion.1.lane_a), channel_id=1, source_target_pairs={{0,2},{2,4},{4,6},{6,0},{1,3},{3,5},{5,7},{7,1},{8,10},{10,12},{12... | collective-permute-start | bytes 786440 | tf_op jit(solution)/shard_map/lane/ppermute | solution.py:21
  102.3 20.6 %collective-permute-start.2 = (bf16[64,1024]{1,0:T(8,128)(2,1)S(1)}, bf16[64,1024]{1,0:T(8,128)(2,1)S(1)}, u32[]{:S(2)}, u32[]{:S(2)}) collective-permute-start(bf16[64,1024]{1,0:T(8,128)(2,1)S(1)} %slice.314), channel_id=1, source_target_pairs={{0,6},{2,0},{4,2},{6,4},{1,7},{3,1},{5,3},{7,5},{8,14},{10,8},{12,... | collective-permute-start | bytes 393224 | tf_op jit(solution)/shard_map/lane/ppermute | solution.py:21
  105.2 17.8 %collective-permute-start.5 = (bf16[64,1024]{1,0:T(8,128)(2,1)S(1)}, bf16[64,1024]{1,0:T(8,128)(2,1)S(1)}, u32[]{:S(2)}, u32[]{:S(2)}) collective-permute-start(bf16[64,1024]{1,0:T(8,128)(2,1)S(1)} %slice.317), channel_id=1, source_target_pairs={{0,2},{2,4},{4,6},{6,0},{1,3},{3,5},{5,7},{7,1},{8,10},{10,12},{12... | collective-permute-start | bytes 393224 | tf_op jit(solution)/shard_map/lane/ppermute | solution.py:21
  129.3 133.4 %all-gather.10.cloned.1.call-start = ((), (), s32[]{:S(2)}) async-start(), calls=%async_computation.12 | async-start | bytes 4718592 | tf_op jit(solution)/shard_map/all_gather | solution.py:836
  130.4 10.4 %collective-permute-start.7 = (bf16[256,2048]{1,0:T(8,128)(2,1)S(1)}, bf16[256,2048]{1,0:T(8,128)(2,1)S(1)}, u32[]{:S(2)}, u32[]{:S(2)}) collective-permute-start(bf16[256,2048]{1,0:T(8,128)(2,1)S(1)} %broadcast_add_fusion.1), channel_id=1, source_target_pairs={{0,1},{1,0},{2,3},{3,2},{4,5},{5,4},{6,7},{7,6},{8,9},{9,8},{10,11... | collective-permute-start | bytes 3145736 | tf_op jit(solution)/shard_map/out_chip/ppermute | solution.py:21
  143.7 43.8 %copy-start.2 = (bf16[4,128,2048]{2,1,0:T(8,128)(2,1)}, bf16[4,128,2048]{2,1,0:T(8,128)(2,1)S(1)}, u32[]{:S(2)}) copy-start(bf16[4,128,2048]{2,1,0:T(8,128)(2,1)S(1)} %project.1.part_ref) | copy-start | bytes 6291460
  143.8 43.8 %collective-permute-start.8 = (bf16[64,2048]{1,0:T(8,128)(2,1)S(1)}, bf16[64,2048]{1,0:T(8,128)(2,1)}, u32[]{:S(2)}, u32[]{:S(2)}) collective-permute-start(bf16[64,2048]{1,0:T(8,128)(2,1)S(1)} %get-tuple-element.124), channel_id=1, source_target_pairs={{0,2},{2,4},{4,6},{6,0},{1,3},{3,5},{5,7},{7,1},{8,10},{10,12},{12... | collective-permute-start | bytes 786440 | tf_op jit(solution)/shard_map/residual/ppermute | solution.py:21
  143.9 43.7 %collective-permute-start.9 = (bf16[64,2048]{1,0:T(8,128)(2,1)S(1)}, bf16[64,2048]{1,0:T(8,128)(2,1)}, u32[]{:S(2)}, u32[]{:S(2)}) collective-permute-start(bf16[64,2048]{1,0:T(8,128)(2,1)S(1)} %get-tuple-element.123), channel_id=1, source_target_pairs={{0,6},{2,0},{4,2},{6,4},{1,7},{3,1},{5,3},{7,5},{8,14},{10,8},{12,... | collective-permute-start | bytes 786440 | tf_op jit(solution)/shard_map/residual/ppermute | solution.py:21
  190.0 15.3 %collective-permute-start.10 = (bf16[128,2048]{1,0:T(8,128)(2,1)}, bf16[128,2048]{1,0:T(8,128)(2,1)S(1)}, u32[]{:S(2)}, u32[]{:S(2)}) collective-permute-start(bf16[128,2048]{1,0:T(8,128)(2,1)} %get-tuple-element.84), channel_id=1, source_target_pairs={{0,2},{2,4},{4,6},{6,0},{1,3},{3,5},{5,7},{7,1},{8,10},{10,12},{12... | collective-permute-start | bytes 1572872 | tf_op jit(solution)/shard_map/residual/ppermute | solution.py:21
  190.0 15.3 %collective-permute-start.11 = (bf16[128,2048]{1,0:T(8,128)(2,1)}, bf16[128,2048]{1,0:T(8,128)(2,1)S(1)}, u32[]{:S(2)}, u32[]{:S(2)}) collective-permute-start(bf16[128,2048]{1,0:T(8,128)(2,1)} %get-tuple-element.85), channel_id=1, source_target_pairs={{0,6},{2,0},{4,2},{6,4},{1,7},{3,1},{5,3},{7,5},{8,14},{10,8},{12,... | collective-permute-start | bytes 1572872 | tf_op jit(solution)/shard_map/residual/ppermute | solution.py:21
  209.0 131.4 %reduce-scatter.4.cloned.1.call-start = ((), (), s32[]{:S(2)}) async-start(), calls=%async_computation.14 | async-start | bytes 4718592 | tf_op jit(solution)/shard_map/reduce_scatter | solution.py:852
  212.1 19.0 %collective-permute-start.12 = (bf16[1536,256]{1,0:T(8,128)(2,1)S(1)}, bf16[1536,256]{1,0:T(8,128)(2,1)S(1)}, u32[]{:S(2)}, u32[]{:S(2)}) collective-permute-start(bf16[1536,256]{1,0:T(8,128)(2,1)S(1)} %bitcast.169), channel_id=1, source_target_pairs={{0,48},{16,0},{32,16},{48,32},{1,49},{17,1},{33,17},{49,33},{2,50}... | collective-permute-start | bytes 2359304 | tf_op jit(solution)/shard_map/feed_weights/ppermute | solution.py:21
  214.8 20.0 %collective-permute-start.14 = (bf16[1536,256]{1,0:T(8,128)(2,1)S(1)}, bf16[1536,256]{1,0:T(8,128)(2,1)}, u32[]{:S(2)}, u32[]{:S(2)}) collective-permute-start(bf16[1536,256]{1,0:T(8,128)(2,1)S(1)} %bitcast.170), channel_id=1, source_target_pairs={{0,16},{16,32},{32,48},{48,0},{1,17},{17,33},{33,49},{49,1},{2,18}... | collective-permute-start | bytes 2359304 | tf_op jit(solution)/shard_map/feed_weights/ppermute | solution.py:21
  231.1 10.7 %collective-permute-start.13 = (bf16[768,256]{1,0:T(8,128)(2,1)S(1)}, bf16[768,256]{1,0:T(8,128)(2,1)}, u32[]{:S(2)}, u32[]{:S(2)}) collective-permute-start(bf16[768,256]{1,0:T(8,128)(2,1)S(1)} %slice.332), channel_id=1, source_target_pairs={{0,48},{16,0},{32,16},{48,32},{1,49},{17,1},{33,17},{49,33},{2,50}... | collective-permute-start | bytes 1179656 | tf_op jit(solution)/shard_map/feed_weights/ppermute | solution.py:21
  235.9 10.4 %collective-permute-start.15 = (bf16[768,256]{1,0:T(8,128)(2,1)S(1)}, bf16[768,256]{1,0:T(8,128)(2,1)S(1)}, u32[]{:S(2)}, u32[]{:S(2)}) collective-permute-start(bf16[768,256]{1,0:T(8,128)(2,1)S(1)} %slice.333), channel_id=1, source_target_pairs={{0,16},{16,32},{32,48},{48,0},{1,17},{17,33},{33,49},{49,1},{2,18}... | collective-permute-start | bytes 1179656 | tf_op jit(solution)/shard_map/feed_weights/ppermute | solution.py:21
  247.6 10.3 %collective-permute-start.16 = (bf16[3,2048,256]{2,1,0:T(8,128)(2,1)S(1)}, bf16[3,2048,256]{2,1,0:T(8,128)(2,1)}, u32[]{:S(2)}, u32[]{:S(2)}) collective-permute-start(bf16[3,2048,256]{2,1,0:T(8,128)(2,1)S(1)} %bitcast.173), channel_id=1, source_target_pairs={{0,1},{1,0},{2,3},{3,2},{4,5},{5,4},{6,7},{7,6},{8,9},{9,8},{10,11... | collective-permute-start | bytes 9437192 | tf_op jit(solution)/shard_map/feed_weights/ppermute | solution.py:21
  249.3 6.3 collective-permute-start.17
  288.3 108.0 %reduce-scatter.6.cloned.1.call-start = ((), (), s32[]{:S(2)}) async-start(), calls=%async_computation.15 | async-start | bytes 5898240 | tf_op jit(solution)/shard_map/feed_grad/reduce_scatter | solution.py:862
  294.7 9.4 %collective-permute-start.18 = (bf16[2048,768]{1,0:T(8,128)(2,1)S(1)}, bf16[2048,768]{1,0:T(8,128)(2,1)S(1)}, u32[]{:S(2)}, u32[]{:S(2)}) collective-permute-start(bf16[2048,768]{1,0:T(8,128)(2,1)S(1)} %convolution_convert_fusion.1), channel_id=1, source_target_pairs={{0,1},{1,0},{2,3},{3,2},{4,5},{5,4},{6,7},{7,6},{8,9},{9,8},{10,11... | collective-permute-start | bytes 9437192 | tf_op jit(solution)/shard_map/feed_grad/ppermute | solution.py:21
  297.2 6.9 %collective-permute-start.19 = (bf16[2048,384]{1,0:T(8,128)(2,1)S(1)}, bf16[2048,384]{1,0:T(8,128)(2,1)S(1)}, u32[]{:S(2)}, u32[]{:S(2)}) collective-permute-start(bf16[2048,384]{1,0:T(8,128)(2,1)S(1)} %convolution_convert_fusion.3), channel_id=1, source_target_pairs={{0,1},{1,0},{2,3},{3,2},{4,5},{5,4},{6,7},{7,6},{8,9},{9,8},{10,11... | collective-permute-start | bytes 4718600 | tf_op jit(solution)/shard_map/feed_grad/ppermute | solution.py:21
  307.9 34.2 %copy-start.42 = (bf16[128,2048]{1,0:T(8,128)(2,1)S(1)}, bf16[128,2048]{1,0:T(8,128)(2,1)}, u32[]{:S(2)}) copy-start(bf16[128,2048]{1,0:T(8,128)(2,1)} %param.33) | copy-start | bytes 1572868
  343.6 13.8 %collective-permute-start.20 = (bf16[128,2048]{1,0:T(8,128)(2,1)S(1)}, bf16[128,2048]{1,0:T(8,128)(2,1)S(1)}, u32[]{:S(2)}, u32[]{:S(2)}) collective-permute-start(bf16[128,2048]{1,0:T(8,128)(2,1)S(1)} %fusion.34.branch_a), channel_id=1, source_target_pairs={{0,6},{2,0},{4,2},{6,4},{1,7},{3,1},{5,3},{7,5},{8,14},{10,8},{12,... | collective-permute-start | bytes 1572872 | tf_op jit(solution)/shard_map/branch/ppermute | solution.py:21
  344.1 14.9 %collective-permute-start.23 = (bf16[128,2048]{1,0:T(8,128)(2,1)S(1)}, bf16[128,2048]{1,0:T(8,128)(2,1)S(1)}, u32[]{:S(2)}, u32[]{:S(2)}) collective-permute-start(bf16[128,2048]{1,0:T(8,128)(2,1)S(1)} %fusion.34.branch_a), channel_id=1, source_target_pairs={{0,2},{2,4},{4,6},{6,0},{1,3},{3,5},{5,7},{7,1},{8,10},{10,12},{12... | collective-permute-start | bytes 1572872 | tf_op jit(solution)/shard_map/branch/ppermute | solution.py:21
  357.4 7.4 %collective-permute-start.21 = (bf16[64,2048]{1,0:T(8,128)(2,1)S(1)}, bf16[64,2048]{1,0:T(8,128)(2,1)S(1)}, u32[]{:S(2)}, u32[]{:S(2)}) collective-permute-start(bf16[64,2048]{1,0:T(8,128)(2,1)S(1)} %slice.336), channel_id=1, source_target_pairs={{0,6},{2,0},{4,2},{6,4},{1,7},{3,1},{5,3},{7,5},{8,14},{10,8},{12,... | collective-permute-start | bytes 786440 | tf_op jit(solution)/shard_map/branch/ppermute | solution.py:21
  359.0 10.9 %collective-permute-start.24 = (bf16[64,2048]{1,0:T(8,128)(2,1)S(1)}, bf16[64,2048]{1,0:T(8,128)(2,1)S(1)}, u32[]{:S(2)}, u32[]{:S(2)}) collective-permute-start(bf16[64,2048]{1,0:T(8,128)(2,1)S(1)} %slice.339), channel_id=1, source_target_pairs={{0,2},{2,4},{4,6},{6,0},{1,3},{3,5},{5,7},{7,1},{8,10},{10,12},{12... | collective-permute-start | bytes 786440 | tf_op jit(solution)/shard_map/branch/ppermute | solution.py:21
  369.2 73.0 %collective-permute-start.22 = (bf16[512,2048]{1,0:T(8,128)(2,1)}, bf16[512,2048]{1,0:T(8,128)(2,1)}, u32[]{:S(2)}, u32[]{:S(2)}) collective-permute-start(bf16[512,2048]{1,0:T(8,128)(2,1)} %add_bitcast_fusion), channel_id=1, source_target_pairs={{0,8},{8,0},{1,9},{9,1},{2,10},{10,2},{3,11},{11,3},{4,12},{12,4},... | collective-permute-start | bytes 6291464 | tf_op jit(solution)/shard_map/layer_out/ppermute | solution.py:21
  395.7 31.8 %copy-start.4 = (bf16[4,128,1024]{2,1,0:T(8,128)(2,1)}, bf16[4,128,1024]{2,1,0:T(8,128)(2,1)S(1)}, u32[]{:S(2)}) copy-start(bf16[4,128,1024]{2,1,0:T(8,128)(2,1)S(1)} %get-tuple-element.91.part_ref) | copy-start | bytes 3145732
  395.7 50.7 %collective-permute-start.29 = (bf16[512,2048]{1,0:T(8,128)(2,1)}, bf16[512,2048]{1,0:T(8,128)(2,1)}, u32[]{:S(2)}, u32[]{:S(2)}) collective-permute-start(bf16[512,2048]{1,0:T(8,128)(2,1)} %get-tuple-element.95), channel_id=1, source_target_pairs={{0,1},{1,0},{2,3},{3,2},{4,5},{5,4},{6,7},{7,6},{8,9},{9,8},{10,11... | collective-permute-start | bytes 6291464 | tf_op jit(solution)/shard_map/heads_grad/ppermute | solution.py:21
  395.8 50.6 %collective-permute-start.30 = (bf16[1024,512]{1,0:T(8,128)(2,1)}, bf16[1024,512]{1,0:T(8,128)(2,1)}, u32[]{:S(2)}, u32[]{:S(2)}) collective-permute-start(bf16[1024,512]{1,0:T(8,128)(2,1)} %get-tuple-element.97), channel_id=1, source_target_pairs={{0,1},{1,0},{2,3},{3,2},{4,5},{5,4},{6,7},{7,6},{8,9},{9,8},{10,11... | collective-permute-start | bytes 3145736 | tf_op jit(solution)/shard_map/heads_grad/ppermute | solution.py:21
  398.3 46.3 %all-to-all-start.1 = ((bf16[16,32,768]{2,1,0:T(8,128)(2,1)}), bf16[16,32,768]{2,1,0:T(8,128)(2,1)}, u32[]{:S(2)}, u32[]{:S(2)}) async-start(bf16[16,32,768]{2,1,0:T(8,128)(2,1)} %slice.341), calls=%async_computation.3 | async-start | bytes 1572864 | tf_op jit(solution)/shard_map/feed_grad/all_to_all | solution.py:38
  411.9 34.5 %copy-start.7 = (bf16[512,2048]{1,0:T(8,128)(2,1)S(1)}, bf16[512,2048]{1,0:T(8,128)(2,1)}, u32[]{:S(2)}) copy-start(bf16[512,2048]{1,0:T(8,128)(2,1)} %get-tuple-element.94.out_ref) | copy-start | bytes 6291460
  412.0 15.5 %collective-permute-start.25 = (bf16[64,1024]{1,0:T(8,128)(2,1)S(1)}, bf16[64,1024]{1,0:T(8,128)(2,1)S(1)}, u32[]{:S(2)}, u32[]{:S(2)}) collective-permute-start(bf16[64,1024]{1,0:T(8,128)(2,1)S(1)} %get-tuple-element.134), channel_id=1, source_target_pairs={{0,2},{2,4},{4,6},{6,0},{1,3},{3,5},{5,7},{7,1},{8,10},{10,12},{12... | collective-permute-start | bytes 393224 | tf_op jit(solution)/shard_map/latent_grad/ppermute | solution.py:21
  413.9 13.6 %collective-permute-start.26 = (bf16[64,1024]{1,0:T(8,128)(2,1)S(1)}, bf16[64,1024]{1,0:T(8,128)(2,1)}, u32[]{:S(2)}, u32[]{:S(2)}) collective-permute-start(bf16[64,1024]{1,0:T(8,128)(2,1)S(1)} %get-tuple-element.133), channel_id=1, source_target_pairs={{0,6},{2,0},{4,2},{6,4},{1,7},{3,1},{5,3},{7,5},{8,14},{10,8},{12,... | collective-permute-start | bytes 393224 | tf_op jit(solution)/shard_map/latent_grad/ppermute | solution.py:21
  430.1 9.4 %collective-permute-start.27 = (bf16[128,1024]{1,0:T(8,128)(2,1)}, bf16[128,1024]{1,0:T(8,128)(2,1)S(1)}, u32[]{:S(2)}, u32[]{:S(2)}) collective-permute-start(bf16[128,1024]{1,0:T(8,128)(2,1)} %get-tuple-element.92), channel_id=1, source_target_pairs={{0,2},{2,4},{4,6},{6,0},{1,3},{3,5},{5,7},{7,1},{8,10},{10,12},{12... | collective-permute-start | bytes 786440 | tf_op jit(solution)/shard_map/latent_grad/ppermute | solution.py:21
  430.1 9.4 %collective-permute-start.28 = (bf16[128,1024]{1,0:T(8,128)(2,1)}, bf16[128,1024]{1,0:T(8,128)(2,1)S(1)}, u32[]{:S(2)}, u32[]{:S(2)}) collective-permute-start(bf16[128,1024]{1,0:T(8,128)(2,1)} %get-tuple-element.93), channel_id=1, source_target_pairs={{0,6},{2,0},{4,2},{6,4},{1,7},{3,1},{5,3},{7,5},{8,14},{10,8},{12,... | collective-permute-start | bytes 786440 | tf_op jit(solution)/shard_map/latent_grad/ppermute | solution.py:21
  450.8 48.2 %all-to-all-start.2 = ((bf16[16,48,2048]{2,1,0:T(8,128)(2,1)}), bf16[16,48,2048]{2,1,0:T(8,128)(2,1)S(1)}, u32[]{:S(2)}, u32[]{:S(2)}) async-start(bf16[16,48,2048]{2,1,0:T(8,128)(2,1)} %pack_heads.1), calls=%async_computation.5 | async-start | bytes 6291456 | tf_op jit(solution)/shard_map/heads_grad/all_to_all | solution.py:38
  456.6 165.2 %reduce-scatter.8.cloned.1.call-start = ((), (), s32[]{:S(2)}) async-start(), calls=%async_computation.16 | async-start | bytes 2621440 | tf_op jit(solution)/shard_map/layer_out/reduce_scatter | solution.py:931
  463.0 162.8 %all-gather.14.cloned.1.call-start = ((), (), s32[]{:S(2)}) async-start(), calls=%async_computation.17 | async-start | bytes 5898240 | tf_op jit(solution)/shard_map/feed_grad/all_gather | solution.py:926
  463.1 37.1 %collective-permute-start.31 = (bf16[8,128,512]{2,1,0:T(8,128)(2,1)}, bf16[8,128,512]{2,1,0:T(8,128)(2,1)}, u32[]{:S(2)}, u32[]{:S(2)}) collective-permute-start(bf16[8,128,512]{2,1,0:T(8,128)(2,1)} %get-tuple-element.99), channel_id=1, source_target_pairs={{0,1},{1,0},{2,3},{3,2},{4,5},{5,4},{6,7},{7,6},{8,9},{9,8},{10,11... | collective-permute-start | bytes 3145736 | tf_op jit(solution)/shard_map/kv_grad/ppermute | solution.py:21
  466.6 67.2 %collective-permute-start.40 = (bf16[16,32,1152]{2,1,0:T(8,128)(2,1)}, bf16[16,32,1152]{2,1,0:T(8,128)(2,1)}, u32[]{:S(2)}, u32[]{:S(2)}) collective-permute-start(bf16[16,32,1152]{2,1,0:T(8,128)(2,1)} %pad_maximum_fusion.2), channel_id=1, source_target_pairs={{0,64},{64,0},{1,65},{65,1},{2,66},{66,2},{3,67},{67,3},{4,68},{68... | collective-permute-start | bytes 3538952 | tf_op jit(solution)/shard_map/feed_grad/ppermute | solution.py:21
  499.0 33.4 %copy-start.37 = (bf16[16,48,2048]{2,1,0:T(8,128)(2,1)}, bf16[16,48,2048]{2,1,0:T(8,128)(2,1)S(1)}, u32[]{:S(2)}) copy-start(bf16[16,48,2048]{2,1,0:T(8,128)(2,1)S(1)} %all-to-all-done.2) | copy-start | bytes 9437188
  502.1 31.7 %copy-start.48 = (bf16[16,32,384]{2,1,0:T(8,128)(2,1)S(1)}, bf16[16,32,384]{2,1,0:T(8,128)(2,1)}, u32[]{:S(2)}) copy-start(bf16[16,32,384]{2,1,0:T(8,128)(2,1)} %copy-done.47) | copy-start | bytes 1179652
  538.8 9.3 %collective-permute-start.35 = (bf16[128,1536]{1,0:T(8,128)(2,1)S(1)}, bf16[128,1536]{1,0:T(8,128)(2,1)S(1)}, u32[]{:S(2)}, u32[]{:S(2)}) collective-permute-start(bf16[128,1536]{1,0:T(8,128)(2,1)S(1)} %pad_maximum_fusion.5.g_a), channel_id=1, source_target_pairs={{0,6},{2,0},{4,2},{6,4},{1,7},{3,1},{5,3},{7,5},{8,14},{10,8},{12,... | collective-permute-start | bytes 1179656 | tf_op jit(solution)/shard_map/first_lane/ppermute | solution.py:21
  539.7 9.9 %collective-permute-start.37 = (bf16[128,1536]{1,0:T(8,128)(2,1)S(1)}, bf16[128,1536]{1,0:T(8,128)(2,1)S(1)}, u32[]{:S(2)}, u32[]{:S(2)}) collective-permute-start(bf16[128,1536]{1,0:T(8,128)(2,1)S(1)} %pad_maximum_fusion.5.g_a), channel_id=1, source_target_pairs={{0,2},{2,4},{4,6},{6,0},{1,3},{3,5},{5,7},{7,1},{8,10},{10,12},{12... | collective-permute-start | bytes 1179656 | tf_op jit(solution)/shard_map/first_lane/ppermute | solution.py:21
  548.0 14.5 %collective-permute-start.36 = (bf16[64,1536]{1,0:T(8,128)(2,1)S(1)}, bf16[64,1536]{1,0:T(8,128)(2,1)S(1)}, u32[]{:S(2)}, u32[]{:S(2)}) collective-permute-start(bf16[64,1536]{1,0:T(8,128)(2,1)S(1)} %slice.353), channel_id=1, source_target_pairs={{0,6},{2,0},{4,2},{6,4},{1,7},{3,1},{5,3},{7,5},{8,14},{10,8},{12,... | collective-permute-start | bytes 589832 | tf_op jit(solution)/shard_map/first_lane/ppermute | solution.py:21
  549.7 12.8 %collective-permute-start.38 = (bf16[64,1536]{1,0:T(8,128)(2,1)S(1)}, bf16[64,1536]{1,0:T(8,128)(2,1)S(1)}, u32[]{:S(2)}, u32[]{:S(2)}) collective-permute-start(bf16[64,1536]{1,0:T(8,128)(2,1)S(1)} %slice.354), channel_id=1, source_target_pairs={{0,2},{2,4},{4,6},{6,0},{1,3},{3,5},{5,7},{7,1},{8,10},{10,12},{12... | collective-permute-start | bytes 589832 | tf_op jit(solution)/shard_map/first_lane/ppermute | solution.py:21
  552.8 6.8 %collective-permute-start.32 = (bf16[128,512]{1,0:T(8,128)(2,1)}, bf16[128,512]{1,0:T(8,128)(2,1)S(1)}, u32[]{:S(2)}, u32[]{:S(2)}) collective-permute-start(bf16[128,512]{1,0:T(8,128)(2,1)} %get-tuple-element.101), channel_id=1, source_target_pairs={{0,4},{2,6},{4,0},{6,2},{1,5},{3,7},{5,1},{7,3},{8,12},{10,14},{12... | collective-permute-start | bytes 393224 | tf_op jit(solution)/shard_map/columns/ppermute | solution.py:21
  553.8 7.1 %collective-permute-start.33 = (bf16[128,512]{1,0:T(8,128)(2,1)}, bf16[128,512]{1,0:T(8,128)(2,1)S(1)}, u32[]{:S(2)}, u32[]{:S(2)}) collective-permute-start(bf16[128,512]{1,0:T(8,128)(2,1)} %get-tuple-element.102), channel_id=1, source_target_pairs={{0,6},{2,0},{4,2},{6,4},{1,7},{3,1},{5,3},{7,5},{8,14},{10,8},{12,... | collective-permute-start | bytes 393224 | tf_op jit(solution)/shard_map/columns/ppermute | solution.py:21
  556.1 6.4 collective-permute-start.34
  564.4 2.4 collective-permute-start.39
  567.9 28.4 %all-to-all-start.5 = ((bf16[16,16,1536]{2,1,0:T(8,128)(2,1)}), bf16[16,16,1536]{2,1,0:T(8,128)(2,1)}, u32[]{:S(2)}, u32[]{:S(2)}) async-start(bf16[16,16,1536]{2,1,0:T(8,128)(2,1)} %bitcast.172), calls=%async_computation.8 | async-start | bytes 1572864 | tf_op jit(solution)/shard_map/all_to_all | solution.py:38
  596.3 9.6 %all-to-all-start.4 = ((bf16[16,8,256]{2,1,0:T(8,128)(2,1)}), bf16[16,8,256]{2,1,0:T(8,128)(2,1)S(1)}, u32[]{:S(2)}, u32[]{:S(2)}) async-start(bf16[16,8,256]{2,1,0:T(8,128)(2,1)} %bitcast.75), calls=%async_computation.7 | async-start | bytes 131072 | tf_op jit(solution)/shard_map/up_grad/all_to_all | solution.py:38
  607.5 35.2 %all-to-all-start.6 = ((bf16[8,64,2048]{2,1,0:T(8,128)(2,1)}), bf16[8,64,2048]{2,1,0:T(8,128)(2,1)S(1)}, u32[]{:S(2)}, u32[]{:S(2)}) async-start(bf16[8,64,2048]{2,1,0:T(8,128)(2,1)} %broadcast_in_dim.86), calls=%async_computation.9 | async-start | bytes 4194304 | tf_op jit(solution)/shard_map/all_to_all | solution.py:38
  (72 other events, 428.0 us)
Sparse Core Ops, SparseCore 0:
  10.3 66.3 all-gather.5
  81.7 38.3 all-gather.7
  129.4 61.2 all-gather.11
  209.1 53.5 all-gather.9
  288.4 51.9 reduce-scatter.3
  342.6 49.7 reduce-scatter.5
  463.2 31.6 reduce-scatter.7
  537.0 60.4 all-gather.13

commit v3 on v2

--- a/solution.py
+++ b/solution.py
@@ -13,7 +13,8 @@
 SIZES = (2, 4, 2, 4, 2)
 DP, SEQ, ACROSS = ("v", "x"), ("y", "z", "c"), ("v", "x", "y")
 SLOT = 384
-KEY_CHUNK = 512
+KEY_CHUNK = 1024
+BACK_CHUNK = 512
 
 
 def turn(value, axis, step):
@@ -145,11 +146,11 @@
     return jnp.where((key >= begin) & (key <= place), scores, -1e30)
 
 
-def chunk_bounds(meta, block, width):
+def chunk_bounds(meta, block, width, size):
     number = meta[6 + block]
-    count = ((number + 1) * width + KEY_CHUNK - 1) // KEY_CHUNK
-    clear_from = jnp.minimum((meta[2 + block] + KEY_CHUNK - 1) // KEY_CHUNK, count)
-    clear_to = jnp.maximum((number * width + 1) // KEY_CHUNK, clear_from)
+    count = ((number + 1) * width + size - 1) // size
+    clear_from = jnp.minimum((meta[2 + block] + size - 1) // size, count)
+    clear_to = jnp.maximum((number * width + 1) // size, clear_from)
     return clear_from, clear_to, count
 
 
@@ -157,11 +158,13 @@
     return jnp.concatenate([ref[...] for ref in refs], axis=0)
 
 
-def stack_heads(ref, block, first, head):
-    return jnp.concatenate(
-        [ref[block, :, first : first + head], ref[block, :, first + head : first + 2 * head]],
-        axis=0,
-    )
+def stack_heads(ref, block, head):
+    count = ref.shape[2] // head
+    return jnp.concatenate([ref[block, :, h * head : (h + 1) * head] for h in range(count)], axis=0)
+
+
+def wide_row(ref, block, heads):
+    return jnp.concatenate([ref[block]] * heads, axis=1)
 
 
 def query_kernel(lane_a, lane_b, lane_c, lane_d, lane_e, up_ref, cos_ref, sin_ref, q_ref):
@@ -183,48 +186,43 @@
 def attend_kernel(meta, q_ref, kv_ref, place_ref, begin_ref, out_ref, log_ref):
     blocks, width, size = q_ref.shape
     head = kv_ref.shape[1] // 2
-    pairs = range(size // head // 2)
+    heads = size // head
+    rows_all = heads * width
 
     @pl.loop(0, blocks)
     def per_block(block):
-        clear_from, clear_to, count = chunk_bounds(meta, block, width)
-        place, begin = place_ref[block], begin_ref[block]
-        queries = [stack_heads(q_ref, block, pair * 2 * head, head) for pair in pairs]
-
-        def chunk(step, carries, clear):
+        clear_from, clear_to, count = chunk_bounds(meta, block, width, KEY_CHUNK)
+        place, begin = wide_row(place_ref, block, heads), wide_row(begin_ref, block, heads)
+        query = stack_heads(q_ref, block, head)
+
+        def chunk(step, carry, clear):
+            top, total, mixed = carry
             start = pl.multiple_of(step * KEY_CHUNK, KEY_CHUNK)
-            key_chunk = kv_ref[pl.ds(start, KEY_CHUNK), :head]
-            value_chunk = kv_ref[pl.ds(start, KEY_CHUNK), head:]
-            result = []
-            for query, (top, total, mixed) in zip(queries, carries):
-                scores = dot_nt(key_chunk, query)
-                if not clear:
-                    scores = masked(scores, start, place, begin)
-                new_top = jnp.maximum(top, jnp.max(scores, axis=0, keepdims=True))
-                factor = jnp.exp(top - new_top)
-                weights = jnp.exp(scores - new_top)
-                total = total * factor + jnp.sum(weights, axis=0, keepdims=True)
-                mixed = mixed * factor + dot_tn(value_chunk, weights.astype(BF16))
-                result.append((new_top, total, mixed))
-            return tuple(result)
-
-        carry = tuple(
-            (
-                jnp.full((1, 2 * width), -1e30, F32),
-                jnp.zeros((1, 2 * width), F32),
-                jnp.zeros((head, 2 * width), F32),
+            scores = dot_nt(kv_ref[pl.ds(start, KEY_CHUNK), :head], query)
+            if not clear:
+                scores = masked(scores, start, place, begin)
+            new_top = jnp.maximum(top, jnp.max(scores, axis=0, keepdims=True))
+            factor = jnp.exp(top - new_top)
+            weights = jnp.exp(scores - new_top)
+            total = total * factor + jnp.sum(weights, axis=0, keepdims=True)
+            mixed = mixed * factor + dot_tn(
+                kv_ref[pl.ds(start, KEY_CHUNK), head:], weights.astype(BF16)
             )
-            for _ in pairs
+            return (new_top, total, mixed)
+
+        carry = (
+            jnp.full((1, rows_all), -1e30, F32),
+            jnp.zeros((1, rows_all), F32),
+            jnp.zeros((head, rows_all), F32),
         )
         carry = lax.fori_loop(0, clear_from, lambda s, w: chunk(s, w, False), carry)
         carry = lax.fori_loop(clear_from, clear_to, lambda s, w: chunk(s, w, True), carry)
         carry = lax.fori_loop(clear_to, count, lambda s, w: chunk(s, w, False), carry)
-        for pair, (top, total, mixed) in zip(pairs, carry):
-            first = pair * 2 * head
-            result = (mixed / total).T.astype(BF16)
-            out_ref[block, :, first : first + head] = result[:width]
-            out_ref[block, :, first + head : first + 2 * head] = result[width:]
-            log_ref[block, pair] = top + jnp.log(total)
+        top, total, mixed = carry
+        result = (mixed / total).T.astype(BF16)
+        for h in range(heads):
+            out_ref[block, :, h * head : (h + 1) * head] = result[h * width : (h + 1) * width]
+        log_ref[block] = top + jnp.log(total)
 
 
 def attend_back_kernel(
@@ -279,63 +277,51 @@
     key_grad[...] = jnp.zeros_like(key_grad)
     value_grad[...] = jnp.zeros_like(value_grad)
 
-    pairs = range(heads // 2)
 
     @pl.loop(0, blocks)
     def per_block(block):
-        clear_from, clear_to, count = chunk_bounds(meta, block, width)
-        place, begin = place_ref[block], begin_ref[block]
+        clear_from, clear_to, count = chunk_bounds(meta, block, width, BACK_CHUNK)
+        place, begin = wide_row(place_ref, block, heads), wide_row(begin_ref, block, heads)
         token = pl.ds(pl.multiple_of(block * width, width), width)
         cosine, sine = cos_ref[token, :], sin_ref[token, :]
-        fixed = []
-        for pair in pairs:
-            query, grad, out = (
-                stack_heads(ref, block, pair * 2 * head, head) for ref in (q_ref, grads, out_ref)
-            )
-            row_dot = jnp.sum((grad.astype(F32) * out.astype(F32)).T, axis=0, keepdims=True)
-            fixed.append((query, grad, row_dot, log_ref[block, pair]))
-
-        def chunk(step, accs, clear):
-            start = pl.multiple_of(step * KEY_CHUNK, KEY_CHUNK)
-            span = pl.ds(start, KEY_CHUNK)
-            key_chunk, value_chunk = kv_ref[span, :head], kv_ref[span, head:]
-            key_sum, value_sum = key_grad[span, :], value_grad[span, :]
-            result = []
-            for (query, grad, row_dot, log_total), acc in zip(fixed, accs):
-                scores = dot_nt(key_chunk, query)
-                if not clear:
-                    scores = masked(scores, start, place, begin)
-                probs = jnp.exp(scores - log_total)
-                grad_probs = dot_nt(value_chunk, grad)
-                grad_scores = (probs * (grad_probs - row_dot)).astype(BF16)
-                value_sum += dot(probs.astype(BF16), grad)
-                key_sum += dot(grad_scores, query)
-                result.append(acc + dot_tn(grad_scores, key_chunk))
-            key_grad[span, :] = key_sum
-            value_grad[span, :] = value_sum
-            return tuple(result)
-
-        accs = tuple(jnp.zeros((2 * width, head), F32) for _ in pairs)
-        accs = lax.fori_loop(0, clear_from, lambda s, w: chunk(s, w, False), accs)
-        accs = lax.fori_loop(clear_from, clear_to, lambda s, w: chunk(s, w, True), accs)
-        accs = lax.fori_loop(clear_to, count, lambda s, w: chunk(s, w, False), accs)
-        for pair, acc in zip(pairs, accs):
-            acc = acc * (head**-0.5)
-            for h in range(2):
-                value = acc[h * width : (h + 1) * width]
-                low, high = value[:, :half], value[:, half:]
-                start = (pair * 2 + h) * head
-                gq_ref[block, :, start : start + half] = (low * cosine + high * sine).astype(BF16)
-                gq_ref[block, :, start + half : start + head] = (
-                    high * cosine - low * sine
-                ).astype(BF16)
+        query, grad, out = (stack_heads(ref, block, head) for ref in (q_ref, grads, out_ref))
+        row_dot = jnp.sum((grad.astype(F32) * out.astype(F32)).T, axis=0, keepdims=True)
+        log_total = log_ref[block]
+
+        def chunk(step, acc, clear):
+            start = pl.multiple_of(step * BACK_CHUNK, BACK_CHUNK)
+            span = pl.ds(start, BACK_CHUNK)
+            key_chunk = kv_ref[span, :head]
+            scores = dot_nt(key_chunk, query)
+            if not clear:
+                scores = masked(scores, start, place, begin)
+            probs = jnp.exp(scores - log_total)
+            grad_probs = dot_nt(kv_ref[span, head:], grad)
+            grad_scores = (probs * (grad_probs - row_dot)).astype(BF16)
+            value_grad[span, :] += dot(probs.astype(BF16), grad)
+            key_grad[span, :] += dot(grad_scores, query)
+            return acc + dot_tn(grad_scores, key_chunk)
+
+        acc = jnp.zeros((heads * width, head), F32)
+        acc = lax.fori_loop(0, clear_from, lambda s, w: chunk(s, w, False), acc)
+        acc = lax.fori_loop(clear_from, clear_to, lambda s, w: chunk(s, w, True), acc)
+        acc = lax.fori_loop(clear_to, count, lambda s, w: chunk(s, w, False), acc)
+        acc = acc * (head**-0.5)
+        for h in range(heads):
+            value = acc[h * width : (h + 1) * width]
+            low, high = value[:, :half], value[:, half:]
+            start = h * head
+            gq_ref[block, :, start : start + half] = (low * cosine + high * sine).astype(BF16)
+            gq_ref[block, :, start + half : start + head] = (high * cosine - low * sine).astype(BF16)
 
     grad_query = gq_ref[...].reshape(blocks * width, heads * head)
     size = latent_ref.shape[2]
     piece = 256
     for start in range(0, size, piece):
         value = dot_nt(grad_query, up_ref[start : start + piece, :])
-        latent_ref[:, :, start : start + piece] = value.astype(BF16).reshape(blocks, width, piece)
+        for slot in range(blocks):
+            block = value[slot * width : (slot + 1) * width].astype(BF16)
+            latent_ref[(meta[6 + slot] // 2) % 4, :, start : start + piece] = block
     mixed = out_ref[...].reshape(blocks * width, heads * head)
     latent = stack_lane((lane_a, lane_b, lane_c, lane_d, lane_e))
     for h in range(heads):
@@ -429,7 +415,7 @@
         attend_kernel,
         out_shape=(
             shape(query.shape, BF16),
-            shape((blocks, size // head // 2, 1, 2 * width), F32),
+            shape((blocks, 1, size // head * width), F32),
         ),
         in_specs=kernel_specs(4),
         out_specs=tuple(kernel_specs(2)[1:]),
@@ -690,8 +676,8 @@
 
 
 def attend_back(meta, branch, kv, up, proj, cosine, sine, place, begin, query, out, log, lane):
-    blocks, _, rows_all = place.shape
-    width, head = rows_all // 2, kv.shape[1] // 2
+    blocks, _, width = place.shape
+    head = kv.shape[1] // 2
     shape = jax.ShapeDtypeStruct
     return pl.pallas_call(
         attend_back_kernel,
@@ -794,8 +780,8 @@
     cosine, sine = rope_tables((token_index - doc_start).reshape(-1), head)
     meta = jnp.concatenate([jnp.stack([y, c]), jnp.max(doc_start, axis=1), blocks])
     meta = meta.astype(jnp.int32)
-    place_row = jnp.tile(token_index, (1, 2))[:, None, :]
-    begin_row = jnp.tile(doc_start, (1, 2))[:, None, :]
+    place_row = token_index[:, None, :]
+    begin_row = doc_start[:, None, :]
     cos_own, sin_own = cosine[:width], sine[:width]
 
     tokens_float = tokens.astype(F32)
@@ -825,7 +811,7 @@
         out_across_sib = sibling(after(out_across, query_rot))
     attended, log_total = attend(meta, query_rot, kv, place_row, begin_row)
     out_pieces = (out_proj, out_across, out_sib, out_across_sib)
-    cot_all = lax.all_gather(after(after(cotangent, kv), query_rot), ("y", "z"), axis=0, tiled=True)
+    cot_all = lax.all_gather(after(cotangent, first), ("y", "z"), axis=0, tiled=True)
     attended_rows = attended.reshape(4 * width, 4 * head)
     mixed = project(meta, attended, out_pieces)
     with jax.named_scope("residual"):
@@ -871,7 +857,7 @@
         fed = fed.reshape(2, 4 * width, model)
         fed_own = lax.dynamic_index_in_dim(fed, y, 0, keepdims=False)
         fed_across = lax.dynamic_index_in_dim(fed, 1 - y, 0, keepdims=False)
-        fed_across = turn(after(fed_across, branch[1]), "y", 1)
+        fed_across = turn(after(fed_across, grad_residual), "y", 1)
     grad_queries, latent_parts, kv_own, kv_sib, out_grad, out_grad_sib, up_grad, up_sib = attend_back(
         meta,
         branch,
@@ -887,26 +873,36 @@
         log_total,
         lane,
     )
+    with jax.named_scope("kv_grad"):
+        kv_grad = kv_own.astype(F32) + sibling(kv_sib).astype(F32)
+        kv_grad = after(kv_grad, feed_part[0, 0] + fed_across[0, 0]).astype(BF16)
+        kv_sum = total_of(exchange(kv_grad, ("y", "z")))
     with jax.named_scope("feed_grad"):
+        feed_part = after(feed_part, grad_queries)
+        feed_across = turn(feed_part, "v", 1)
+        feed_part = (feed_part.astype(F32) + feed_across.astype(F32)).astype(BF16)
         feed_part = feed_part.reshape(16, quarter, 3 * SLOT)
-        swapped = exchange(feed_part[..., : 2 * SLOT], SEQ)
+        v_sum = feed_part
+        swapped = exchange(after(feed_part[..., : 2 * SLOT], kv_sum), SEQ)
+        feed_part = jnp.concatenate([swapped, feed_part[..., 2 * SLOT :]], axis=2)
+        feed_sum = lax.all_gather(
+            feed_part.reshape(16 * quarter, 3 * SLOT), "x", axis=0, tiled=True
+        )
     with jax.named_scope("latent_grad"):
-        grad_latent_n = ring_scatter(latent_parts)
+        latent_parts = latent_parts.reshape(4 * width, latent_width)
+        grad_latent_n = lax.psum_scatter(latent_parts, "z", scatter_dimension=0, tiled=True)
+        grad_latent_n = grad_latent_n.astype(F32)
     with jax.named_scope("heads_grad"):
         heads_parts = pack_heads(
-            ((fed_across[0, 0] + grad_latent_n[0, 0] + swapped[0, 0, 0]) * 0).astype(jnp.int32).reshape(1),
+            ((swapped[0, 0, 0] + grad_latent_n[0, 0]) * 0).astype(jnp.int32).reshape(1),
             out_grad,
             sibling(out_grad_sib),
             up_grad,
             sibling(up_sib),
         )
         heads_got = exchange(heads_parts, ACROSS)
-    with jax.named_scope("kv_grad"):
-        kv_grad = kv_own.astype(F32) + sibling(kv_sib).astype(F32)
-        kv_grad = after(kv_grad, heads_got).astype(BF16)
-        kv_sum = total_of(exchange(kv_grad, ("y", "z")))
     grad_keys = rotate_back(kv_sum[:, :head], cos_own, sin_own).astype(BF16)
-    grad_values = kv_sum[:, head:].astype(BF16)
+    grad_values = after(kv_sum[:, head:], v_sum).astype(BF16)
     grad_latent = rms_back(latent, inv_latent, gain_query, grad_latent_n)
     grad_latent = grad_latent.astype(BF16)
     grad_first = jnp.concatenate([grad_latent, grad_keys, grad_values], axis=1)
@@ -919,36 +915,29 @@
         )
     own_first, first_other = first_weights(columns, first_lane)
     own_first = own_first + sibling(first_other).astype(F32)
-    with jax.named_scope("feed_grad"):
-        feed_part = jnp.concatenate([swapped, feed_part[..., 2 * SLOT :]], axis=2)
-        feed_across = after(turn(feed_part, "v", 1), kv_sum)
-        feed_part = (feed_part.astype(F32) + feed_across.astype(F32)).astype(BF16)
-        feed_sum = lax.all_gather(
-            feed_part.reshape(16 * quarter, 3 * SLOT), "x", axis=0, tiled=True
-        )
-    with jax.named_scope("layer_out"):
-        fed = fed_own.astype(F32) + after(fed_across.astype(F32), heads_parts)
-        fed_part = lax.psum_scatter(fed.astype(BF16), "z", scatter_dimension=0, tiled=True)
-        layer_out = (residual + fed_part.astype(F32)).astype(BF16)
     with jax.named_scope("heads_grad"):
         heads_part = total_of(heads_got).astype(BF16)
         out_part, up_part = heads_part[: head // 8], heads_part[head // 8 :]
         up_part = up_part.reshape(16, 8, head).transpose(1, 0, 2)
-    with jax.named_scope("up_grad"):
-        up_part = exchange(after(up_part, kv_sum).reshape(16, depth // 8, head), SEQ)
-        up_part = up_part.reshape(2, 8, depth // 8, head).transpose(0, 2, 1, 3)
-        up_part = up_part.reshape(-1, model)
     grad_normed = dot_nt(grad_latent, weights[:, :latent_width])
     grad_normed = grad_normed + dot_nt(grad_first[:, latent_width:], weights[:, latent_width:])
     grad_one = rms_back(tokens_float, inv_one, gain_one, grad_normed)
     input_grad = grad_residual + grad_one
 
     share = width // 8
-    tail = own_first.reshape(2, 8, share, lane_width).transpose(1, 0, 2, 3)
+    tail = after(after(own_first, input_grad), heads_got).reshape(2, 8, share, lane_width).transpose(1, 0, 2, 3)
     tail = total_of(exchange(tail.reshape(16, share, lane_width).astype(BF16), ACROSS))
-    first_part = jnp.pad(tail.astype(BF16), ((0, 0), (0, model - lane_width)))
-    last_sum = spread(jnp.concatenate([out_part, up_part, first_part], axis=0), DP)
-
+    with jax.named_scope("up_grad"):
+        up_part = exchange(after(up_part, tail).reshape(16, depth // 8, head), SEQ)
+        up_part = up_part.reshape(2, 8, depth // 8, head).transpose(0, 2, 1, 3)
+        up_part = up_part.reshape(-1, model)
+    with jax.named_scope("layer_out"):
+        fed = fed_own.astype(F32) + after(fed_across.astype(F32), up_part)
+        fed_part = lax.psum_scatter(fed.astype(BF16), "z", scatter_dimension=0, tiled=True)
+        layer_out = (residual + fed_part.astype(F32)).astype(BF16)
+    with jax.named_scope("heads_sum"):
+        first_part = jnp.pad(tail.astype(BF16), ((0, 0), (0, model - lane_width)))
+        last_sum = spread(jnp.concatenate([out_part, up_part, first_part], axis=0), DP)
     gate_sum, lift_sum, down_sum, second_gain_sum = spill(
         feed_sum.reshape(4, 16, quarter, 3 * SLOT), gate_proj, up_proj, hidden_width
     )

time: 668 us -> 662 us (level)
  blocking collectives: 30.3 us -> 0 us
  waiting for transfers between devices: 285 us -> 312 us
  local copies, waits for them, and re-layouts: 53.3 us -> 66.7 us
  starting transfers between devices: 88.6 us -> 76.8 us
    all_to_all x6 -> x7, waiting for transfers between devices: 94.1 us -> 147 us  [exchange(): return lax.all_to_all(parts, axes, 0, 0)]
    all_to_all x1 -> x0, blocking collectives: 30.3 us -> none  [exchange(): return lax.all_to_all(parts, axes, 0, 0)]
    ppermute x41 -> x37, waiting for transfers between devices: 159 us -> 136 us  [turn(): lax.ppermute(value, axis, [(i, (i + step) % size) for i in range(size)])]
    all_to_all x6 -> x7, starting transfers between devices: 43.2 us -> 35.6 us  [exchange(): return lax.all_to_all(parts, axes, 0, 0)]
    ppermute x41 -> x37, starting transfers between devices: 45 us -> 40.9 us  [turn(): lax.ppermute(value, axis, [(i, (i + step) % size) for i in range(size)])]
    slice x14 -> x18, local copies, waits for them, and re-layouts: 10.8 us -> 14.2 us  [after(): first = other[(0,) * other.ndim] if other.ndim else other]
  transfers between devices with their start and end apart: 55 -> 53, of which waited for: 25 -> 26; matrix products, arithmetic and copies ran while one was open for 17% -> 19% of each run, Pallas kernels for 8% -> 8%
where the time goes in v3:
time: 662 us; the launch traced here: 651 us
  waiting for transfers between devices  312 us (47%)
  Pallas kernels  78.5 us (12%)
  starting transfers between devices  76.8 us (12%)
  local copies, waits for them, and re-layouts  66.7 us (10%)
  other arithmetic  55.4 us (8%)
  matrix products  30.8 us (5%)
  between operations  30.3 us (5%)
    all_to_all x7, waiting for transfers between devices, exchange(): return lax.all_to_all(parts, axes, 0, 0)  147 us
    ppermute x37, waiting for transfers between devices, turn(): lax.ppermute(value, axis, [(i, (i + step) % size) for i in range(size)])  136 us
    ppermute x37, starting transfers between devices, turn(): lax.ppermute(value, axis, [(i, (i + step) % size) for i in range(size)])  40.9 us
    all_to_all x7, starting transfers between devices, exchange(): return lax.all_to_all(parts, axes, 0, 0)  35.6 us
    unnamed x169, local copies, waits for them, and re-layouts  27.6 us
    pallas_call x1, Pallas kernels, feed_forward(): pl.pallas_call(feed_kernel, grid=(count // tile,), out_shape=(shape((coun...  25.6 us
    pallas_call x1, Pallas kernels, attend_back(): pl.pallas_call(attend_back_kernel, out_shape=(shape(query.shape, BF16), s...  23 us
    reduce_scatter x1, waiting for transfers between devices, shards(): lax.psum_scatter(back, ('y', 'z'), scatter_dimension=0, tiled=True)  21.9 us
  transfers between devices with their start and end apart: 53, of which 26 were waited for; matrix products, arithmetic and copies ran while one was open for 19% of the time, Pallas kernels for 8%

profile of v3, /device:TPU:0, one launch (start us, length us, event | category | flops | bytes accessed | tf_op | source)
XLA Modules:
  0.0 650.7 jit_solution(17505147294340134969)
XLA Ops:
  17.4 6.6 %all-to-all-start = ((bf16[16,240,256]{2,1,0:T(8,128)(2,1)}), bf16[16,240,256]{2,1,0:T(8,128)(2,1)}, u32[]{:S(2)}, u32[]{:S(2)}) async-start(bf16[16,240,256]{2,1,0:T(8,128)(2,1)} %broadcast_dynamic-update-slice_fusion), calls=%async_computation | async-start | bytes 3932160 | tf_op jit(solution)/shard_map/all_to_all | solution.py:39
  28.6 36.7 %all-to-all-done = bf16[16,240,256]{2,1,0:T(8,128)(2,1)} async-done(((bf16[16,240,256]{2,1,0:T(8,128)(2,1)}), bf16[16,240,256]{2,1,0:T(8,128)(2,1)}, u32[]{:S(2)}, u32[]{:S(2)}) %all-to-all-start) | async-done | bytes 1966112 | tf_op jit(solution)/shard_map/all_to_all | solution.py:39
  65.3 2.1 fusion.35
  71.2 5.5 all-gather.6.cloned.1.call-done
  76.7 4.0 fusion.37
  92.7 9.3 %collective-permute-done.1.lane_d = bf16[128,1024]{1,0:T(8,128)(2,1)S(1)} collective-permute-done((bf16[128,1024]{1,0:T(8,128)(2,1)S(1)}, bf16[128,1024]{1,0:T(8,128)(2,1)S(1)}, u32[]{:S(2)}, u32[]{:S(2)}) %collective-permute-start.1) | collective-permute-done | bytes 262176 | tf_op jit(solution)/shard_map/lane/ppermute | solution.py:22
  105.7 16.4 %collective-permute-done.3.across_ref.proj_b = bf16[256,2048]{1,0:T(8,128)(2,1)S(1)} collective-permute-done((bf16[256,2048]{1,0:T(8,128)(2,1)S(1)}, bf16[256,2048]{1,0:T(8,128)(2,1)S(1)}, u32[]{:S(2)}, u32[]{:S(2)}) %collective-permute-start.3) | collective-permute-done | bytes 1048608 | tf_op jit(solution)/shard_map/out_chip/ppermute | solution.py:22
  128.9 7.1 %attend.1 = (bf16[4,128,1024]{2,1,0:T(8,128)(2,1)S(1)}, f32[4,1,512]{2,1,0:T(1,128)S(1)}) custom-call(s32[10]{0:T(128)S(1)} %pad_add_fusion.meta, bf16[4,128,1024]{2,1,0:T(8,128)(2,1)S(1)} %make_queries.1.q_ref, bf16[2048,512]{1,0:T(8,128)(2,1)S(1)} %copy-done.19, s32[4,1,128]{2,1,0:T(1,128)S(1)} %iota_add_fusion.place_ref, s32[4,1,128]{2,1,0:T(1,128)S(1)} %bitcast.156), custom_call_target="tpu_custom_call" | custom-call | flops 20000000000 | bytes 5000000 | tf_op jit(solution)/shard_map/attend/pallas_call | solution.py:414
  138.9 2.9 project.1.part_ref
  142.9 3.2 collective-permute-start.9
  146.1 34.0 %collective-permute-done.8.low_ref = bf16[64,2048]{1,0:T(8,128)(2,1)} collective-permute-done((bf16[64,2048]{1,0:T(8,128)(2,1)S(1)}, bf16[64,2048]{1,0:T(8,128)(2,1)}, u32[]{:S(2)}, u32[]{:S(2)}) %collective-permute-start.8) | collective-permute-done | bytes 262176 | tf_op jit(solution)/shard_map/residual/ppermute | solution.py:22
  180.1 2.4 ring_merge.1
  182.5 3.2 collective-permute-start.11
  186.6 11.3 %collective-permute-done.10 = bf16[128,2048]{1,0:T(8,128)(2,1)S(1)} collective-permute-done((bf16[128,2048]{1,0:T(8,128)(2,1)}, bf16[128,2048]{1,0:T(8,128)(2,1)S(1)}, u32[]{:S(2)}, u32[]{:S(2)}) %collective-permute-start.10) | collective-permute-done | bytes 524320 | tf_op jit(solution)/shard_map/residual/ppermute | solution.py:22
  204.6 2.8 collective-permute-start.12
  207.4 16.2 %collective-permute-done.12 = bf16[1536,256]{1,0:T(8,128)(2,1)S(1)} collective-permute-done((bf16[1536,256]{1,0:T(8,128)(2,1)S(1)}, bf16[1536,256]{1,0:T(8,128)(2,1)S(1)}, u32[]{:S(2)}, u32[]{:S(2)}) %collective-permute-start.12) | collective-permute-done | bytes 786464 | tf_op jit(solution)/shard_map/feed_weights/ppermute | solution.py:22
  223.6 3.8 collective-permute-start.13
  228.5 2.2 broadcast_in_dim.43
  231.7 2.7 collective-permute-done.13
  236.2 2.7 collective-permute-done.15
  240.6 2.1 copy_dynamic-update-slice_fusion
  246.1 4.6 collective-permute-done.17
  251.8 2.1 pad_maximum_fusion.down_ref
  255.3 25.6 %feed_forward.1 = (bf16[1024,768]{1,0:T(8,128)(2,1)S(1)}, bf16[1024,768]{1,0:T(8,128)(2,1)}, bf16[1024,768]{1,0:T(8,128)(2,1)}, bf16[1024,2048]{1,0:T(8,128)(2,1)}) custom-call(bf16[1024,2048]{1,0:T(8,128)(2,1)} %all-gather.10.cloned.1.call-done.n_ref, bf16[1024,2048]{1,0:T(8,128)(2,1)} %all-gather.12.cloned.1.call-done.cot_ref, ...), custom_call_target="tpu_custom_call" | custom-call | flops 19000000512 | bytes 32000000 | tf_op jit(solution)/shard_map/feed_forward/pallas_call | solution.py:664
  280.9 6.3 convolution_convert_fusion.1
  287.4 2.4 convolution_convert_fusion.3
  290.6 2.4 convolution_convert_fusion.4.down_ref
  293.0 3.7 convolution_convert_fusion.2.feed_ref
  298.3 2.1 copy-done
  300.4 5.6 convolution_convert_fusion
  311.0 21.9 %reduce-scatter.5.cloned.1.call-done = bf16[128,2048]{1,0:T(8,128)(2,1)} async-done(((bf16[1024,2048]{1,0:T(8,128)(2,1)}), bf16[128,2048]{1,0:T(8,128)(2,1)}) %reduce-scatter.5.cloned.1.call-update) | async-done | bytes 524304 | tf_op jit(solution)/shard_map/reduce_scatter | solution.py:838
  334.6 2.5 fusion.33
  341.0 9.9 %collective-permute-done.21.branch_d = bf16[128,2048]{1,0:T(8,128)(2,1)S(1)} collective-permute-done((bf16[128,2048]{1,0:T(8,128)(2,1)S(1)}, bf16[128,2048]{1,0:T(8,128)(2,1)S(1)}, u32[]{:S(2)}, u32[]{:S(2)}) %collective-permute-start.21) | collective-permute-done | bytes 524320 | tf_op jit(solution)/shard_map/branch/ppermute | solution.py:22
  355.9 2.4 collective-permute-done.22.branch_b
  358.3 2.3 collective-permute-done.24.branch_c
  360.6 23.0 %attend_back.1 = (bf16[4,128,1024]{2,1,0:T(8,128)(2,1)S(1)}, bf16[4,128,1024]{2,1,0:T(8,128)(2,1)}, bf16[8,128,512]{2,1,0:T(8,128)(2,1)}, bf16[8,128,512]{2,1,0:...) custom-call(s32[10]{0:T(128)S(1)} %pad_add_fusion.meta, ...), custom_call_target="tpu_custom_call" | custom-call | flops 24000000000 | bytes 20000000 | tf_op jit(solution)/shard_map/attend_back/pallas_call | solution.py:682
  384.9 16.3 %collective-permute-done.20 = bf16[512,2048]{1,0:T(8,128)(2,1)S(1)} collective-permute-done((bf16[512,2048]{1,0:T(8,128)(2,1)S(1)}, bf16[512,2048]{1,0:T(8,128)(2,1)S(1)}, u32[]{:S(2)}, u32[]{:S(2)}) %collective-permute-start.20) | collective-permute-done | bytes 2097184 | tf_op jit(solution)/shard_map/layer_out/ppermute | solution.py:22
  405.6 2.4 broadcast_add_fusion.1
  408.0 2.7 collective-permute-start.25
  412.0 4.4 all-to-all-start.1
  417.1 29.1 %all-to-all-done.1 = bf16[8,128,512]{2,1,0:T(8,128)(2,1)} async-done(((bf16[8,128,512]{2,1,0:T(8,128)(2,1)}), bf16[8,128,512]{2,1,0:T(8,128)(2,1)}, u32[]{:S(2)}, u32[]{:S(2)}) %all-to-all-start.1) | async-done | bytes 1048608 | tf_op jit(solution)/shard_map/kv_grad/all_to_all | solution.py:39
  452.4 4.3 all-to-all-start.2
  459.2 11.3 %all-to-all-done.2 = bf16[16,32,768]{2,1,0:T(8,128)(2,1)} async-done(((bf16[16,32,768]{2,1,0:T(8,128)(2,1)}), bf16[16,32,768]{2,1,0:T(8,128)(2,1)}, u32[]{:S(2)}, u32[]{:S(2)}) %all-to-all-start.2) | async-done | bytes 786464 | tf_op jit(solution)/shard_map/feed_grad/all_to_all | solution.py:39
  470.5 2.4 pad_maximum_fusion.2
  479.0 4.5 pack_heads.1
  483.6 5.8 all-to-all-start.3
  499.5 4.1 collective-permute-done.32.g_d
  503.6 4.9 collective-permute-start.33
  509.0 3.7 fusion
  512.9 3.0 collective-permute-done.35.g_c
  517.0 2.7 fusion.11
  522.4 35.2 %all-to-all-done.3 = bf16[16,48,2048]{2,1,0:T(8,128)(2,1)} async-done(((bf16[16,48,2048]{2,1,0:T(8,128)(2,1)}), bf16[16,48,2048]{2,1,0:T(8,128)(2,1)}, u32[]{:S(2)}, u32[]{:S(2)}) %all-to-all-start.3) | async-done | bytes 3145760 | tf_op jit(solution)/shard_map/heads_grad/all_to_all | solution.py:39
  561.7 6.2 all-to-all-start.4
  568.0 2.7 reduce_sum.109
  570.6 12.1 %all-to-all-done.4 = bf16[16,16,1536]{2,1,0:T(8,128)(2,1)S(1)} async-done(((bf16[16,16,1536]{2,1,0:T(8,128)(2,1)}), bf16[16,16,1536]{2,1,0:T(8,128)(2,1)S(1)}, u32[]{:S(2)}, u32[]{:S(2)}) %all-to-all-start.4) | async-done | bytes 786464 | tf_op jit(solution)/shard_map/all_to_all | solution.py:39
  584.7 4.3 all-to-all-start.5
  589.0 6.1 all-to-all-done.5
  596.3 3.7 fusion.2
  601.7 4.0 all-to-all-start.6
  605.8 2.3 copy-done.3
  609.5 5.0 spill.1
  618.3 16.4 %all-to-all-done.6.last_ref = bf16[8,64,2048]{2,1,0:T(8,128)(2,1)S(1)} async-done(((bf16[8,64,2048]{2,1,0:T(8,128)(2,1)}), bf16[8,64,2048]{2,1,0:T(8,128)(2,1)S(1)}, u32[]{:S(2)}, u32[]{:S(2)}) %all-to-all-start.6) | async-done | bytes 2097184 | tf_op jit(solution)/shard_map/heads_sum/all_to_all | solution.py:39
  637.5 2.1 finish.1
  641.4 2.3 add_convert_fusion.3
  (370 shorter events, 122.3 us)
Async XLA Ops:
  7.2 69.5 %all-gather.6.cloned.1.call-start = ((), (), s32[]{:S(2)}) async-start(), calls=%async_computation.11 | async-start | bytes 6684672 | tf_op jit(solution)/shard_map/all_gather | solution.py:731
  17.4 47.9 %all-to-all-start = ((bf16[16,240,256]{2,1,0:T(8,128)(2,1)}), bf16[16,240,256]{2,1,0:T(8,128)(2,1)}, u32[]{:S(2)}, u32[]{:S(2)}) async-start(bf16[16,240,256]{2,1,0:T(8,128)(2,1)} %broadcast_dynamic-update-slice_fusion), calls=%async_computation | async-start | bytes 3932160 | tf_op jit(solution)/shard_map/all_to_all | solution.py:39
  24.0 103.3 %all-gather.8.cloned.1.call-start = ((), (), s32[]{:S(2)}) async-start(), calls=%async_computation.12 | async-start | bytes 2228224 | tf_op jit(solution)/shard_map/all_gather | solution.py:801
  24.0 3.3 collective-permute-start
  25.2 44.2 %copy-start.61 = (s32[4]{0:T(128)}, s32[4]{0:T(128)S(1)}, u32[]{:S(2)}) copy-start(s32[4]{0:T(128)S(1)} %get-tuple-element.119) | copy-start | bytes 52
  26.3 44.9 %copy-start.63 = (f32[128]{0:T(128)}, f32[128]{0:T(128)S(1)}, u32[]{:S(2)}) copy-start(f32[128]{0:T(128)S(1)} %get-tuple-element.138) | copy-start | bytes 1540
  27.4 53.3 %copy-start.20 = (bf16[256,2048]{1,0:T(8,128)(2,1)}, bf16[256,2048]{1,0:T(8,128)(2,1)S(1)}, u32[]{:S(2)}) copy-start(bf16[256,2048]{1,0:T(8,128)(2,1)S(1)} %collective-permute-done.sib_ref.proj_c) | copy-start | bytes 3145732
  81.4 172.5 %all-gather.12.cloned.1.call-start = ((), (), s32[]{:S(2)}) async-start(), calls=%async_computation.14 | async-start | bytes 4718592 | tf_op jit(solution)/shard_map/all_gather | solution.py:814
  84.6 170.7 %all-gather.10.cloned.1.call-start = ((), (), s32[]{:S(2)}) async-start(), calls=%async_computation.13 | async-start | bytes 4718592 | tf_op jit(solution)/shard_map/all_gather | solution.py:822
  85.7 17.6 %collective-permute-start.6 = (bf16[1024,512]{1,0:T(8,128)(2,1)}, bf16[1024,512]{1,0:T(8,128)(2,1)}, u32[]{:S(2)}, u32[]{:S(2)}) collective-permute-start(bf16[1024,512]{1,0:T(8,128)(2,1)} %pad_maximum_fusion.3), channel_id=1, source_target_pairs={{0,1},{1,0},{2,3},{3,2},{4,5},{5,4},{6,7},{7,6},{8,9},{9,8},{10,11... | collective-permute-start | bytes 3145736 | tf_op jit(solution)/shard_map/ppermute | solution.py:22
  86.9 35.2 %collective-permute-start.3 = (bf16[256,2048]{1,0:T(8,128)(2,1)S(1)}, bf16[256,2048]{1,0:T(8,128)(2,1)S(1)}, u32[]{:S(2)}, u32[]{:S(2)}) collective-permute-start(bf16[256,2048]{1,0:T(8,128)(2,1)S(1)} %broadcast_add_fusion.3), channel_id=1, source_target_pairs={{0,8},{8,0},{1,9},{9,1},{2,10},{10,2},{3,11},{11,3},{4,12},{12,4},... | collective-permute-start | bytes 3145736 | tf_op jit(solution)/shard_map/out_chip/ppermute | solution.py:22
  90.3 11.7 %collective-permute-start.1 = (bf16[128,1024]{1,0:T(8,128)(2,1)S(1)}, bf16[128,1024]{1,0:T(8,128)(2,1)S(1)}, u32[]{:S(2)}, u32[]{:S(2)}) collective-permute-start(bf16[128,1024]{1,0:T(8,128)(2,1)S(1)} %multiply_convert_fusion.1.lane_a), channel_id=1, source_target_pairs={{0,6},{2,0},{4,2},{6,4},{1,7},{3,1},{5,3},{7,5},{8,14},{10,8},{12,... | collective-permute-start | bytes 786440 | tf_op jit(solution)/shard_map/lane/ppermute | solution.py:22
  92.2 12.7 %collective-permute-start.4 = (bf16[128,1024]{1,0:T(8,128)(2,1)S(1)}, bf16[128,1024]{1,0:T(8,128)(2,1)S(1)}, u32[]{:S(2)}, u32[]{:S(2)}) collective-permute-start(bf16[128,1024]{1,0:T(8,128)(2,1)S(1)} %multiply_convert_fusion.1.lane_a), channel_id=1, source_target_pairs={{0,2},{2,4},{4,6},{6,0},{1,3},{3,5},{5,7},{7,1},{8,10},{10,12},{12... | collective-permute-start | bytes 786440 | tf_op jit(solution)/shard_map/lane/ppermute | solution.py:22
  102.0 21.3 %collective-permute-start.2 = (bf16[64,1024]{1,0:T(8,128)(2,1)S(1)}, bf16[64,1024]{1,0:T(8,128)(2,1)S(1)}, u32[]{:S(2)}, u32[]{:S(2)}) collective-permute-start(bf16[64,1024]{1,0:T(8,128)(2,1)S(1)} %slice.319), channel_id=1, source_target_pairs={{0,6},{2,0},{4,2},{6,4},{1,7},{3,1},{5,3},{7,5},{8,14},{10,8},{12,... | collective-permute-start | bytes 393224 | tf_op jit(solution)/shard_map/lane/ppermute | solution.py:22
  104.9 18.5 %collective-permute-start.5 = (bf16[64,1024]{1,0:T(8,128)(2,1)S(1)}, bf16[64,1024]{1,0:T(8,128)(2,1)S(1)}, u32[]{:S(2)}, u32[]{:S(2)}) collective-permute-start(bf16[64,1024]{1,0:T(8,128)(2,1)S(1)} %slice.322), channel_id=1, source_target_pairs={{0,2},{2,4},{4,6},{6,0},{1,3},{3,5},{5,7},{7,1},{8,10},{10,12},{12... | collective-permute-start | bytes 393224 | tf_op jit(solution)/shard_map/lane/ppermute | solution.py:22
  127.1 9.6 %collective-permute-start.7 = (bf16[256,2048]{1,0:T(8,128)(2,1)}, bf16[256,2048]{1,0:T(8,128)(2,1)S(1)}, u32[]{:S(2)}, u32[]{:S(2)}) collective-permute-start(bf16[256,2048]{1,0:T(8,128)(2,1)} %broadcast_add_fusion.2), channel_id=1, source_target_pairs={{0,1},{1,0},{2,3},{3,2},{4,5},{5,4},{6,7},{7,6},{8,9},{9,8},{10,11... | collective-permute-start | bytes 3145736 | tf_op jit(solution)/shard_map/out_chip/ppermute | solution.py:22
  142.8 37.4 %copy-start.2 = (bf16[4,128,2048]{2,1,0:T(8,128)(2,1)}, bf16[4,128,2048]{2,1,0:T(8,128)(2,1)S(1)}, u32[]{:S(2)}) copy-start(bf16[4,128,2048]{2,1,0:T(8,128)(2,1)S(1)} %project.1.part_ref) | copy-start | bytes 6291460
  142.8 37.3 %collective-permute-start.8 = (bf16[64,2048]{1,0:T(8,128)(2,1)S(1)}, bf16[64,2048]{1,0:T(8,128)(2,1)}, u32[]{:S(2)}, u32[]{:S(2)}) collective-permute-start(bf16[64,2048]{1,0:T(8,128)(2,1)S(1)} %get-tuple-element.122), channel_id=1, source_target_pairs={{0,2},{2,4},{4,6},{6,0},{1,3},{3,5},{5,7},{7,1},{8,10},{10,12},{12... | collective-permute-start | bytes 786440 | tf_op jit(solution)/shard_map/residual/ppermute | solution.py:22
  142.9 37.2 %collective-permute-start.9 = (bf16[64,2048]{1,0:T(8,128)(2,1)S(1)}, bf16[64,2048]{1,0:T(8,128)(2,1)}, u32[]{:S(2)}, u32[]{:S(2)}) collective-permute-start(bf16[64,2048]{1,0:T(8,128)(2,1)S(1)} %get-tuple-element.121), channel_id=1, source_target_pairs={{0,6},{2,0},{4,2},{6,4},{1,7},{3,1},{5,3},{7,5},{8,14},{10,8},{12,... | collective-permute-start | bytes 786440 | tf_op jit(solution)/shard_map/residual/ppermute | solution.py:22
  182.5 15.3 %collective-permute-start.10 = (bf16[128,2048]{1,0:T(8,128)(2,1)}, bf16[128,2048]{1,0:T(8,128)(2,1)S(1)}, u32[]{:S(2)}, u32[]{:S(2)}) collective-permute-start(bf16[128,2048]{1,0:T(8,128)(2,1)} %get-tuple-element.83), channel_id=1, source_target_pairs={{0,2},{2,4},{4,6},{6,0},{1,3},{3,5},{5,7},{7,1},{8,10},{10,12},{12... | collective-permute-start | bytes 1572872 | tf_op jit(solution)/shard_map/residual/ppermute | solution.py:22
  182.5 15.3 %collective-permute-start.11 = (bf16[128,2048]{1,0:T(8,128)(2,1)}, bf16[128,2048]{1,0:T(8,128)(2,1)S(1)}, u32[]{:S(2)}, u32[]{:S(2)}) collective-permute-start(bf16[128,2048]{1,0:T(8,128)(2,1)} %get-tuple-element.84), channel_id=1, source_target_pairs={{0,6},{2,0},{4,2},{6,4},{1,7},{3,1},{5,3},{7,5},{8,14},{10,8},{12,... | collective-permute-start | bytes 1572872 | tf_op jit(solution)/shard_map/residual/ppermute | solution.py:22
  201.5 131.4 %reduce-scatter.5.cloned.1.call-start = ((), (), s32[]{:S(2)}) async-start(), calls=%async_computation.15 | async-start | bytes 4718592 | tf_op jit(solution)/shard_map/reduce_scatter | solution.py:838
  204.6 19.0 %collective-permute-start.12 = (bf16[1536,256]{1,0:T(8,128)(2,1)S(1)}, bf16[1536,256]{1,0:T(8,128)(2,1)S(1)}, u32[]{:S(2)}, u32[]{:S(2)}) collective-permute-start(bf16[1536,256]{1,0:T(8,128)(2,1)S(1)} %bitcast.169), channel_id=1, source_target_pairs={{0,48},{16,0},{32,16},{48,32},{1,49},{17,1},{33,17},{49,33},{2,50}... | collective-permute-start | bytes 2359304 | tf_op jit(solution)/shard_map/feed_weights/ppermute | solution.py:22
  207.4 20.0 %collective-permute-start.14 = (bf16[1536,256]{1,0:T(8,128)(2,1)S(1)}, bf16[1536,256]{1,0:T(8,128)(2,1)}, u32[]{:S(2)}, u32[]{:S(2)}) collective-permute-start(bf16[1536,256]{1,0:T(8,128)(2,1)S(1)} %bitcast.170), channel_id=1, source_target_pairs={{0,16},{16,32},{32,48},{48,0},{1,17},{17,33},{33,49},{49,1},{2,18}... | collective-permute-start | bytes 2359304 | tf_op jit(solution)/shard_map/feed_weights/ppermute | solution.py:22
  223.6 10.7 %collective-permute-start.13 = (bf16[768,256]{1,0:T(8,128)(2,1)S(1)}, bf16[768,256]{1,0:T(8,128)(2,1)}, u32[]{:S(2)}, u32[]{:S(2)}) collective-permute-start(bf16[768,256]{1,0:T(8,128)(2,1)S(1)} %slice.336), channel_id=1, source_target_pairs={{0,48},{16,0},{32,16},{48,32},{1,49},{17,1},{33,17},{49,33},{2,50}... | collective-permute-start | bytes 1179656 | tf_op jit(solution)/shard_map/feed_weights/ppermute | solution.py:22
  228.4 10.4 %collective-permute-start.15 = (bf16[768,256]{1,0:T(8,128)(2,1)S(1)}, bf16[768,256]{1,0:T(8,128)(2,1)S(1)}, u32[]{:S(2)}, u32[]{:S(2)}) collective-permute-start(bf16[768,256]{1,0:T(8,128)(2,1)S(1)} %slice.337), channel_id=1, source_target_pairs={{0,16},{16,32},{32,48},{48,0},{1,17},{17,33},{33,49},{49,1},{2,18}... | collective-permute-start | bytes 1179656 | tf_op jit(solution)/shard_map/feed_weights/ppermute | solution.py:22
  242.8 11.2 %collective-permute-start.16 = (bf16[3,2048,256]{2,1,0:T(8,128)(2,1)}, bf16[3,2048,256]{2,1,0:T(8,128)(2,1)}, u32[]{:S(2)}, u32[]{:S(2)}) collective-permute-start(bf16[3,2048,256]{2,1,0:T(8,128)(2,1)} %bitcast.54.own_ref), channel_id=1, source_target_pairs={{0,1},{1,0},{2,3},{3,2},{4,5},{5,4},{6,7},{7,6},{8,9},{9,8},{10,11... | collective-permute-start | bytes 9437192 | tf_op jit(solution)/shard_map/feed_weights/ppermute | solution.py:22
  245.1 5.6 collective-permute-start.17
  280.9 122.2 %reduce-scatter.7.cloned.1.call-start = ((), (), s32[]{:S(2)}) async-start(), calls=%async_computation.16 | async-start | bytes 5898240 | tf_op jit(solution)/shard_map/feed_grad/reduce_scatter | solution.py:848
  287.3 9.4 %collective-permute-start.18 = (bf16[2048,768]{1,0:T(8,128)(2,1)S(1)}, bf16[2048,768]{1,0:T(8,128)(2,1)S(1)}, u32[]{:S(2)}, u32[]{:S(2)}) collective-permute-start(bf16[2048,768]{1,0:T(8,128)(2,1)S(1)} %convolution_convert_fusion.1), channel_id=1, source_target_pairs={{0,1},{1,0},{2,3},{3,2},{4,5},{5,4},{6,7},{7,6},{8,9},{9,8},{10,11... | collective-permute-start | bytes 9437192 | tf_op jit(solution)/shard_map/feed_grad/ppermute | solution.py:22
  289.8 6.9 %collective-permute-start.19 = (bf16[2048,384]{1,0:T(8,128)(2,1)S(1)}, bf16[2048,384]{1,0:T(8,128)(2,1)S(1)}, u32[]{:S(2)}, u32[]{:S(2)}) collective-permute-start(bf16[2048,384]{1,0:T(8,128)(2,1)S(1)} %convolution_convert_fusion.3), channel_id=1, source_target_pairs={{0,1},{1,0},{2,3},{3,2},{4,5},{5,4},{6,7},{7,6},{8,9},{9,8},{10,11... | collective-permute-start | bytes 4718600 | tf_op jit(solution)/shard_map/feed_grad/ppermute | solution.py:22
  300.4 34.2 %copy-start.42 = (bf16[128,2048]{1,0:T(8,128)(2,1)S(1)}, bf16[128,2048]{1,0:T(8,128)(2,1)}, u32[]{:S(2)}) copy-start(bf16[128,2048]{1,0:T(8,128)(2,1)} %param.33) | copy-start | bytes 1572868
  308.0 26.6 %copy-start.29 = (f32[128,2048]{1,0:T(8,128)S(1)}, f32[128,2048]{1,0:T(8,128)}, u32[]{:S(2)}) copy-start(f32[128,2048]{1,0:T(8,128)} %copy-done.28) | copy-start | bytes 3145732
  337.1 13.7 %collective-permute-start.21 = (bf16[128,2048]{1,0:T(8,128)(2,1)S(1)}, bf16[128,2048]{1,0:T(8,128)(2,1)S(1)}, u32[]{:S(2)}, u32[]{:S(2)}) collective-permute-start(bf16[128,2048]{1,0:T(8,128)(2,1)S(1)} %get-tuple-element.115.branch_a), channel_id=1, source_target_pairs={{0,6},{2,0},{4,2},{6,4},{1,7},{3,1},{5,3},{7,5},{8,14},{10,8},{12,... | collective-permute-start | bytes 1572872 | tf_op jit(solution)/shard_map/branch/ppermute | solution.py:22
  337.6 14.9 %collective-permute-start.23 = (bf16[128,2048]{1,0:T(8,128)(2,1)S(1)}, bf16[128,2048]{1,0:T(8,128)(2,1)S(1)}, u32[]{:S(2)}, u32[]{:S(2)}) collective-permute-start(bf16[128,2048]{1,0:T(8,128)(2,1)S(1)} %get-tuple-element.115.branch_a), channel_id=1, source_target_pairs={{0,2},{2,4},{4,6},{6,0},{1,3},{3,5},{5,7},{7,1},{8,10},{10,12},{12... | collective-permute-start | bytes 1572872 | tf_op jit(solution)/shard_map/branch/ppermute | solution.py:22
  350.9 7.4 %collective-permute-start.22 = (bf16[64,2048]{1,0:T(8,128)(2,1)S(1)}, bf16[64,2048]{1,0:T(8,128)(2,1)S(1)}, u32[]{:S(2)}, u32[]{:S(2)}) collective-permute-start(bf16[64,2048]{1,0:T(8,128)(2,1)S(1)} %slice.342), channel_id=1, source_target_pairs={{0,6},{2,0},{4,2},{6,4},{1,7},{3,1},{5,3},{7,5},{8,14},{10,8},{12,... | collective-permute-start | bytes 786440 | tf_op jit(solution)/shard_map/branch/ppermute | solution.py:22
  352.5 8.2 %collective-permute-start.24 = (bf16[64,2048]{1,0:T(8,128)(2,1)S(1)}, bf16[64,2048]{1,0:T(8,128)(2,1)S(1)}, u32[]{:S(2)}, u32[]{:S(2)}) collective-permute-start(bf16[64,2048]{1,0:T(8,128)(2,1)S(1)} %slice.343), channel_id=1, source_target_pairs={{0,2},{2,4},{4,6},{6,0},{1,3},{3,5},{5,7},{7,1},{8,10},{10,12},{12... | collective-permute-start | bytes 786440 | tf_op jit(solution)/shard_map/branch/ppermute | solution.py:22
  354.9 46.3 %collective-permute-start.20 = (bf16[512,2048]{1,0:T(8,128)(2,1)S(1)}, bf16[512,2048]{1,0:T(8,128)(2,1)S(1)}, u32[]{:S(2)}, u32[]{:S(2)}) collective-permute-start(bf16[512,2048]{1,0:T(8,128)(2,1)S(1)} %add_bitcast_fusion), channel_id=1, source_target_pairs={{0,8},{8,0},{1,9},{9,1},{2,10},{10,2},{3,11},{11,3},{4,12},{12,4},... | collective-permute-start | bytes 6291464 | tf_op jit(solution)/shard_map/layer_out/ppermute | solution.py:22
  383.7 27.0 %copy-start.50 = (bf16[8,128,512]{2,1,0:T(8,128)(2,1)S(1)}, bf16[8,128,512]{2,1,0:T(8,128)(2,1)}, u32[]{:S(2)}) copy-start(bf16[8,128,512]{2,1,0:T(8,128)(2,1)} %get-tuple-element.91) | copy-start | bytes 3145732
  383.7 27.0 %collective-permute-start.26 = (bf16[8,128,512]{2,1,0:T(8,128)(2,1)}, bf16[8,128,512]{2,1,0:T(8,128)(2,1)S(1)}, u32[]{:S(2)}, u32[]{:S(2)}) collective-permute-start(bf16[8,128,512]{2,1,0:T(8,128)(2,1)} %get-tuple-element.92), channel_id=1, source_target_pairs={{0,1},{1,0},{2,3},{3,2},{4,5},{5,4},{6,7},{7,6},{8,9},{9,8},{10,11... | collective-permute-start | bytes 3145736 | tf_op jit(solution)/shard_map/kv_grad/ppermute | solution.py:22
  408.0 40.9 %collective-permute-start.25 = (bf16[512,1152]{1,0:T(8,128)(2,1)}, bf16[512,1152]{1,0:T(8,128)(2,1)}, u32[]{:S(2)}, u32[]{:S(2)}) collective-permute-start(bf16[512,1152]{1,0:T(8,128)(2,1)} %broadcast_add_fusion.1), channel_id=1, source_target_pairs={{0,64},{64,0},{1,65},{65,1},{2,66},{66,2},{3,67},{67,3},{4,68},{68... | collective-permute-start | bytes 3538952 | tf_op jit(solution)/shard_map/feed_grad/ppermute | solution.py:22
  412.0 36.9 %copy-start.35 = (bf16[512,1152]{1,0:T(8,128)(2,1)S(1)}, bf16[512,1152]{1,0:T(8,128)(2,1)}, u32[]{:S(2)}) copy-start(bf16[512,1152]{1,0:T(8,128)(2,1)} %reduce-scatter.7.cloned.1.call-done) | copy-start | bytes 3538948
  412.0 34.2 %all-to-all-start.1 = ((bf16[8,128,512]{2,1,0:T(8,128)(2,1)}), bf16[8,128,512]{2,1,0:T(8,128)(2,1)}, u32[]{:S(2)}, u32[]{:S(2)}) async-start(bf16[8,128,512]{2,1,0:T(8,128)(2,1)} %add_convert_fusion.1), calls=%async_computation.3 | async-start | bytes 2097152 | tf_op jit(solution)/shard_map/kv_grad/all_to_all | solution.py:39
  416.4 56.6 %reduce-scatter.9.cloned.1.call-start = ((), (), s32[]{:S(2)}) async-start(), calls=%async_computation.17 | async-start | bytes 1310720 | tf_op jit(solution)/shard_map/latent_grad/reduce_scatter | solution.py:893
  452.4 18.1 %all-to-all-start.2 = ((bf16[16,32,768]{2,1,0:T(8,128)(2,1)}), bf16[16,32,768]{2,1,0:T(8,128)(2,1)}, u32[]{:S(2)}, u32[]{:S(2)}) async-start(bf16[16,32,768]{2,1,0:T(8,128)(2,1)} %slice_add_fusion), calls=%async_computation.4 | async-start | bytes 1572864 | tf_op jit(solution)/shard_map/feed_grad/all_to_all | solution.py:39
  456.7 149.1 %all-gather.14.cloned.1.call-start = ((), (), s32[]{:S(2)}) async-start(), calls=%async_computation.19 | async-start | bytes 5898240 | tf_op jit(solution)/shard_map/feed_grad/all_gather | solution.py:888
  456.8 21.0 %collective-permute-start.27 = (bf16[512,2048]{1,0:T(8,128)(2,1)}, bf16[512,2048]{1,0:T(8,128)(2,1)}, u32[]{:S(2)}, u32[]{:S(2)}) collective-permute-start(bf16[512,2048]{1,0:T(8,128)(2,1)} %get-tuple-element.95), channel_id=1, source_target_pairs={{0,1},{1,0},{2,3},{3,2},{4,5},{5,4},{6,7},{7,6},{8,9},{9,8},{10,11... | collective-permute-start | bytes 6291464 | tf_op jit(solution)/shard_map/heads_grad/ppermute | solution.py:22
  472.9 4.9 collective-permute-start.28
  483.6 74.0 %all-to-all-start.3 = ((bf16[16,48,2048]{2,1,0:T(8,128)(2,1)}), bf16[16,48,2048]{2,1,0:T(8,128)(2,1)}, u32[]{:S(2)}, u32[]{:S(2)}) async-start(bf16[16,48,2048]{2,1,0:T(8,128)(2,1)} %pack_heads.1), calls=%async_computation.6 | async-start | bytes 6291456 | tf_op jit(solution)/shard_map/heads_grad/all_to_all | solution.py:39
  491.6 12.0 %collective-permute-start.32 = (bf16[128,1536]{1,0:T(8,128)(2,1)S(1)}, bf16[128,1536]{1,0:T(8,128)(2,1)S(1)}, u32[]{:S(2)}, u32[]{:S(2)}) collective-permute-start(bf16[128,1536]{1,0:T(8,128)(2,1)S(1)} %pad_maximum_fusion.5.g_a), channel_id=1, source_target_pairs={{0,6},{2,0},{4,2},{6,4},{1,7},{3,1},{5,3},{7,5},{8,14},{10,8},{12,... | collective-permute-start | bytes 1179656 | tf_op jit(solution)/shard_map/first_lane/ppermute | solution.py:22
  492.8 16.1 %collective-permute-start.34 = (bf16[128,1536]{1,0:T(8,128)(2,1)S(1)}, bf16[128,1536]{1,0:T(8,128)(2,1)S(1)}, u32[]{:S(2)}, u32[]{:S(2)}) collective-permute-start(bf16[128,1536]{1,0:T(8,128)(2,1)S(1)} %pad_maximum_fusion.5.g_a), channel_id=1, source_target_pairs={{0,2},{2,4},{4,6},{6,0},{1,3},{3,5},{5,7},{7,1},{8,10},{10,12},{12... | collective-permute-start | bytes 1179656 | tf_op jit(solution)/shard_map/first_lane/ppermute | solution.py:22
  496.3 16.5 %collective-permute-start.29 = (bf16[128,512]{1,0:T(8,128)(2,1)}, bf16[128,512]{1,0:T(8,128)(2,1)S(1)}, u32[]{:S(2)}, u32[]{:S(2)}) collective-permute-start(bf16[128,512]{1,0:T(8,128)(2,1)} %get-tuple-element.99), channel_id=1, source_target_pairs={{0,4},{2,6},{4,0},{6,2},{1,5},{3,7},{5,1},{7,3},{8,12},{10,14},{12... | collective-permute-start | bytes 393224 | tf_op jit(solution)/shard_map/columns/ppermute | solution.py:22
  496.9 15.8 %collective-permute-start.30 = (bf16[128,512]{1,0:T(8,128)(2,1)}, bf16[128,512]{1,0:T(8,128)(2,1)S(1)}, u32[]{:S(2)}, u32[]{:S(2)}) collective-permute-start(bf16[128,512]{1,0:T(8,128)(2,1)} %get-tuple-element.100), channel_id=1, source_target_pairs={{0,6},{2,0},{4,2},{6,4},{1,7},{3,1},{5,3},{7,5},{8,14},{10,8},{12,... | collective-permute-start | bytes 393224 | tf_op jit(solution)/shard_map/columns/ppermute | solution.py:22
  499.0 13.8 %collective-permute-start.31 = (bf16[128,512]{1,0:T(8,128)(2,1)}, bf16[128,512]{1,0:T(8,128)(2,1)S(1)}, u32[]{:S(2)}, u32[]{:S(2)}) collective-permute-start(bf16[128,512]{1,0:T(8,128)(2,1)} %get-tuple-element.101), channel_id=1, source_target_pairs={{0,2},{2,4},{4,6},{6,0},{1,3},{3,5},{5,7},{7,1},{8,10},{10,12},{12... | collective-permute-start | bytes 393224 | tf_op jit(solution)/shard_map/columns/ppermute | solution.py:22
  503.6 9.2 %collective-permute-start.33 = (bf16[64,1536]{1,0:T(8,128)(2,1)S(1)}, bf16[64,1536]{1,0:T(8,128)(2,1)S(1)}, u32[]{:S(2)}, u32[]{:S(2)}) collective-permute-start(bf16[64,1536]{1,0:T(8,128)(2,1)S(1)} %slice.355), channel_id=1, source_target_pairs={{0,6},{2,0},{4,2},{6,4},{1,7},{3,1},{5,3},{7,5},{8,14},{10,8},{12,... | collective-permute-start | bytes 589832 | tf_op jit(solution)/shard_map/first_lane/ppermute | solution.py:22
  508.9 7.0 %collective-permute-start.35 = (bf16[64,1536]{1,0:T(8,128)(2,1)S(1)}, bf16[64,1536]{1,0:T(8,128)(2,1)S(1)}, u32[]{:S(2)}, u32[]{:S(2)}) collective-permute-start(bf16[64,1536]{1,0:T(8,128)(2,1)S(1)} %slice.356), channel_id=1, source_target_pairs={{0,2},{2,4},{4,6},{6,0},{1,3},{3,5},{5,7},{7,1},{8,10},{10,12},{12... | collective-permute-start | bytes 589832 | tf_op jit(solution)/shard_map/first_lane/ppermute | solution.py:22
  516.9 42.5 %collective-permute-start.36 = (bf16[256,1536]{1,0:T(8,128)(2,1)S(1)}, bf16[256,1536]{1,0:T(8,128)(2,1)}, u32[]{:S(2)}, u32[]{:S(2)}) collective-permute-start(bf16[256,1536]{1,0:T(8,128)(2,1)S(1)} %get-tuple-element.103), channel_id=1, source_target_pairs={{0,1},{1,0},{2,3},{3,2},{4,5},{5,4},{6,7},{7,6},{8,9},{9,8},{10,11... | collective-permute-start | bytes 2359304 | tf_op jit(solution)/shard_map/ppermute | solution.py:22
  561.7 21.0 %all-to-all-start.4 = ((bf16[16,16,1536]{2,1,0:T(8,128)(2,1)}), bf16[16,16,1536]{2,1,0:T(8,128)(2,1)S(1)}, u32[]{:S(2)}, u32[]{:S(2)}) async-start(bf16[16,16,1536]{2,1,0:T(8,128)(2,1)} %bitcast.78), calls=%async_computation.7 | async-start | bytes 1572864 | tf_op jit(solution)/shard_map/all_to_all | solution.py:39
  568.0 28.4 %copy-start.44 = (bf16[512,2048]{1,0:T(8,128)(2,1)S(1)}, bf16[512,2048]{1,0:T(8,128)(2,1)}, u32[]{:S(2)}) copy-start(bf16[512,2048]{1,0:T(8,128)(2,1)} %copy-done.43) | copy-start | bytes 6291460
  584.7 10.5 %all-to-all-start.5 = ((bf16[16,8,256]{2,1,0:T(8,128)(2,1)}), bf16[16,8,256]{2,1,0:T(8,128)(2,1)S(1)}, u32[]{:S(2)}, u32[]{:S(2)}) async-start(bf16[16,8,256]{2,1,0:T(8,128)(2,1)} %bitcast.81), calls=%async_computation.8 | async-start | bytes 131072 | tf_op jit(solution)/shard_map/up_grad/all_to_all | solution.py:39
  589.0 52.4 %reduce-scatter.11.cloned.1.call-start = ((), (), s32[]{:S(2)}) async-start(), calls=%async_computation.18 | async-start | bytes 2621440 | tf_op jit(solution)/shard_map/layer_out/reduce_scatter | solution.py:936
  601.7 32.9 %all-to-all-start.6 = ((bf16[8,64,2048]{2,1,0:T(8,128)(2,1)}), bf16[8,64,2048]{2,1,0:T(8,128)(2,1)S(1)}, u32[]{:S(2)}, u32[]{:S(2)}) async-start(bf16[8,64,2048]{2,1,0:T(8,128)(2,1)} %broadcast_in_dim.87), calls=%async_computation.10 | async-start | bytes 4194304 | tf_op jit(solution)/shard_map/heads_sum/all_to_all | solution.py:39
  614.6 25.8 %copy-start.72 = (bf16[128]{0:T(256)(128)(2,1)S(1)}, bf16[128]{0:T(256)(128)(2,1)}, u32[]{:S(2)}) copy-start(bf16[128]{0:T(256)(128)(2,1)} %param.22) | copy-start | bytes 772
  614.6 26.3 %copy-start.76 = (bf16[128]{0:T(256)(128)(2,1)S(1)}, bf16[128]{0:T(256)(128)(2,1)}, u32[]{:S(2)}) copy-start(bf16[128]{0:T(256)(128)(2,1)} %param.29) | copy-start | bytes 772
  (70 other events, 359.4 us)
Sparse Core Ops, SparseCore 0:
  10.3 66.3 all-gather.5
  81.6 38.0 all-gather.7
  121.4 57.2 all-gather.11
  201.7 53.5 all-gather.9
  281.0 51.8 reduce-scatter.4
  335.2 49.7 reduce-scatter.6
  419.6 25.7 reduce-scatter.8
  473.0 84.3 all-gather.13
  600.2 25.8 reduce-scatter.10

commit v4 on v3

--- a/solution.py
+++ b/solution.py
@@ -877,13 +877,25 @@
         kv_grad = kv_own.astype(F32) + sibling(kv_sib).astype(F32)
         kv_grad = after(kv_grad, feed_part[0, 0] + fed_across[0, 0]).astype(BF16)
         kv_sum = total_of(exchange(kv_grad, ("y", "z")))
+    with jax.named_scope("heads_grad"):
+        heads_parts = pack_heads(
+            (kv_sum[0, 0] * 0).astype(jnp.int32).reshape(1),
+            out_grad,
+            sibling(out_grad_sib),
+            up_grad,
+            sibling(up_sib),
+        )
+        heads_got = exchange(heads_parts, ACROSS)
+    with jax.named_scope("layer_out"):
+        fed = fed_own.astype(F32) + after(fed_across.astype(F32), heads_parts)
+        fed_part = lax.psum_scatter(fed.astype(BF16), "z", scatter_dimension=0, tiled=True)
+        layer_out = (residual + fed_part.astype(F32)).astype(BF16)
     with jax.named_scope("feed_grad"):
-        feed_part = after(feed_part, grad_queries)
+        feed_part = after(feed_part, kv_sum)
         feed_across = turn(feed_part, "v", 1)
         feed_part = (feed_part.astype(F32) + feed_across.astype(F32)).astype(BF16)
         feed_part = feed_part.reshape(16, quarter, 3 * SLOT)
-        v_sum = feed_part
-        swapped = exchange(after(feed_part[..., : 2 * SLOT], kv_sum), SEQ)
+        swapped = exchange(after(feed_part[..., : 2 * SLOT], heads_got), SEQ)
         feed_part = jnp.concatenate([swapped, feed_part[..., 2 * SLOT :]], axis=2)
         feed_sum = lax.all_gather(
             feed_part.reshape(16 * quarter, 3 * SLOT), "x", axis=0, tiled=True
@@ -892,17 +904,8 @@
         latent_parts = latent_parts.reshape(4 * width, latent_width)
         grad_latent_n = lax.psum_scatter(latent_parts, "z", scatter_dimension=0, tiled=True)
         grad_latent_n = grad_latent_n.astype(F32)
-    with jax.named_scope("heads_grad"):
-        heads_parts = pack_heads(
-            ((swapped[0, 0, 0] + grad_latent_n[0, 0]) * 0).astype(jnp.int32).reshape(1),
-            out_grad,
-            sibling(out_grad_sib),
-            up_grad,
-            sibling(up_sib),
-        )
-        heads_got = exchange(heads_parts, ACROSS)
     grad_keys = rotate_back(kv_sum[:, :head], cos_own, sin_own).astype(BF16)
-    grad_values = after(kv_sum[:, head:], v_sum).astype(BF16)
+    grad_values = kv_sum[:, head:].astype(BF16)
     grad_latent = rms_back(latent, inv_latent, gain_query, grad_latent_n)
     grad_latent = grad_latent.astype(BF16)
     grad_first = jnp.concatenate([grad_latent, grad_keys, grad_values], axis=1)
@@ -925,16 +928,12 @@
     input_grad = grad_residual + grad_one
 
     share = width // 8
-    tail = after(after(own_first, input_grad), heads_got).reshape(2, 8, share, lane_width).transpose(1, 0, 2, 3)
+    tail = after(after(own_first, input_grad), swapped).reshape(2, 8, share, lane_width).transpose(1, 0, 2, 3)
     tail = total_of(exchange(tail.reshape(16, share, lane_width).astype(BF16), ACROSS))
     with jax.named_scope("up_grad"):
         up_part = exchange(after(up_part, tail).reshape(16, depth // 8, head), SEQ)
         up_part = up_part.reshape(2, 8, depth // 8, head).transpose(0, 2, 1, 3)
         up_part = up_part.reshape(-1, model)
-    with jax.named_scope("layer_out"):
-        fed = fed_own.astype(F32) + after(fed_across.astype(F32), up_part)
-        fed_part = lax.psum_scatter(fed.astype(BF16), "z", scatter_dimension=0, tiled=True)
-        layer_out = (residual + fed_part.astype(F32)).astype(BF16)
     with jax.named_scope("heads_sum"):
         first_part = jnp.pad(tail.astype(BF16), ((0, 0), (0, model - lane_width)))
         last_sum = spread(jnp.concatenate([out_part, up_part, first_part], axis=0), DP)

time: 662 us -> 664 us (level)
  waiting for transfers between devices: 312 us -> 319 us
    ppermute x37, waiting for transfers between devices: 136 us -> 192 us  [turn(): lax.ppermute(value, axis, [(i, (i + step) % size) for i in range(size)])]
    all_to_all x7, waiting for transfers between devices: 147 us -> 98.2 us  [exchange(): return lax.all_to_all(parts, axes, 0, 0)]
    unnamed x169 -> x157, local copies, waits for them, and re-layouts: 27.6 us -> 27.1 us
    slice x18 -> x16, local copies, waits for them, and re-layouts: 14.2 us -> 13.8 us  [after(): first = other[(0,) * other.ndim] if other.ndim else other]
  transfers between devices with their start and end apart: 53 -> 53, of which waited for: 26 -> 25; matrix products, arithmetic and copies ran while one was open for 19% -> 18% of each run, Pallas kernels for 8% -> 8%
where the time goes in v4:
time: 664 us; the launch traced here: 653 us
  waiting for transfers between devices  319 us (48%)
  Pallas kernels  78.5 us (12%)
  starting transfers between devices  75.6 us (11%)
  local copies, waits for them, and re-layouts  63.9 us (10%)
  other arithmetic  57 us (9%)
  matrix products  30.8 us (5%)
  between operations  28.3 us (4%)
    ppermute x37, waiting for transfers between devices, turn(): lax.ppermute(value, axis, [(i, (i + step) % size) for i in range(size)])  192 us
    all_to_all x7, waiting for transfers between devices, exchange(): return lax.all_to_all(parts, axes, 0, 0)  98.2 us
    ppermute x37, starting transfers between devices, turn(): lax.ppermute(value, axis, [(i, (i + step) % size) for i in range(size)])  40.5 us
    all_to_all x7, starting transfers between devices, exchange(): return lax.all_to_all(parts, axes, 0, 0)  34.5 us
    unnamed x157, local copies, waits for them, and re-layouts  27.1 us
    pallas_call x1, Pallas kernels, feed_forward(): pl.pallas_call(feed_kernel, grid=(count // tile,), out_shape=(shape((coun...  25.6 us
    pallas_call x1, Pallas kernels, attend_back(): pl.pallas_call(attend_back_kernel, out_shape=(shape(query.shape, BF16), s...  23.1 us
    reduce_scatter x1, waiting for transfers between devices, shards(): lax.psum_scatter(back, ('y', 'z'), scatter_dimension=0, tiled=True)  21.9 us
  transfers between devices with their start and end apart: 53, of which 25 were waited for; matrix products, arithmetic and copies ran while one was open for 18% of the time, Pallas kernels for 8%

profile of v4, /device:TPU:0, one launch (start us, length us, event | category | flops | bytes accessed | tf_op | source)
XLA Modules:
  0.0 653.3 jit_solution(1179016717329388758)
XLA Ops:
  17.4 6.6 %all-to-all-start = ((bf16[16,240,256]{2,1,0:T(8,128)(2,1)}), bf16[16,240,256]{2,1,0:T(8,128)(2,1)}, u32[]{:S(2)}, u32[]{:S(2)}) async-start(bf16[16,240,256]{2,1,0:T(8,128)(2,1)} %broadcast_dynamic-update-slice_fusion), calls=%async_computation | async-start | bytes 3932160 | tf_op jit(solution)/shard_map/all_to_all | solution.py:39
  28.6 36.8 %all-to-all-done = bf16[16,240,256]{2,1,0:T(8,128)(2,1)} async-done(((bf16[16,240,256]{2,1,0:T(8,128)(2,1)}), bf16[16,240,256]{2,1,0:T(8,128)(2,1)}, u32[]{:S(2)}, u32[]{:S(2)}) %all-to-all-start) | async-done | bytes 1966112 | tf_op jit(solution)/shard_map/all_to_all | solution.py:39
  65.3 2.1 fusion.34
  71.2 5.5 all-gather.6.cloned.1.call-done
  76.7 4.0 fusion.36
  92.7 9.2 %collective-permute-done.1.lane_d = bf16[128,1024]{1,0:T(8,128)(2,1)S(1)} collective-permute-done((bf16[128,1024]{1,0:T(8,128)(2,1)S(1)}, bf16[128,1024]{1,0:T(8,128)(2,1)S(1)}, u32[]{:S(2)}, u32[]{:S(2)}) %collective-permute-start.1) | collective-permute-done | bytes 262176 | tf_op jit(solution)/shard_map/lane/ppermute | solution.py:22
  105.7 16.5 %collective-permute-done.3.across_ref.proj_b = bf16[256,2048]{1,0:T(8,128)(2,1)S(1)} collective-permute-done((bf16[256,2048]{1,0:T(8,128)(2,1)S(1)}, bf16[256,2048]{1,0:T(8,128)(2,1)S(1)}, u32[]{:S(2)}, u32[]{:S(2)}) %collective-permute-start.3) | collective-permute-done | bytes 1048608 | tf_op jit(solution)/shard_map/out_chip/ppermute | solution.py:22
  128.9 7.1 %attend.1 = (bf16[4,128,1024]{2,1,0:T(8,128)(2,1)S(1)}, f32[4,1,512]{2,1,0:T(1,128)S(1)}) custom-call(s32[10]{0:T(128)S(1)} %pad_add_fusion.meta, bf16[4,128,1024]{2,1,0:T(8,128)(2,1)S(1)} %make_queries.1.q_ref, bf16[2048,512]{1,0:T(8,128)(2,1)S(1)} %copy-done.19, s32[4,1,128]{2,1,0:T(1,128)S(1)} %iota_add_fusion.place_ref, s32[4,1,128]{2,1,0:T(1,128)S(1)} %bitcast.151), custom_call_target="tpu_custom_call" | custom-call | flops 20000000000 | bytes 5000000 | tf_op jit(solution)/shard_map/attend/pallas_call | solution.py:414
  138.9 2.9 project.1.part_ref
  142.9 3.2 collective-permute-start.9
  146.1 34.3 %collective-permute-done.8.low_ref = bf16[64,2048]{1,0:T(8,128)(2,1)} collective-permute-done((bf16[64,2048]{1,0:T(8,128)(2,1)S(1)}, bf16[64,2048]{1,0:T(8,128)(2,1)}, u32[]{:S(2)}, u32[]{:S(2)}) %collective-permute-start.8) | collective-permute-done | bytes 262176 | tf_op jit(solution)/shard_map/residual/ppermute | solution.py:22
  180.4 2.4 ring_merge.1
  182.8 3.2 collective-permute-start.11
  186.8 11.3 %collective-permute-done.10 = bf16[128,2048]{1,0:T(8,128)(2,1)S(1)} collective-permute-done((bf16[128,2048]{1,0:T(8,128)(2,1)}, bf16[128,2048]{1,0:T(8,128)(2,1)S(1)}, u32[]{:S(2)}, u32[]{:S(2)}) %collective-permute-start.10) | collective-permute-done | bytes 524320 | tf_op jit(solution)/shard_map/residual/ppermute | solution.py:22
  204.9 2.8 collective-permute-start.12
  207.7 16.2 %collective-permute-done.12 = bf16[1536,256]{1,0:T(8,128)(2,1)S(1)} collective-permute-done((bf16[1536,256]{1,0:T(8,128)(2,1)S(1)}, bf16[1536,256]{1,0:T(8,128)(2,1)S(1)}, u32[]{:S(2)}, u32[]{:S(2)}) %collective-permute-start.12) | collective-permute-done | bytes 786464 | tf_op jit(solution)/shard_map/feed_weights/ppermute | solution.py:22
  223.9 3.8 collective-permute-start.13
  228.8 2.2 broadcast_in_dim.43
  231.9 2.7 collective-permute-done.13
  236.4 2.7 collective-permute-done.15
  240.9 2.1 copy_dynamic-update-slice_fusion
  246.3 4.6 collective-permute-done.17
  252.1 2.1 pad_maximum_fusion.down_ref
  255.6 25.6 %feed_forward.1 = (bf16[1024,768]{1,0:T(8,128)(2,1)S(1)}, bf16[1024,768]{1,0:T(8,128)(2,1)}, bf16[1024,768]{1,0:T(8,128)(2,1)}, bf16[1024,2048]{1,0:T(8,128)(2,1)}) custom-call(bf16[1024,2048]{1,0:T(8,128)(2,1)} %all-gather.10.cloned.1.call-done.n_ref, bf16[1024,2048]{1,0:T(8,128)(2,1)} %all-gather.12.cloned.1.call-done.cot_ref, ...), custom_call_target="tpu_custom_call" | custom-call | flops 19000000512 | bytes 32000000 | tf_op jit(solution)/shard_map/feed_forward/pallas_call | solution.py:664
  281.2 6.3 convolution_convert_fusion.1
  287.7 2.4 convolution_convert_fusion.3
  290.8 2.4 convolution_convert_fusion.4.down_ref
  293.3 3.8 convolution_convert_fusion.2.feed_ref
  298.6 2.1 copy-done
  300.8 5.6 convolution_convert_fusion
  311.4 21.9 %reduce-scatter.5.cloned.1.call-done = bf16[128,2048]{1,0:T(8,128)(2,1)} async-done(((bf16[1024,2048]{1,0:T(8,128)(2,1)}), bf16[128,2048]{1,0:T(8,128)(2,1)}) %reduce-scatter.5.cloned.1.call-update) | async-done | bytes 524304 | tf_op jit(solution)/shard_map/reduce_scatter | solution.py:838
  334.9 2.5 fusion.32
  341.3 9.8 %collective-permute-done.21.branch_d = bf16[128,2048]{1,0:T(8,128)(2,1)S(1)} collective-permute-done((bf16[128,2048]{1,0:T(8,128)(2,1)S(1)}, bf16[128,2048]{1,0:T(8,128)(2,1)S(1)}, u32[]{:S(2)}, u32[]{:S(2)}) %collective-permute-start.21) | collective-permute-done | bytes 524320 | tf_op jit(solution)/shard_map/branch/ppermute | solution.py:22
  353.4 3.1 add_bitcast_fusion
  358.6 2.4 collective-permute-done.24.branch_c
  361.0 23.1 %attend_back.1 = (bf16[4,128,1024]{2,1,0:T(8,128)(2,1)}, bf16[4,128,1024]{2,1,0:T(8,128)(2,1)}, bf16[8,128,512]{2,1,0:T(8,128)(2,1)}, bf16[8,128,512]{2,1,0:T(8,...) custom-call(s32[10]{0:T(128)S(1)} %pad_add_fusion.meta, ...), custom_call_target="tpu_custom_call" | custom-call | flops 24000000000 | bytes 20000000 | tf_op jit(solution)/shard_map/attend_back/pallas_call | solution.py:682
  384.7 18.3 %collective-permute-done.20 = bf16[512,2048]{1,0:T(8,128)(2,1)} collective-permute-done((bf16[512,2048]{1,0:T(8,128)(2,1)}, bf16[512,2048]{1,0:T(8,128)(2,1)}, u32[]{:S(2)}, u32[]{:S(2)}) %collective-permute-start.20) | collective-permute-done | bytes 2097184 | tf_op jit(solution)/shard_map/layer_out/ppermute | solution.py:22
  406.8 2.5 add_convert_fusion.1
  409.3 4.4 all-to-all-start.1
  413.8 12.7 %all-to-all-done.1 = bf16[8,128,512]{2,1,0:T(8,128)(2,1)} async-done(((bf16[8,128,512]{2,1,0:T(8,128)(2,1)}), bf16[8,128,512]{2,1,0:T(8,128)(2,1)}, u32[]{:S(2)}, u32[]{:S(2)}) %all-to-all-start.1) | async-done | bytes 1048608 | tf_op jit(solution)/shard_map/kv_grad/all_to_all | solution.py:39
  430.3 4.3 pack_heads.1
  434.7 6.8 %all-to-all-start.2 = ((bf16[16,48,2048]{2,1,0:T(8,128)(2,1)}), bf16[16,48,2048]{2,1,0:T(8,128)(2,1)}, u32[]{:S(2)}, u32[]{:S(2)}) async-start(bf16[16,48,2048]{2,1,0:T(8,128)(2,1)} %pack_heads.1), calls=%async_computation.6 | async-start | bytes 6291456 | tf_op jit(solution)/shard_map/heads_grad/all_to_all | solution.py:39
  443.6 4.5 fusion.2
  449.5 3.5 collective-permute-start.36
  453.0 54.5 %collective-permute-done.36 = bf16[512,1152]{1,0:T(8,128)(2,1)S(1)} collective-permute-done((bf16[512,1152]{1,0:T(8,128)(2,1)S(1)}, bf16[512,1152]{1,0:T(8,128)(2,1)S(1)}, u32[]{:S(2)}, u32[]{:S(2)}) %collective-permute-start.36) | collective-permute-done | bytes 1179680 | tf_op jit(solution)/shard_map/feed_grad/ppermute | solution.py:22
  512.8 3.6 all-to-all-start.3
  517.6 12.5 %all-to-all-done.3 = bf16[16,32,768]{2,1,0:T(8,128)(2,1)S(1)} async-done(((bf16[16,32,768]{2,1,0:T(8,128)(2,1)}), bf16[16,32,768]{2,1,0:T(8,128)(2,1)S(1)}, u32[]{:S(2)}, u32[]{:S(2)}) %all-to-all-start.3) | async-done | bytes 786464 | tf_op jit(solution)/shard_map/feed_grad/all_to_all | solution.py:39
  539.6 2.1 collective-permute-start.29
  542.1 4.6 collective-permute-done.31.g_d
  546.7 4.3 collective-permute-start.32
  551.6 3.7 fusion
  555.4 3.1 collective-permute-done.34.g_c
  559.6 2.7 fusion.11
  569.1 5.0 all-to-all-start.4
  574.1 2.5 reduce_sum.111
  576.6 16.4 %all-to-all-done.4 = bf16[16,16,1536]{2,1,0:T(8,128)(2,1)S(1)} async-done(((bf16[16,16,1536]{2,1,0:T(8,128)(2,1)}), bf16[16,16,1536]{2,1,0:T(8,128)(2,1)S(1)}, u32[]{:S(2)}, u32[]{:S(2)}) %all-to-all-start.4) | async-done | bytes 786464 | tf_op jit(solution)/shard_map/all_to_all | solution.py:39
  595.0 3.5 all-to-all-start.5
  598.5 6.1 all-to-all-done.5
  606.2 4.7 all-to-all-start.6
  611.0 2.4 add_convert_fusion.3
  613.3 2.3 copy-done.3
  617.0 5.0 spill.1
  625.8 13.8 %all-to-all-done.6.last_ref = bf16[8,64,2048]{2,1,0:T(8,128)(2,1)S(1)} async-done(((bf16[8,64,2048]{2,1,0:T(8,128)(2,1)}), bf16[8,64,2048]{2,1,0:T(8,128)(2,1)S(1)}, u32[]{:S(2)}, u32[]{:S(2)}) %all-to-all-start.6) | async-done | bytes 2097184 | tf_op jit(solution)/shard_map/heads_sum/all_to_all | solution.py:39
  642.4 2.1 finish.1
  (355 shorter events, 118.0 us)
Async XLA Ops:
  7.2 69.5 %all-gather.6.cloned.1.call-start = ((), (), s32[]{:S(2)}) async-start(), calls=%async_computation.11 | async-start | bytes 6684672 | tf_op jit(solution)/shard_map/all_gather | solution.py:731
  17.4 47.9 %all-to-all-start = ((bf16[16,240,256]{2,1,0:T(8,128)(2,1)}), bf16[16,240,256]{2,1,0:T(8,128)(2,1)}, u32[]{:S(2)}, u32[]{:S(2)}) async-start(bf16[16,240,256]{2,1,0:T(8,128)(2,1)} %broadcast_dynamic-update-slice_fusion), calls=%async_computation | async-start | bytes 3932160 | tf_op jit(solution)/shard_map/all_to_all | solution.py:39
  24.0 103.3 %all-gather.8.cloned.1.call-start = ((), (), s32[]{:S(2)}) async-start(), calls=%async_computation.12 | async-start | bytes 2228224 | tf_op jit(solution)/shard_map/all_gather | solution.py:801
  24.0 3.3 collective-permute-start
  25.2 44.2 %copy-start.55 = (s32[4]{0:T(128)}, s32[4]{0:T(128)S(1)}, u32[]{:S(2)}) copy-start(s32[4]{0:T(128)S(1)} %get-tuple-element.117) | copy-start | bytes 52
  26.3 44.9 %copy-start.57 = (f32[128]{0:T(128)}, f32[128]{0:T(128)S(1)}, u32[]{:S(2)}) copy-start(f32[128]{0:T(128)S(1)} %get-tuple-element.136) | copy-start | bytes 1540
  27.3 53.3 %copy-start.20 = (bf16[256,2048]{1,0:T(8,128)(2,1)}, bf16[256,2048]{1,0:T(8,128)(2,1)S(1)}, u32[]{:S(2)}) copy-start(bf16[256,2048]{1,0:T(8,128)(2,1)S(1)} %collective-permute-done.sib_ref.proj_c) | copy-start | bytes 3145732
  81.4 172.7 %all-gather.12.cloned.1.call-start = ((), (), s32[]{:S(2)}) async-start(), calls=%async_computation.14 | async-start | bytes 4718592 | tf_op jit(solution)/shard_map/all_gather | solution.py:814
  84.6 171.0 %all-gather.10.cloned.1.call-start = ((), (), s32[]{:S(2)}) async-start(), calls=%async_computation.13 | async-start | bytes 4718592 | tf_op jit(solution)/shard_map/all_gather | solution.py:822
  85.7 17.6 %collective-permute-start.6 = (bf16[1024,512]{1,0:T(8,128)(2,1)}, bf16[1024,512]{1,0:T(8,128)(2,1)}, u32[]{:S(2)}, u32[]{:S(2)}) collective-permute-start(bf16[1024,512]{1,0:T(8,128)(2,1)} %pad_maximum_fusion.3), channel_id=1, source_target_pairs={{0,1},{1,0},{2,3},{3,2},{4,5},{5,4},{6,7},{7,6},{8,9},{9,8},{10,11... | collective-permute-start | bytes 3145736 | tf_op jit(solution)/shard_map/ppermute | solution.py:22
  86.9 35.2 %collective-permute-start.3 = (bf16[256,2048]{1,0:T(8,128)(2,1)S(1)}, bf16[256,2048]{1,0:T(8,128)(2,1)S(1)}, u32[]{:S(2)}, u32[]{:S(2)}) collective-permute-start(bf16[256,2048]{1,0:T(8,128)(2,1)S(1)} %broadcast_add_fusion.3), channel_id=1, source_target_pairs={{0,8},{8,0},{1,9},{9,1},{2,10},{10,2},{3,11},{11,3},{4,12},{12,4},... | collective-permute-start | bytes 3145736 | tf_op jit(solution)/shard_map/out_chip/ppermute | solution.py:22
  90.3 11.7 %collective-permute-start.1 = (bf16[128,1024]{1,0:T(8,128)(2,1)S(1)}, bf16[128,1024]{1,0:T(8,128)(2,1)S(1)}, u32[]{:S(2)}, u32[]{:S(2)}) collective-permute-start(bf16[128,1024]{1,0:T(8,128)(2,1)S(1)} %multiply_convert_fusion.1.lane_a), channel_id=1, source_target_pairs={{0,6},{2,0},{4,2},{6,4},{1,7},{3,1},{5,3},{7,5},{8,14},{10,8},{12,... | collective-permute-start | bytes 786440 | tf_op jit(solution)/shard_map/lane/ppermute | solution.py:22
  92.1 12.7 %collective-permute-start.4 = (bf16[128,1024]{1,0:T(8,128)(2,1)S(1)}, bf16[128,1024]{1,0:T(8,128)(2,1)S(1)}, u32[]{:S(2)}, u32[]{:S(2)}) collective-permute-start(bf16[128,1024]{1,0:T(8,128)(2,1)S(1)} %multiply_convert_fusion.1.lane_a), channel_id=1, source_target_pairs={{0,2},{2,4},{4,6},{6,0},{1,3},{3,5},{5,7},{7,1},{8,10},{10,12},{12... | collective-permute-start | bytes 786440 | tf_op jit(solution)/shard_map/lane/ppermute | solution.py:22
  102.0 21.4 %collective-permute-start.2 = (bf16[64,1024]{1,0:T(8,128)(2,1)S(1)}, bf16[64,1024]{1,0:T(8,128)(2,1)S(1)}, u32[]{:S(2)}, u32[]{:S(2)}) collective-permute-start(bf16[64,1024]{1,0:T(8,128)(2,1)S(1)} %slice.309), channel_id=1, source_target_pairs={{0,6},{2,0},{4,2},{6,4},{1,7},{3,1},{5,3},{7,5},{8,14},{10,8},{12,... | collective-permute-start | bytes 393224 | tf_op jit(solution)/shard_map/lane/ppermute | solution.py:22
  104.8 20.0 %copy-start.1 = (bf16[1024,1024]{1,0:T(8,128)(2,1)}, bf16[1024,1024]{1,0:T(8,128)(2,1)S(1)}, u32[]{:S(2)}) copy-start(bf16[1024,1024]{1,0:T(8,128)(2,1)S(1)} %pad_maximum_fusion.1.up_ref) | copy-start | bytes 6291460
  104.8 18.5 %collective-permute-start.5 = (bf16[64,1024]{1,0:T(8,128)(2,1)S(1)}, bf16[64,1024]{1,0:T(8,128)(2,1)S(1)}, u32[]{:S(2)}, u32[]{:S(2)}) collective-permute-start(bf16[64,1024]{1,0:T(8,128)(2,1)S(1)} %slice.312), channel_id=1, source_target_pairs={{0,2},{2,4},{4,6},{6,0},{1,3},{3,5},{5,7},{7,1},{8,10},{10,12},{12... | collective-permute-start | bytes 393224 | tf_op jit(solution)/shard_map/lane/ppermute | solution.py:22
  127.0 9.6 %collective-permute-start.7 = (bf16[256,2048]{1,0:T(8,128)(2,1)}, bf16[256,2048]{1,0:T(8,128)(2,1)S(1)}, u32[]{:S(2)}, u32[]{:S(2)}) collective-permute-start(bf16[256,2048]{1,0:T(8,128)(2,1)} %broadcast_add_fusion.2), channel_id=1, source_target_pairs={{0,1},{1,0},{2,3},{3,2},{4,5},{5,4},{6,7},{7,6},{8,9},{9,8},{10,11... | collective-permute-start | bytes 3145736 | tf_op jit(solution)/shard_map/out_chip/ppermute | solution.py:22
  142.8 37.6 %copy-start.2 = (bf16[4,128,2048]{2,1,0:T(8,128)(2,1)}, bf16[4,128,2048]{2,1,0:T(8,128)(2,1)S(1)}, u32[]{:S(2)}) copy-start(bf16[4,128,2048]{2,1,0:T(8,128)(2,1)S(1)} %project.1.part_ref) | copy-start | bytes 6291460
  142.8 37.6 %collective-permute-start.8 = (bf16[64,2048]{1,0:T(8,128)(2,1)S(1)}, bf16[64,2048]{1,0:T(8,128)(2,1)}, u32[]{:S(2)}, u32[]{:S(2)}) collective-permute-start(bf16[64,2048]{1,0:T(8,128)(2,1)S(1)} %get-tuple-element.120), channel_id=1, source_target_pairs={{0,2},{2,4},{4,6},{6,0},{1,3},{3,5},{5,7},{7,1},{8,10},{10,12},{12... | collective-permute-start | bytes 786440 | tf_op jit(solution)/shard_map/residual/ppermute | solution.py:22
  142.9 37.5 %collective-permute-start.9 = (bf16[64,2048]{1,0:T(8,128)(2,1)S(1)}, bf16[64,2048]{1,0:T(8,128)(2,1)}, u32[]{:S(2)}, u32[]{:S(2)}) collective-permute-start(bf16[64,2048]{1,0:T(8,128)(2,1)S(1)} %get-tuple-element.119), channel_id=1, source_target_pairs={{0,6},{2,0},{4,2},{6,4},{1,7},{3,1},{5,3},{7,5},{8,14},{10,8},{12,... | collective-permute-start | bytes 786440 | tf_op jit(solution)/shard_map/residual/ppermute | solution.py:22
  182.8 15.3 %collective-permute-start.10 = (bf16[128,2048]{1,0:T(8,128)(2,1)}, bf16[128,2048]{1,0:T(8,128)(2,1)S(1)}, u32[]{:S(2)}, u32[]{:S(2)}) collective-permute-start(bf16[128,2048]{1,0:T(8,128)(2,1)} %get-tuple-element.82), channel_id=1, source_target_pairs={{0,2},{2,4},{4,6},{6,0},{1,3},{3,5},{5,7},{7,1},{8,10},{10,12},{12... | collective-permute-start | bytes 1572872 | tf_op jit(solution)/shard_map/residual/ppermute | solution.py:22
  182.8 15.3 %collective-permute-start.11 = (bf16[128,2048]{1,0:T(8,128)(2,1)}, bf16[128,2048]{1,0:T(8,128)(2,1)S(1)}, u32[]{:S(2)}, u32[]{:S(2)}) collective-permute-start(bf16[128,2048]{1,0:T(8,128)(2,1)} %get-tuple-element.83), channel_id=1, source_target_pairs={{0,6},{2,0},{4,2},{6,4},{1,7},{3,1},{5,3},{7,5},{8,14},{10,8},{12,... | collective-permute-start | bytes 1572872 | tf_op jit(solution)/shard_map/residual/ppermute | solution.py:22
  201.8 131.4 %reduce-scatter.5.cloned.1.call-start = ((), (), s32[]{:S(2)}) async-start(), calls=%async_computation.15 | async-start | bytes 4718592 | tf_op jit(solution)/shard_map/reduce_scatter | solution.py:838
  204.9 19.0 %collective-permute-start.12 = (bf16[1536,256]{1,0:T(8,128)(2,1)S(1)}, bf16[1536,256]{1,0:T(8,128)(2,1)S(1)}, u32[]{:S(2)}, u32[]{:S(2)}) collective-permute-start(bf16[1536,256]{1,0:T(8,128)(2,1)S(1)} %bitcast.163), channel_id=1, source_target_pairs={{0,48},{16,0},{32,16},{48,32},{1,49},{17,1},{33,17},{49,33},{2,50}... | collective-permute-start | bytes 2359304 | tf_op jit(solution)/shard_map/feed_weights/ppermute | solution.py:22
  207.7 20.0 %collective-permute-start.14 = (bf16[1536,256]{1,0:T(8,128)(2,1)S(1)}, bf16[1536,256]{1,0:T(8,128)(2,1)}, u32[]{:S(2)}, u32[]{:S(2)}) collective-permute-start(bf16[1536,256]{1,0:T(8,128)(2,1)S(1)} %bitcast.164), channel_id=1, source_target_pairs={{0,16},{16,32},{32,48},{48,0},{1,17},{17,33},{33,49},{49,1},{2,18}... | collective-permute-start | bytes 2359304 | tf_op jit(solution)/shard_map/feed_weights/ppermute | solution.py:22
  223.9 10.7 %collective-permute-start.13 = (bf16[768,256]{1,0:T(8,128)(2,1)S(1)}, bf16[768,256]{1,0:T(8,128)(2,1)}, u32[]{:S(2)}, u32[]{:S(2)}) collective-permute-start(bf16[768,256]{1,0:T(8,128)(2,1)S(1)} %slice.326), channel_id=1, source_target_pairs={{0,48},{16,0},{32,16},{48,32},{1,49},{17,1},{33,17},{49,33},{2,50}... | collective-permute-start | bytes 1179656 | tf_op jit(solution)/shard_map/feed_weights/ppermute | solution.py:22
  228.7 10.4 %collective-permute-start.15 = (bf16[768,256]{1,0:T(8,128)(2,1)S(1)}, bf16[768,256]{1,0:T(8,128)(2,1)S(1)}, u32[]{:S(2)}, u32[]{:S(2)}) collective-permute-start(bf16[768,256]{1,0:T(8,128)(2,1)S(1)} %slice.327), channel_id=1, source_target_pairs={{0,16},{16,32},{32,48},{48,0},{1,17},{17,33},{33,49},{49,1},{2,18}... | collective-permute-start | bytes 1179656 | tf_op jit(solution)/shard_map/feed_weights/ppermute | solution.py:22
  243.0 11.2 %collective-permute-start.16 = (bf16[3,2048,256]{2,1,0:T(8,128)(2,1)}, bf16[3,2048,256]{2,1,0:T(8,128)(2,1)}, u32[]{:S(2)}, u32[]{:S(2)}) collective-permute-start(bf16[3,2048,256]{2,1,0:T(8,128)(2,1)} %bitcast.54.own_ref), channel_id=1, source_target_pairs={{0,1},{1,0},{2,3},{3,2},{4,5},{5,4},{6,7},{7,6},{8,9},{9,8},{10,11... | collective-permute-start | bytes 9437192 | tf_op jit(solution)/shard_map/feed_weights/ppermute | solution.py:22
  245.3 5.6 collective-permute-start.17
  281.2 123.1 %reduce-scatter.7.cloned.1.call-start = ((), (), s32[]{:S(2)}) async-start(), calls=%async_computation.16 | async-start | bytes 5898240 | tf_op jit(solution)/shard_map/feed_grad/reduce_scatter | solution.py:848
  287.6 9.4 %collective-permute-start.18 = (bf16[2048,768]{1,0:T(8,128)(2,1)S(1)}, bf16[2048,768]{1,0:T(8,128)(2,1)S(1)}, u32[]{:S(2)}, u32[]{:S(2)}) collective-permute-start(bf16[2048,768]{1,0:T(8,128)(2,1)S(1)} %convolution_convert_fusion.1), channel_id=1, source_target_pairs={{0,1},{1,0},{2,3},{3,2},{4,5},{5,4},{6,7},{7,6},{8,9},{9,8},{10,11... | collective-permute-start | bytes 9437192 | tf_op jit(solution)/shard_map/feed_grad/ppermute | solution.py:22
  290.1 6.9 %collective-permute-start.19 = (bf16[2048,384]{1,0:T(8,128)(2,1)S(1)}, bf16[2048,384]{1,0:T(8,128)(2,1)S(1)}, u32[]{:S(2)}, u32[]{:S(2)}) collective-permute-start(bf16[2048,384]{1,0:T(8,128)(2,1)S(1)} %convolution_convert_fusion.3), channel_id=1, source_target_pairs={{0,1},{1,0},{2,3},{3,2},{4,5},{5,4},{6,7},{7,6},{8,9},{9,8},{10,11... | collective-permute-start | bytes 4718600 | tf_op jit(solution)/shard_map/feed_grad/ppermute | solution.py:22
  300.7 34.2 %copy-start.42 = (bf16[128,2048]{1,0:T(8,128)(2,1)S(1)}, bf16[128,2048]{1,0:T(8,128)(2,1)}, u32[]{:S(2)}) copy-start(bf16[128,2048]{1,0:T(8,128)(2,1)} %param.33) | copy-start | bytes 1572868
  300.7 230.7 %reduce-scatter.11.cloned.1.call-start = ((), (), s32[]{:S(2)}) async-start(), calls=%async_computation.18 | async-start | bytes 1310720 | tf_op jit(solution)/shard_map/latent_grad/reduce_scatter | solution.py:905
  308.3 26.6 %copy-start.29 = (f32[128,2048]{1,0:T(8,128)S(1)}, f32[128,2048]{1,0:T(8,128)}, u32[]{:S(2)}) copy-start(f32[128,2048]{1,0:T(8,128)} %copy-done.28) | copy-start | bytes 3145732
  337.5 13.7 %collective-permute-start.21 = (bf16[128,2048]{1,0:T(8,128)(2,1)S(1)}, bf16[128,2048]{1,0:T(8,128)(2,1)S(1)}, u32[]{:S(2)}, u32[]{:S(2)}) collective-permute-start(bf16[128,2048]{1,0:T(8,128)(2,1)S(1)} %get-tuple-element.113.branch_a), channel_id=1, source_target_pairs={{0,6},{2,0},{4,2},{6,4},{1,7},{3,1},{5,3},{7,5},{8,14},{10,8},{12,... | collective-permute-start | bytes 1572872 | tf_op jit(solution)/shard_map/branch/ppermute | solution.py:22
  337.9 14.9 %collective-permute-start.23 = (bf16[128,2048]{1,0:T(8,128)(2,1)S(1)}, bf16[128,2048]{1,0:T(8,128)(2,1)S(1)}, u32[]{:S(2)}, u32[]{:S(2)}) collective-permute-start(bf16[128,2048]{1,0:T(8,128)(2,1)S(1)} %get-tuple-element.113.branch_a), channel_id=1, source_target_pairs={{0,2},{2,4},{4,6},{6,0},{1,3},{3,5},{5,7},{7,1},{8,10},{10,12},{12... | collective-permute-start | bytes 1572872 | tf_op jit(solution)/shard_map/branch/ppermute | solution.py:22
  351.2 7.4 %collective-permute-start.22 = (bf16[64,2048]{1,0:T(8,128)(2,1)S(1)}, bf16[64,2048]{1,0:T(8,128)(2,1)S(1)}, u32[]{:S(2)}, u32[]{:S(2)}) collective-permute-start(bf16[64,2048]{1,0:T(8,128)(2,1)S(1)} %slice.332), channel_id=1, source_target_pairs={{0,6},{2,0},{4,2},{6,4},{1,7},{3,1},{5,3},{7,5},{8,14},{10,8},{12,... | collective-permute-start | bytes 786440 | tf_op jit(solution)/shard_map/branch/ppermute | solution.py:22
  352.8 8.2 %collective-permute-start.24 = (bf16[64,2048]{1,0:T(8,128)(2,1)S(1)}, bf16[64,2048]{1,0:T(8,128)(2,1)S(1)}, u32[]{:S(2)}, u32[]{:S(2)}) collective-permute-start(bf16[64,2048]{1,0:T(8,128)(2,1)S(1)} %slice.333), channel_id=1, source_target_pairs={{0,2},{2,4},{4,6},{6,0},{1,3},{3,5},{5,7},{7,1},{8,10},{10,12},{12... | collective-permute-start | bytes 786440 | tf_op jit(solution)/shard_map/branch/ppermute | solution.py:22
  356.5 46.5 %collective-permute-start.20 = (bf16[512,2048]{1,0:T(8,128)(2,1)}, bf16[512,2048]{1,0:T(8,128)(2,1)}, u32[]{:S(2)}, u32[]{:S(2)}) collective-permute-start(bf16[512,2048]{1,0:T(8,128)(2,1)} %add_bitcast_fusion), channel_id=1, source_target_pairs={{0,8},{8,0},{1,9},{9,1},{2,10},{10,2},{3,11},{11,3},{4,12},{12,4},... | collective-permute-start | bytes 6291464 | tf_op jit(solution)/shard_map/layer_out/ppermute | solution.py:22
  384.1 22.7 %collective-permute-start.25 = (bf16[8,128,512]{2,1,0:T(8,128)(2,1)}, bf16[8,128,512]{2,1,0:T(8,128)(2,1)S(1)}, u32[]{:S(2)}, u32[]{:S(2)}) collective-permute-start(bf16[8,128,512]{2,1,0:T(8,128)(2,1)} %get-tuple-element.90), channel_id=1, source_target_pairs={{0,1},{1,0},{2,3},{3,2},{4,5},{5,4},{6,7},{7,6},{8,9},{9,8},{10,11... | collective-permute-start | bytes 3145736 | tf_op jit(solution)/shard_map/kv_grad/ppermute | solution.py:22
  384.2 44.9 %collective-permute-start.26 = (bf16[512,2048]{1,0:T(8,128)(2,1)}, bf16[512,2048]{1,0:T(8,128)(2,1)}, u32[]{:S(2)}, u32[]{:S(2)}) collective-permute-start(bf16[512,2048]{1,0:T(8,128)(2,1)} %get-tuple-element.92), channel_id=1, source_target_pairs={{0,1},{1,0},{2,3},{3,2},{4,5},{5,4},{6,7},{7,6},{8,9},{9,8},{10,11... | collective-permute-start | bytes 6291464 | tf_op jit(solution)/shard_map/heads_grad/ppermute | solution.py:22
  409.3 19.8 %copy-start.6 = (bf16[512,2048]{1,0:T(8,128)(2,1)S(1)}, bf16[512,2048]{1,0:T(8,128)(2,1)}, u32[]{:S(2)}) copy-start(bf16[512,2048]{1,0:T(8,128)(2,1)} %get-tuple-element.91.out_ref) | copy-start | bytes 6291460
  409.3 17.2 %all-to-all-start.1 = ((bf16[8,128,512]{2,1,0:T(8,128)(2,1)}), bf16[8,128,512]{2,1,0:T(8,128)(2,1)}, u32[]{:S(2)}, u32[]{:S(2)}) async-start(bf16[8,128,512]{2,1,0:T(8,128)(2,1)} %add_convert_fusion.1), calls=%async_computation.3 | async-start | bytes 2097152 | tf_op jit(solution)/shard_map/kv_grad/all_to_all | solution.py:39
  413.7 15.4 %collective-permute-start.27 = (bf16[1024,512]{1,0:T(8,128)(2,1)}, bf16[1024,512]{1,0:T(8,128)(2,1)}, u32[]{:S(2)}, u32[]{:S(2)}) collective-permute-start(bf16[1024,512]{1,0:T(8,128)(2,1)} %get-tuple-element.94), channel_id=1, source_target_pairs={{0,1},{1,0},{2,3},{3,2},{4,5},{5,4},{6,7},{7,6},{8,9},{9,8},{10,11... | collective-permute-start | bytes 3145736 | tf_op jit(solution)/shard_map/heads_grad/ppermute | solution.py:22
  434.7 74.2 %all-to-all-start.2 = ((bf16[16,48,2048]{2,1,0:T(8,128)(2,1)}), bf16[16,48,2048]{2,1,0:T(8,128)(2,1)}, u32[]{:S(2)}, u32[]{:S(2)}) async-start(bf16[16,48,2048]{2,1,0:T(8,128)(2,1)} %pack_heads.1), calls=%async_computation.6 | async-start | bytes 6291456 | tf_op jit(solution)/shard_map/heads_grad/all_to_all | solution.py:39
  441.4 169.5 %reduce-scatter.9.cloned.1.call-start = ((), (), s32[]{:S(2)}) async-start(), calls=%async_computation.17 | async-start | bytes 2621440 | tf_op jit(solution)/shard_map/layer_out/reduce_scatter | solution.py:891
  449.5 58.0 %collective-permute-start.36 = (bf16[512,1152]{1,0:T(8,128)(2,1)S(1)}, bf16[512,1152]{1,0:T(8,128)(2,1)S(1)}, u32[]{:S(2)}, u32[]{:S(2)}) collective-permute-start(bf16[512,1152]{1,0:T(8,128)(2,1)S(1)} %broadcast_add_fusion.1), channel_id=1, source_target_pairs={{0,64},{64,0},{1,65},{65,1},{2,66},{66,2},{3,67},{67,3},{4,68},{68... | collective-permute-start | bytes 3538952 | tf_op jit(solution)/shard_map/feed_grad/ppermute | solution.py:22
  512.8 17.3 %all-to-all-start.3 = ((bf16[16,32,768]{2,1,0:T(8,128)(2,1)}), bf16[16,32,768]{2,1,0:T(8,128)(2,1)S(1)}, u32[]{:S(2)}, u32[]{:S(2)}) async-start(bf16[16,32,768]{2,1,0:T(8,128)(2,1)} %slice_add_fusion), calls=%async_computation.7 | async-start | bytes 1572864 | tf_op jit(solution)/shard_map/feed_grad/all_to_all | solution.py:39
  516.4 96.9 %all-gather.14.cloned.1.call-start = ((), (), s32[]{:S(2)}) async-start(), calls=%async_computation.19 | async-start | bytes 5898240 | tf_op jit(solution)/shard_map/feed_grad/all_gather | solution.py:900
  534.4 12.3 %collective-permute-start.31 = (bf16[128,1536]{1,0:T(8,128)(2,1)S(1)}, bf16[128,1536]{1,0:T(8,128)(2,1)S(1)}, u32[]{:S(2)}, u32[]{:S(2)}) collective-permute-start(bf16[128,1536]{1,0:T(8,128)(2,1)S(1)} %pad_maximum_fusion.5.g_a), channel_id=1, source_target_pairs={{0,6},{2,0},{4,2},{6,4},{1,7},{3,1},{5,3},{7,5},{8,14},{10,8},{12,... | collective-permute-start | bytes 1179656 | tf_op jit(solution)/shard_map/first_lane/ppermute | solution.py:22
  535.4 16.0 %collective-permute-start.33 = (bf16[128,1536]{1,0:T(8,128)(2,1)S(1)}, bf16[128,1536]{1,0:T(8,128)(2,1)S(1)}, u32[]{:S(2)}, u32[]{:S(2)}) collective-permute-start(bf16[128,1536]{1,0:T(8,128)(2,1)S(1)} %pad_maximum_fusion.5.g_a), channel_id=1, source_target_pairs={{0,2},{2,4},{4,6},{6,0},{1,3},{3,5},{5,7},{7,1},{8,10},{10,12},{12... | collective-permute-start | bytes 1179656 | tf_op jit(solution)/shard_map/first_lane/ppermute | solution.py:22
  539.1 16.2 %collective-permute-start.28 = (bf16[128,512]{1,0:T(8,128)(2,1)}, bf16[128,512]{1,0:T(8,128)(2,1)S(1)}, u32[]{:S(2)}, u32[]{:S(2)}) collective-permute-start(bf16[128,512]{1,0:T(8,128)(2,1)} %get-tuple-element.97), channel_id=1, source_target_pairs={{0,4},{2,6},{4,0},{6,2},{1,5},{3,7},{5,1},{7,3},{8,12},{10,14},{12... | collective-permute-start | bytes 393224 | tf_op jit(solution)/shard_map/columns/ppermute | solution.py:22
  539.6 15.8 %collective-permute-start.29 = (bf16[128,512]{1,0:T(8,128)(2,1)}, bf16[128,512]{1,0:T(8,128)(2,1)S(1)}, u32[]{:S(2)}, u32[]{:S(2)}) collective-permute-start(bf16[128,512]{1,0:T(8,128)(2,1)} %get-tuple-element.98), channel_id=1, source_target_pairs={{0,6},{2,0},{4,2},{6,4},{1,7},{3,1},{5,3},{7,5},{8,14},{10,8},{12,... | collective-permute-start | bytes 393224 | tf_op jit(solution)/shard_map/columns/ppermute | solution.py:22
  541.7 13.6 %collective-permute-start.30 = (bf16[128,512]{1,0:T(8,128)(2,1)}, bf16[128,512]{1,0:T(8,128)(2,1)S(1)}, u32[]{:S(2)}, u32[]{:S(2)}) collective-permute-start(bf16[128,512]{1,0:T(8,128)(2,1)} %get-tuple-element.99), channel_id=1, source_target_pairs={{0,2},{2,4},{4,6},{6,0},{1,3},{3,5},{5,7},{7,1},{8,10},{10,12},{12... | collective-permute-start | bytes 393224 | tf_op jit(solution)/shard_map/columns/ppermute | solution.py:22
  546.7 8.7 %collective-permute-start.32 = (bf16[64,1536]{1,0:T(8,128)(2,1)S(1)}, bf16[64,1536]{1,0:T(8,128)(2,1)S(1)}, u32[]{:S(2)}, u32[]{:S(2)}) collective-permute-start(bf16[64,1536]{1,0:T(8,128)(2,1)S(1)} %slice.345), channel_id=1, source_target_pairs={{0,6},{2,0},{4,2},{6,4},{1,7},{3,1},{5,3},{7,5},{8,14},{10,8},{12,... | collective-permute-start | bytes 589832 | tf_op jit(solution)/shard_map/first_lane/ppermute | solution.py:22
  551.5 7.0 %collective-permute-start.34 = (bf16[64,1536]{1,0:T(8,128)(2,1)S(1)}, bf16[64,1536]{1,0:T(8,128)(2,1)S(1)}, u32[]{:S(2)}, u32[]{:S(2)}) collective-permute-start(bf16[64,1536]{1,0:T(8,128)(2,1)S(1)} %slice.346), channel_id=1, source_target_pairs={{0,2},{2,4},{4,6},{6,0},{1,3},{3,5},{5,7},{7,1},{8,10},{10,12},{12... | collective-permute-start | bytes 589832 | tf_op jit(solution)/shard_map/first_lane/ppermute | solution.py:22
  559.5 7.3 %collective-permute-start.35 = (bf16[256,1536]{1,0:T(8,128)(2,1)S(1)}, bf16[256,1536]{1,0:T(8,128)(2,1)}, u32[]{:S(2)}, u32[]{:S(2)}) collective-permute-start(bf16[256,1536]{1,0:T(8,128)(2,1)S(1)} %get-tuple-element.101), channel_id=1, source_target_pairs={{0,1},{1,0},{2,3},{3,2},{4,5},{5,4},{6,7},{7,6},{8,9},{9,8},{10,11... | collective-permute-start | bytes 2359304 | tf_op jit(solution)/shard_map/ppermute | solution.py:22
  569.1 23.9 %all-to-all-start.4 = ((bf16[16,16,1536]{2,1,0:T(8,128)(2,1)}), bf16[16,16,1536]{2,1,0:T(8,128)(2,1)S(1)}, u32[]{:S(2)}, u32[]{:S(2)}) async-start(bf16[16,16,1536]{2,1,0:T(8,128)(2,1)} %bitcast.76), calls=%async_computation.8 | async-start | bytes 1572864 | tf_op jit(solution)/shard_map/all_to_all | solution.py:39
  595.0 9.6 %all-to-all-start.5 = ((bf16[16,8,256]{2,1,0:T(8,128)(2,1)}), bf16[16,8,256]{2,1,0:T(8,128)(2,1)S(1)}, u32[]{:S(2)}, u32[]{:S(2)}) async-start(bf16[16,8,256]{2,1,0:T(8,128)(2,1)} %bitcast.79), calls=%async_computation.9 | async-start | bytes 131072 | tf_op jit(solution)/shard_map/up_grad/all_to_all | solution.py:39
  606.2 33.4 %all-to-all-start.6 = ((bf16[8,64,2048]{2,1,0:T(8,128)(2,1)}), bf16[8,64,2048]{2,1,0:T(8,128)(2,1)S(1)}, u32[]{:S(2)}, u32[]{:S(2)}) async-start(bf16[8,64,2048]{2,1,0:T(8,128)(2,1)} %broadcast_in_dim.87), calls=%async_computation.10 | async-start | bytes 4194304 | tf_op jit(solution)/shard_map/heads_sum/all_to_all | solution.py:39
  622.1 22.5 %copy-start.68 = (bf16[64]{0:T(256)(128)(2,1)S(1)}, bf16[64]{0:T(256)(128)(2,1)}, u32[]{:S(2)}) copy-start(bf16[64]{0:T(256)(128)(2,1)} %param.26) | copy-start | bytes 388
  622.1 23.2 %copy-start.66 = (bf16[128]{0:T(256)(128)(2,1)S(1)}, bf16[128]{0:T(256)(128)(2,1)}, u32[]{:S(2)}) copy-start(bf16[128]{0:T(256)(128)(2,1)} %param.22) | copy-start | bytes 772
  622.1 23.7 %copy-start.70 = (bf16[128]{0:T(256)(128)(2,1)S(1)}, bf16[128]{0:T(256)(128)(2,1)}, u32[]{:S(2)}) copy-start(bf16[128]{0:T(256)(128)(2,1)} %param.29) | copy-start | bytes 772
  (64 other events, 271.0 us)
Sparse Core Ops, SparseCore 0:
  10.3 66.3 all-gather.5
  81.6 38.0 all-gather.7
  121.3 57.5 all-gather.11
  201.9 53.5 all-gather.9
  281.3 51.9 reduce-scatter.4
  335.5 49.7 reduce-scatter.6
  387.7 26.5 reduce-scatter.10
  448.3 30.2 reduce-scatter.8
  531.5 56.1 all-gather.13
